TPU v7x, 256 devices: a whole 4x4x8 slice. The times are simulated.
256 devices in a mesh: rows: 16 (over z_hi, x), cols: 16 (over z_lo, y, core).
Axes of the slice: x: 4, y: 4, z: 8 (z_hi: 4, z_lo: 2; z = z_hi * 2 + z_lo), core: 2. Of those that a mesh axis runs over, the one named last changes fastest.
Arguments:
- frames: float32 [128, 16384], P(None, ('rows', 'cols')), may hold values from -6 to 6
- precision: float32 [16384, 16384], P('rows', 'cols'), as said below
Outputs:
- updated: float32 [16384, 16384], P('rows', 'cols')
- gradient: float32 [16384, 16384], P('rows', 'cols')
Inputs may be any that keep to these rules, and one draw needn't show every extreme that they name: precision is symmetric; its diagonal lies between 1 and 4.
All inputs are finite; a program needn't handle non-finite values.
Results may differ from a plain program's by a relative error of at most 0.0001.
Values sent between devices are 32-bit elements; how exact they have to be, the bound alone decides.
No kernel may reach another device: no remote copies, remote signals or barrier semaphores. Data moves between devices by JAX's collectives and lax.ppermute only.
A program may use at most 128 MiB of HBM per device.

v0:
```python
import jax
import jax.numpy as jnp
from jax import lax
from jax.sharding import PartitionSpec as P

ITERS = 3


step_size = 0.005
penalty = 4.0


def on_device(frames, precision):
    highest = lax.Precision.HIGHEST
    row_len, col_len = precision.shape
    frame_count = frames.shape[0]
    row_idx = lax.axis_index("rows")
    col_idx = lax.axis_index("cols")
    everything = lax.all_gather(frames, ("rows", "cols"), axis=1, tiled=True)
    row_panel = lax.dynamic_slice_in_dim(everything, row_idx * row_len, row_len, 1)
    col_panel = lax.dynamic_slice_in_dim(everything, col_idx * col_len, col_len, 1)
    global_rows = row_idx * row_len + jnp.arange(row_len, dtype=jnp.int32)
    global_cols = col_idx * col_len + jnp.arange(col_len, dtype=jnp.int32)
    mask = global_rows[:, None] == global_cols[None, :]
    current = precision
    gradient = jnp.zeros_like(precision)
    for sweep in range(ITERS):
        local_rows = lax.dot_general(
            current,
            col_panel,
            (((1,), (1,)), ((), ())),
            precision=highest,
            preferred_element_type=jnp.float32,
        )
        product = lax.psum(local_rows, "cols")
        local_cols = lax.dot_general(
            current,
            row_panel,
            (((0,), (1,)), ((), ())),
            precision=highest,
            preferred_element_type=jnp.float32,
        )
        weighted = lax.psum(local_cols, "rows")
        first = jnp.dot(product, col_panel, precision=highest, preferred_element_type=jnp.float32)
        second = lax.dot_general(
            row_panel,
            weighted,
            (((0,), (1,)), ((), ())),
            precision=highest,
            preferred_element_type=jnp.float32,
        )
        inverse = jnp.where(mask, 1.0 / jnp.where(mask, current, 1.0), 0.0)
        gradient = (first + second) * (0.5 / frame_count) - inverse
        moved = current - step_size * gradient
        bound = step_size * penalty
        current = jnp.where(mask, moved, moved - jnp.clip(moved, -bound, bound))
    return (current, gradient)


def solution(mesh):
    placed = (P(None, ("rows", "cols")), P("rows", "cols"))
    return jax.shard_map(
        on_device,
        mesh=mesh,
        in_specs=placed,
        out_specs=(P("rows", "cols"), P("rows", "cols")),
        check_vma=False,
    )
```

profile of v0, /device:TPU:40, one launch (start us, length us, event | category | flops | bytes accessed | tf_op | source)
XLA Modules:
  0.0 1375.1 jit_solution(4830441745117668998)
XLA Ops:
  7.2 0.7 all-gather.2.cloned.1.call-update
  7.9 420.2 %all-gather.2.cloned.1.call-done = f32[128,16384]{0,1:T(8,128)} async-done(((f32[128,64]{0,1:T(8,128)}), f32[128,16384]{0,1:T(8,128)}) %all-gather.2.cloned.1.call-update) | async-done | bytes 8388624 | tf_op jit(solution)/shard_map/all_gather | solution.py:19
  428.2 7.6 convolution_bitcast_fusion.1
  435.9 5.6 convolution_bitcast_fusion
  441.4 0.3 all-reduce.11.cloned.1.call-start
  441.8 114.0 %all-reduce.7.cloned.1.call-done = f32[1024,128]{0,1:T(8,128)} async-done(((f32[1024,128]{0,1:T(8,128)}), f32[1024,128]{0,1:T(8,128)}) %all-reduce.7.cloned.1.call-update) | async-done | bytes 524304 | tf_op jit(solution)/shard_map/psum | solution.py:35
  555.8 6.7 fusion.26
  562.5 166.5 %all-reduce.9.cloned.1.call-done = f32[1024,128]{0,1:T(8,128)} async-done(((f32[1024,128]{0,1:T(8,128)}), f32[1024,128]{0,1:T(8,128)}) %all-reduce.9.cloned.1.call-update) | async-done | bytes 524304 | tf_op jit(solution)/shard_map/psum | solution.py:43
  728.9 8.8 compare_select_fusion.6
  737.7 2.0 copy-done.1
  739.7 17.9 %fusion.24 = f32[1024,128]{1,0:T(8,128)} fusion(f32[1024,1024]{1,0:T(8,128)S(1)} %compare_select_fusion.6, f32[128,16384]{0,1:T(8,128)} %all-gather.2.cloned.1.call-done, s32[]{:T(128)S(6)} %select_n.35), kind=kOutput, calls=%fused_computation.35 | convolution fusion | flops 1610612736 | bytes 5242884 | tf_op jit(solution)/shard_map/dot_general | solution.py:28
  757.7 9.8 fusion.14
  767.5 0.0 all-reduce.15.cloned.1.call-start
  767.5 108.4 %all-reduce.11.cloned.1.call-done = f32[1024,128]{1,0:T(8,128)} async-done(((f32[1024,128]{1,0:T(8,128)}), f32[1024,128]{1,0:T(8,128)}) %all-reduce.11.cloned.1.call-update) | async-done | bytes 524304 | tf_op jit(solution)/shard_map/psum | solution.py:35
  875.9 6.6 fusion.22
  882.5 165.8 %all-reduce.13.cloned.1.call-done = f32[1024,128]{1,0:T(8,128)} async-done(((f32[1024,128]{1,0:T(8,128)}), f32[1024,128]{1,0:T(8,128)}) %all-reduce.13.cloned.1.call-update) | async-done | bytes 524304 | tf_op jit(solution)/shard_map/psum | solution.py:43
  1048.4 8.8 compare_select_fusion.3
  1057.2 2.0 copy-done
  1059.2 5.5 fusion.20
  1064.7 9.8 fusion.11
  1074.5 108.4 %all-reduce.15.cloned.1.call-done = f32[1024,128]{1,0:T(8,128)} async-done(((f32[1024,128]{1,0:T(8,128)}), f32[1024,128]{1,0:T(8,128)}) %all-reduce.15.cloned.1.call-update) | async-done | bytes 524304 | tf_op jit(solution)/shard_map/psum | solution.py:35
  1182.9 6.6 fusion.18
  1189.6 165.9 %all-reduce.17.cloned.1.call-done = f32[1024,128]{1,0:T(8,128)} async-done(((f32[1024,128]{1,0:T(8,128)}), f32[1024,128]{1,0:T(8,128)}) %all-reduce.17.cloned.1.call-update) | async-done | bytes 524304 | tf_op jit(solution)/shard_map/psum | solution.py:43
  1355.5 12.3 compare_select_fusion
  (14 shorter events, 0.3 us)
Async XLA Ops:
  7.2 421.0 %all-gather.2.cloned.1.call-start = ((), (), s32[]{:S(2)}) async-start(), calls=%async_computation | async-start | bytes 8421376 | tf_op jit(solution)/shard_map/all_gather | solution.py:19
  7.9 547.9 %all-reduce.7.cloned.1.call-start = ((), (), s32[]{:S(2)}) async-start(), calls=%async_computation.1 | async-start | bytes 1048576 | tf_op jit(solution)/shard_map/psum | solution.py:35
  435.8 293.1 %all-reduce.9.cloned.1.call-start = ((), (), s32[]{:S(2)}) async-start(), calls=%async_computation.2 | async-start | bytes 1048576 | tf_op jit(solution)/shard_map/psum | solution.py:43
  441.4 434.5 %all-reduce.11.cloned.1.call-start = ((), (), s32[]{:S(2)}) async-start(), calls=%async_computation.3 | async-start | bytes 1048576 | tf_op jit(solution)/shard_map/psum | solution.py:35
  737.7 2.0 copy-start.1
  757.6 290.7 %all-reduce.13.cloned.1.call-start = ((), (), s32[]{:S(2)}) async-start(), calls=%async_computation.4 | async-start | bytes 1048576 | tf_op jit(solution)/shard_map/psum | solution.py:43
  767.5 415.5 %all-reduce.15.cloned.1.call-start = ((), (), s32[]{:S(2)}) async-start(), calls=%async_computation.5 | async-start | bytes 1048576 | tf_op jit(solution)/shard_map/psum | solution.py:35
  1057.2 2.0 copy-start
  1064.7 290.8 %all-reduce.17.cloned.1.call-start = ((), (), s32[]{:S(2)}) async-start(), calls=%async_computation.6 | async-start | bytes 1048576 | tf_op jit(solution)/shard_map/psum | solution.py:43
Sparse Core Ops, SparseCore 0:
  9.9 418.2 all-gather.1
  435.9 119.8 all-reduce.6
  559.2 169.7 all-reduce.8
  757.8 118.0 all-reduce.10
  878.6 169.7 all-reduce.12
  1064.8 118.0 all-reduce.14
  1185.7 169.7 all-reduce.16
where the time goes:
time: 1380 us
  waiting for transfers between devices  1250 us (91%)
  matrix products  106 us (8%)
  between operations  14.6 us (1%)
    psum x3, waiting for transfers between devices, on_device(): weighted = lax.psum(local_cols, 'rows')  498 us
    all_gather x1, waiting for transfers between devices, on_device(): everything = lax.all_gather(frames, ('rows', 'cols'), axis=1, tiled=True)  420 us
    psum x3, waiting for transfers between devices, on_device(): product = lax.psum(local_rows, 'cols')  331 us
    dot_general x3, matrix products, on_device(): lax.dot_general(current, col_panel, (((1,), (1,)), ((), ())), precision=h...  31 us
    dot_general x3, matrix products, on_device(): lax.dot_general(row_panel, weighted, (((0,), (1,)), ((), ())), precision=...  29.9 us
  transfers between devices with their start and end apart: 7, of which 7 were waited for; matrix products, arithmetic and copies ran while one was open for 3% of the time, Pallas kernels for 0%

commit v1 on v0

v1 whole, which is shorter than its diff:
```python
import functools

import jax
import jax.numpy as jnp
from jax import lax
from jax.experimental import pallas as pl
from jax.experimental.pallas import tpu as pltpu
from jax.sharding import PartitionSpec as P

ITERS = 3

step_size = 0.005
penalty = 4.0

SIDE = 16
PIECE = 64
TILE = 256
NT = (((1,), (1,)), ((), ()))


def split(value):
    high = value.astype(jnp.bfloat16)
    low = (value - high.astype(jnp.float32)).astype(jnp.bfloat16)
    return high, low


def dot(a, b, dims=(((1,), (0,)), ((), ()))):
    return lax.dot_general(a, b, dims, preferred_element_type=jnp.float32)


def kernel(update, emit_sums, emit_grad, frame_count, *refs):
    refs = list(refs)
    place = refs.pop(0)
    omega = refs.pop(0)
    xc = refs.pop(0)
    if update:
        xr, yr, yc = refs.pop(0), refs.pop(0), refs.pop(0)
        out = refs.pop(0)
    grad = refs.pop(0) if emit_grad else None
    sums = refs.pop(0) if emit_sums else None
    if update:
        ah, al, bh, bl = refs.pop(0), refs.pop(0), refs.pop(0), refs.pop(0)
    xx = refs.pop(0) if emit_sums else None
    if update and not emit_grad:
        grad = refs.pop(0)
    rows = omega.shape[1]
    tile = pl.program_id(0)
    row, col = place[0], place[1]

    @pl.when(tile == 0)
    def _():
        for q in range(SIDE):
            span = pl.ds(q * PIECE, PIECE)
            high, low = split(xc[q])
            if emit_sums:
                xx[span, :frame_count] = high
                xx[span, frame_count:] = low
            if update:
                bh[span, :frame_count] = high
                bl[span, :frame_count] = low
                high, low = split(yc[q])
                bh[span, frame_count:] = high
                bl[span, frame_count:] = low
                d = q ^ col
                slot = (d & 1) * 8 + ((d >> 1) & 3) * 2 + (d >> 3)
                high, low = split(yr[slot])
                ah[span, :frame_count] = high
                al[span, :frame_count] = low
                high, low = split(xr[slot])
                ah[span, frame_count:] = high
                al[span, frame_count:] = low

    chunks = [slice(j, j + TILE) for j in range(0, rows, TILE)]
    bound = step_size * penalty
    if update:
        mine = pl.ds(tile * TILE, TILE)
        a_high, a_low = ah[mine, :], al[mine, :]
        for j in chunks:
            total = dot(a_high, bh[j, :], NT) + dot(a_high, bl[j, :], NT) + dot(a_low, bh[j, :], NT)
            g = total * (0.5 / frame_count)
            grad[:, j] = g
            moved = omega[:, j] - step_size * g
            out[:, j] = moved - jnp.clip(moved, -bound, bound)

        @pl.when(row == col)
        def _():
            here = pl.ds(tile * TILE, TILE)
            eye = lax.broadcasted_iota(jnp.int32, (TILE, TILE), 0) == lax.broadcasted_iota(jnp.int32, (TILE, TILE), 1)
            old = omega[:, here]
            g = grad[:, here] - jnp.where(eye, 1.0 / jnp.where(eye, old, 1.0), 0.0)
            grad[:, here] = g
            moved = old - step_size * g
            out[:, here] = jnp.where(eye, moved, moved - jnp.clip(moved, -bound, bound))

    if emit_sums:
        source = out if update else omega
        both = jnp.zeros((TILE, 2 * frame_count), jnp.float32)
        rest = jnp.zeros((TILE, frame_count), jnp.float32)
        for j in chunks:
            high, low = split(source[:, j])
            both += dot(high, xx[j, :])
            rest += dot(low, xx[j, :frame_count])
        total = both[:, :frame_count] + both[:, frame_count:] + rest
        for s in range(TILE // PIECE):
            q = tile * (TILE // PIECE) + s
            slot = ((q ^ col) & 1) * 8 + (q >> 3) * 4 + ((q >> 1) & 3)
            sums[slot] = total[s * PIECE : (s + 1) * PIECE]


def sweep(place, omega, xc, panels, emit_sums, emit_grad):
    update = bool(panels)
    rows = omega.shape[0]
    frame_count = xc.shape[-1]
    block = pl.BlockSpec((TILE, rows), lambda i, *_: (i, 0))
    whole = pl.BlockSpec((SIDE, PIECE, frame_count), lambda i, *_: (0, 0, 0))
    matrix = jax.ShapeDtypeStruct(omega.shape, jnp.float32)
    shapes, specs, scratch = [], [], []
    if update:
        shapes.append(matrix)
        specs.append(block)
        scratch += [pltpu.VMEM((rows, 2 * frame_count), jnp.bfloat16)] * 4
    if emit_grad:
        shapes.append(matrix)
        specs.append(block)
    if emit_sums:
        shapes.append(jax.ShapeDtypeStruct((SIDE, PIECE, frame_count), jnp.float32))
        specs.append(whole)
        scratch.append(pltpu.VMEM((rows, 2 * frame_count), jnp.bfloat16))
    if update and not emit_grad:
        scratch.append(pltpu.VMEM((TILE, rows), jnp.float32))
    return pl.pallas_call(
        functools.partial(kernel, update, emit_sums, emit_grad, frame_count),
        out_shape=shapes,
        grid_spec=pltpu.PrefetchScalarGridSpec(
            num_scalar_prefetch=1,
            grid=(rows // TILE,),
            in_specs=[block, whole] + [whole] * len(panels),
            out_specs=specs,
            scratch_shapes=scratch,
        ),
        compiler_params=pltpu.CompilerParams(vmem_limit_bytes=28 * 1024 * 1024),
        cost_estimate=pl.CostEstimate(flops=4 * rows * rows * frame_count * 3, bytes_accessed=8 * rows * rows, transcendentals=0),
    )(place, omega, xc, *panels)


def swap_cols(value, mask):
    return lax.ppermute(value, "cols", [(i, i ^ mask) for i in range(SIDE)])


EIGHTS = [[k + 2 * y + 8 * z for z in range(2) for y in range(4)] for k in range(2)]


def scatter_sum(sums):
    near = sums[:8] + swap_cols(sums[8:], 1)
    return lax.all_to_all(near, "cols", 0, 0, axis_index_groups=EIGHTS).sum(0)


def gather_cols(piece):
    value = piece[None]
    value = jnp.concatenate([value, swap_cols(value, 8)], 0)
    value = jnp.concatenate([value] + [swap_cols(value, 2 * m) for m in (1, 2, 3)], 0)
    return jnp.concatenate([value, swap_cols(value, 1)], 0)


def gather_turned(piece):
    turn = [(r * SIDE + c, c * SIDE + r) for r in range(SIDE) for c in range(SIDE)]
    turned = lax.ppermute(piece, ("rows", "cols"), turn)
    return lax.all_to_all(jnp.broadcast_to(turned, (SIDE,) + piece.shape), "rows", 0, 0)


def on_device(frames, precision):
    place = jnp.stack([lax.axis_index("rows"), lax.axis_index("cols")]).astype(jnp.int32)
    own = frames.T
    xc = gather_turned(own)
    xr = gather_cols(own)
    (sums,) = sweep(place, precision, xc, (), True, False)
    current = precision
    for index in range(ITERS):
        piece = scatter_sum(sums)
        yc = gather_turned(piece)
        yr = gather_cols(piece)
        if index < ITERS - 1:
            current, sums = sweep(place, current, xc, (xr, yr, yc), True, False)
        else:
            current, gradient = sweep(place, current, xc, (xr, yr, yc), False, True)
    return (current, gradient)


def solution(mesh):
    placed = (P(None, ("rows", "cols")), P("rows", "cols"))
    return jax.shard_map(
        on_device,
        mesh=mesh,
        in_specs=placed,
        out_specs=(P("rows", "cols"), P("rows", "cols")),
        check_vma=False,
    )
```

time: 1380 us -> 214 us (0.16)
  waiting for transfers between devices: 1250 us -> 81 us
  matrix products: 106 us -> 0 us
  starting transfers between devices: 0.54 us -> 72.4 us
  blocking collectives: 0 us -> 21.7 us
  Pallas kernels: 0 us -> 18.8 us
    psum x6 -> x0, waiting for transfers between devices: 829 us -> none  [the longest x3 498 us: on_device(): weighted = lax.psum(local_cols, 'rows')]
    all_gather x1 -> x0, waiting for transfers between devices: 420 us -> none  [on_device(): everything = lax.all_gather(frames, ('rows', 'cols'), axis=1, tiled=True)]
    dot_general x12 -> x0, matrix products: 106 us -> none  [the longest x3 31 us: on_device(): lax.dot_general(current, col_panel, (((1,), (1,)), ((), ())), precision=h...]
    ppermute x0 -> x27, starting transfers between devices: none -> 49.1 us  [the longest x4 25.1 us: gather_turned(): turned = lax.ppermute(piece, ('rows', 'cols'), turn)]
    ppermute x0 -> x27, waiting for transfers between devices: none -> 43.5 us  [the longest x4 22.5 us: gather_turned(): turned = lax.ppermute(piece, ('rows', 'cols'), turn)]
    all_to_all x0 -> x5, waiting for transfers between devices: none -> 37.5 us  [the longest x4 37.5 us: gather_turned(): lax.all_to_all(jnp.broadcast_to(turned, (SIDE,) + piece.shape), 'rows', 0...]
    all_to_all x0 -> x5, starting transfers between devices: none -> 23.3 us  [the longest x4 17.4 us: gather_turned(): lax.all_to_all(jnp.broadcast_to(turned, (SIDE,) + piece.shape), 'rows', 0...]
    all_to_all x0 -> x2, blocking collectives: none -> 21.7 us  [scatter_sum(): return lax.all_to_all(near, 'cols', 0, 0, axis_index_groups=EIGHTS).sum(0)]
  transfers between devices with their start and end apart: 7 -> 32, of which waited for: 7 -> 18; matrix products, arithmetic and copies ran while one was open for 3% -> 2% of each run, Pallas kernels for 0% -> 0%
where the time goes in v1:
time: 214 us; the launch traced here: 213 us
  waiting for transfers between devices  81 us (38%)
  starting transfers between devices  72.4 us (34%)
  blocking collectives  21.7 us (10%)
  Pallas kernels  18.8 us (9%)
  local copies, waits for them, and re-layouts  16.5 us (8%)
    all_to_all x4, waiting for transfers between devices, gather_turned(): lax.all_to_all(jnp.broadcast_to(turned, (SIDE,) + piece.shape), 'rows', 0...  37.5 us
    ppermute x4, starting transfers between devices, gather_turned(): turned = lax.ppermute(piece, ('rows', 'cols'), turn)  25.1 us
    ppermute x23, starting transfers between devices, swap_cols(): return lax.ppermute(value, 'cols', [(i, i ^ mask) for i in range(SIDE)])  24 us
    ppermute x4, waiting for transfers between devices, gather_turned(): turned = lax.ppermute(piece, ('rows', 'cols'), turn)  22.5 us
    all_to_all x2, blocking collectives, scatter_sum(): return lax.all_to_all(near, 'cols', 0, 0, axis_index_groups=EIGHTS).sum(0)  21.7 us
    ppermute x23, waiting for transfers between devices, swap_cols(): return lax.ppermute(value, 'cols', [(i, i ^ mask) for i in range(SIDE)])  20.9 us
    pallas_call x4, Pallas kernels, sweep(): pl.pallas_call(functools.partial(kernel, update, emit_sums, emit_grad, fr...  18.8 us
    all_to_all x4, starting transfers between devices, gather_turned(): lax.all_to_all(jnp.broadcast_to(turned, (SIDE,) + piece.shape), 'rows', 0...  17.4 us
  transfers between devices with their start and end apart: 32, of which 18 were waited for; matrix products, arithmetic and copies ran while one was open for 2% of the time, Pallas kernels for 0%

profile of v1, /device:TPU:40, one launch (start us, length us, event | category | flops | bytes accessed | tf_op | source)
XLA Modules:
  0.0 212.5 jit_solution(17094234979166375260)
XLA Ops:
  0.6 10.1 %collective-permute-start = (f32[64,128]{1,0:T(8,128)}, f32[64,128]{1,0:T(8,128)S(1)}, u32[]{:S(2)}, u32[]{:S(2)}) collective-permute-start(f32[64,128]{1,0:T(8,128)} %bitcast.22), channel_id=1, source_target_pairs={{0,0},{1,16},{2,32},{3,48},{4,64},{5,80},{6,96},{7,112},{8,128},{9... | collective-permute-start | bytes 98312 | tf_op jit(solution)/shard_map/ppermute | solution.py:167
  14.1 6.6 %all-to-all-start = ((f32[16,64,128]{2,1,0:T(8,128)}), f32[16,64,128]{2,1,0:T(8,128)S(1)}, u32[]{:S(2)}, u32[]{:S(2)}) async-start(f32[16,64,128]{2,1,0:T(8,128)} %broadcast_in_dim.24), calls=%async_computation | async-start | bytes 1048576 | tf_op jit(solution)/shard_map/all_to_all | solution.py:168
  20.8 15.2 %all-to-all-done.refs_2_ = f32[16,64,128]{2,1,0:T(8,128)S(1)} async-done(((f32[16,64,128]{2,1,0:T(8,128)}), f32[16,64,128]{2,1,0:T(8,128)S(1)}, u32[]{:S(2)}, u32[]{:S(2)}) %all-to-all-start) | async-done | bytes 524320 | tf_op jit(solution)/shard_map/all_to_all | solution.py:168
  40.8 5.2 %collective-permute-start.1 = (f32[1,64,128]{2,1,0:T(8,128)S(1)}, f32[1,64,128]{2,1,0:T(8,128)S(1)}, u32[]{:S(2)}, u32[]{:S(2)}) collective-permute-start(f32[1,64,128]{2,1,0:T(8,128)S(1)} %bitcast.23), channel_id=1, source_target_pairs={{0,8},{1,9},{2,10},{3,11},{4,12},{5,13},{6,14},{7,15},{8,0},{9,1},... | collective-permute-start | bytes 98312 | tf_op jit(solution)/shard_map/ppermute | solution.py:147
  46.7 6.0 %all-to-all-start.1 = ((f32[8,64,128]{2,1,0:T(8,128)}), f32[8,64,128]{2,1,0:T(8,128)S(1)}, u32[]{:S(2)}, u32[]{:S(2)}) async-start(f32[8,64,128]{2,1,0:T(8,128)} %slice_add_fusion), calls=%async_computation.1 | async-start | bytes 524288 | tf_op jit(solution)/shard_map/all_to_all | solution.py:155
  60.4 4.7 %collective-permute-start.12 = (f32[64,128]{1,0:T(8,128)S(1)}, f32[64,128]{1,0:T(8,128)S(1)}, u32[]{:S(2)}, u32[]{:S(2)}) collective-permute-start(f32[64,128]{1,0:T(8,128)S(1)} %reduce_sum.27), channel_id=1, source_target_pairs={{0,0},{1,16},{2,32},{3,48},{4,64},{5,80},{6,96},{7,112},{8,128},{9... | collective-permute-start | bytes 98312 | tf_op jit(solution)/shard_map/ppermute | solution.py:167
  65.7 6.9 %collective-permute-done.12 = f32[64,128]{1,0:T(8,128)S(1)} collective-permute-done((f32[64,128]{1,0:T(8,128)S(1)}, f32[64,128]{1,0:T(8,128)S(1)}, u32[]{:S(2)}, u32[]{:S(2)}) %collective-permute-start.12) | collective-permute-done | bytes 32800 | tf_op jit(solution)/shard_map/ppermute | solution.py:167
  73.5 3.6 %all-to-all-start.2 = ((f32[16,64,128]{2,1,0:T(8,128)}), f32[16,64,128]{2,1,0:T(8,128)S(1)}, u32[]{:S(2)}, u32[]{:S(2)}) async-start(f32[16,64,128]{2,1,0:T(8,128)} %broadcast_in_dim.27), calls=%async_computation.2 | async-start | bytes 1048576 | tf_op jit(solution)/shard_map/all_to_all | solution.py:168
  81.5 3.4 %collective-permute-done.8 = f32[2,64,128]{2,1,0:T(8,128)S(1)} collective-permute-done((f32[2,64,128]{2,1,0:T(8,128)S(1)}, f32[2,64,128]{2,1,0:T(8,128)S(1)}, u32[]{:S(2)}, u32[]{:S(2)}) %collective-permute-start.8) | collective-permute-done | bytes 65568 | tf_op jit(solution)/shard_map/ppermute | solution.py:147
  86.6 6.4 %all-to-all-done.2.refs_5_ = f32[16,64,128]{2,1,0:T(8,128)S(1)} async-done(((f32[16,64,128]{2,1,0:T(8,128)}), f32[16,64,128]{2,1,0:T(8,128)S(1)}, u32[]{:S(2)}, u32[]{:S(2)}) %all-to-all-start.2) | async-done | bytes 524320 | tf_op jit(solution)/shard_map/all_to_all | solution.py:168
  95.3 5.4 %shard_map.42 = (f32[1024,1024]{1,0:T(8,128)S(1)}, f32[16,64,128]{2,1,0:T(8,128)S(1)}) custom-call(s32[2]{0:T(128)S(1)} %pad_add_fusion.refs_0_, f32[1024,1024]{1,0:T(8,128)S(1)} %copy-done.1, f32[16,64,128]{2,1,0:T(8,128)S(1)} %all-to-all-done.refs_2_, f32[16,64,128]{2,1,0:T(8,128)S(1)} %constant_dynamic-update-slice_fusion.5.refs_3_, ...), custom_call_target="tpu_custom_call" | custom-call | flops 1610612736 | bytes 8388608 | tf_op jit(solution)/shard_map/pallas_call | solution.py:131
  104.4 11.4 %all_to_all.35 = f32[8,64,128]{2,1,0:T(8,128)S(1)} all-to-all(f32[8,64,128]{2,1,0:T(8,128)S(1)} %slice_add_fusion.2), channel_id=1, replica_groups={{0,2,4,6,8,10,12,14},{1,3,5,7,9,11,13,15},{16,18,20,22,24,26,28,30},{17..., dimensions={0} | all-to-all | bytes 524288 | tf_op jit(solution)/shard_map/all_to_all | solution.py:155
  115.8 4.9 %collective-permute-start.19 = (f32[64,128]{1,0:T(8,128)S(1)}, f32[64,128]{1,0:T(8,128)S(1)}, u32[]{:S(2)}, u32[]{:S(2)}) collective-permute-start(f32[64,128]{1,0:T(8,128)S(1)} %reduce_sum.28), channel_id=1, source_target_pairs={{0,0},{1,16},{2,32},{3,48},{4,64},{5,80},{6,96},{7,112},{8,128},{9... | collective-permute-start | bytes 98312 | tf_op jit(solution)/shard_map/ppermute | solution.py:167
  121.1 6.8 %collective-permute-done.19 = f32[64,128]{1,0:T(8,128)S(1)} collective-permute-done((f32[64,128]{1,0:T(8,128)S(1)}, f32[64,128]{1,0:T(8,128)S(1)}, u32[]{:S(2)}, u32[]{:S(2)}) %collective-permute-start.19) | collective-permute-done | bytes 32800 | tf_op jit(solution)/shard_map/ppermute | solution.py:167
  128.8 3.6 %all-to-all-start.4 = ((f32[16,64,128]{2,1,0:T(8,128)}), f32[16,64,128]{2,1,0:T(8,128)S(1)}, u32[]{:S(2)}, u32[]{:S(2)}) async-start(f32[16,64,128]{2,1,0:T(8,128)} %broadcast_in_dim.29), calls=%async_computation.4 | async-start | bytes 1048576 | tf_op jit(solution)/shard_map/all_to_all | solution.py:168
  141.3 8.0 %all-to-all-done.4.refs_5_ = f32[16,64,128]{2,1,0:T(8,128)S(1)} async-done(((f32[16,64,128]{2,1,0:T(8,128)}), f32[16,64,128]{2,1,0:T(8,128)S(1)}, u32[]{:S(2)}, u32[]{:S(2)}) %all-to-all-start.4) | async-done | bytes 524320 | tf_op jit(solution)/shard_map/all_to_all | solution.py:168
  151.5 5.4 %shard_map.43 = (f32[1024,1024]{1,0:T(8,128)S(1)}, f32[16,64,128]{2,1,0:T(8,128)S(1)}) custom-call(s32[2]{0:T(128)S(1)} %pad_add_fusion.refs_0_, f32[1024,1024]{1,0:T(8,128)S(1)} %copy-done.5, f32[16,64,128]{2,1,0:T(8,128)S(1)} %all-to-all-done.refs_2_, f32[16,64,128]{2,1,0:T(8,128)S(1)} %constant_dynamic-update-slice_fusion.5.refs_3_, ...), custom_call_target="tpu_custom_call" | custom-call | flops 1610612736 | bytes 8388608 | tf_op jit(solution)/shard_map/pallas_call | solution.py:131
  160.6 10.3 %all_to_all.36 = f32[8,64,128]{2,1,0:T(8,128)S(1)} all-to-all(f32[8,64,128]{2,1,0:T(8,128)S(1)} %slice_add_fusion.1), channel_id=1, replica_groups={{0,2,4,6,8,10,12,14},{1,3,5,7,9,11,13,15},{16,18,20,22,24,26,28,30},{17..., dimensions={0} | all-to-all | bytes 524288 | tf_op jit(solution)/shard_map/all_to_all | solution.py:155
  171.0 5.3 %collective-permute-start.26 = (f32[64,128]{1,0:T(8,128)S(1)}, f32[64,128]{1,0:T(8,128)S(1)}, u32[]{:S(2)}, u32[]{:S(2)}) collective-permute-start(f32[64,128]{1,0:T(8,128)S(1)} %reduce_sum.29), channel_id=1, source_target_pairs={{0,0},{1,16},{2,32},{3,48},{4,64},{5,80},{6,96},{7,112},{8,128},{9... | collective-permute-start | bytes 98312 | tf_op jit(solution)/shard_map/ppermute | solution.py:167
  176.8 6.3 %collective-permute-done.26 = f32[64,128]{1,0:T(8,128)S(1)} collective-permute-done((f32[64,128]{1,0:T(8,128)S(1)}, f32[64,128]{1,0:T(8,128)S(1)}, u32[]{:S(2)}, u32[]{:S(2)}) %collective-permute-start.26) | collective-permute-done | bytes 32800 | tf_op jit(solution)/shard_map/ppermute | solution.py:167
  183.9 3.6 %all-to-all-start.6 = ((f32[16,64,128]{2,1,0:T(8,128)}), f32[16,64,128]{2,1,0:T(8,128)S(1)}, u32[]{:S(2)}, u32[]{:S(2)}) async-start(f32[16,64,128]{2,1,0:T(8,128)} %broadcast_in_dim.31), calls=%async_computation.6 | async-start | bytes 1048576 | tf_op jit(solution)/shard_map/all_to_all | solution.py:168
  191.7 3.5 %collective-permute-done.22 = f32[2,64,128]{2,1,0:T(8,128)S(1)} collective-permute-done((f32[2,64,128]{2,1,0:T(8,128)S(1)}, f32[2,64,128]{2,1,0:T(8,128)S(1)}, u32[]{:S(2)}, u32[]{:S(2)}) %collective-permute-start.22) | collective-permute-done | bytes 65568 | tf_op jit(solution)/shard_map/ppermute | solution.py:147
  196.9 7.8 %all-to-all-done.6.refs_5_ = f32[16,64,128]{2,1,0:T(8,128)S(1)} async-done(((f32[16,64,128]{2,1,0:T(8,128)}), f32[16,64,128]{2,1,0:T(8,128)S(1)}, u32[]{:S(2)}, u32[]{:S(2)}) %all-to-all-start.6) | async-done | bytes 524320 | tf_op jit(solution)/shard_map/all_to_all | solution.py:168
  207.0 5.6 %shard_map.44 = (f32[1024,1024]{1,0:T(8,128)}, f32[1024,1024]{1,0:T(8,128)}) custom-call(s32[2]{0:T(128)S(1)} %pad_add_fusion.refs_0_, f32[1024,1024]{1,0:T(8,128)S(1)} %copy-done.3, f32[16,64,128]{2,1,0:T(8,128)S(1)} %all-to-all-done.refs_2_, f32[16,64,128]{2,1,0:T(8,128)S(1)} %constant_dynamic-update-slice_fusion.5.refs_3_, ...), custom_call_target="tpu_custom_call" | custom-call | flops 1610612736 | bytes 8388608 | tf_op jit(solution)/shard_map/pallas_call | solution.py:131
  (102 shorter events, 55.3 us)
Async XLA Ops:
  0.6 12.6 %collective-permute-start = (f32[64,128]{1,0:T(8,128)}, f32[64,128]{1,0:T(8,128)S(1)}, u32[]{:S(2)}, u32[]{:S(2)}) collective-permute-start(f32[64,128]{1,0:T(8,128)} %bitcast.22), channel_id=1, source_target_pairs={{0,0},{1,16},{2,32},{3,48},{4,64},{5,80},{6,96},{7,112},{8,128},{9... | collective-permute-start | bytes 98312 | tf_op jit(solution)/shard_map/ppermute | solution.py:167
  14.1 22.0 %all-to-all-start = ((f32[16,64,128]{2,1,0:T(8,128)}), f32[16,64,128]{2,1,0:T(8,128)S(1)}, u32[]{:S(2)}, u32[]{:S(2)}) async-start(f32[16,64,128]{2,1,0:T(8,128)} %broadcast_in_dim.24), calls=%async_computation | async-start | bytes 1048576 | tf_op jit(solution)/shard_map/all_to_all | solution.py:168
  40.7 5.3 %collective-permute-start.6 = (f32[8,64,128]{2,1,0:T(8,128)S(1)}, f32[8,64,128]{2,1,0:T(8,128)S(1)}, u32[]{:S(2)}, u32[]{:S(2)}) collective-permute-start(f32[8,64,128]{2,1,0:T(8,128)S(1)} %slice.25), channel_id=1, source_target_pairs={{0,1},{1,0},{2,3},{3,2},{4,5},{5,4},{6,7},{7,6},{8,9},{9,8},{10,11... | collective-permute-start | bytes 786440 | tf_op jit(solution)/shard_map/ppermute | solution.py:147
  40.8 11.9 %collective-permute-start.1 = (f32[1,64,128]{2,1,0:T(8,128)S(1)}, f32[1,64,128]{2,1,0:T(8,128)S(1)}, u32[]{:S(2)}, u32[]{:S(2)}) collective-permute-start(f32[1,64,128]{2,1,0:T(8,128)S(1)} %bitcast.23), channel_id=1, source_target_pairs={{0,8},{1,9},{2,10},{3,11},{4,12},{5,13},{6,14},{7,15},{8,0},{9,1},... | collective-permute-start | bytes 98312 | tf_op jit(solution)/shard_map/ppermute | solution.py:147
  46.7 13.7 %all-to-all-start.1 = ((f32[8,64,128]{2,1,0:T(8,128)}), f32[8,64,128]{2,1,0:T(8,128)S(1)}, u32[]{:S(2)}, u32[]{:S(2)}) async-start(f32[8,64,128]{2,1,0:T(8,128)} %slice_add_fusion), calls=%async_computation.1 | async-start | bytes 524288 | tf_op jit(solution)/shard_map/all_to_all | solution.py:155
  52.7 12.5 %collective-permute-start.4 = (f32[2,64,128]{2,1,0:T(8,128)S(1)}, f32[2,64,128]{2,1,0:T(8,128)S(1)}, u32[]{:S(2)}, u32[]{:S(2)}) collective-permute-start(f32[2,64,128]{2,1,0:T(8,128)S(1)} %pad_maximum_fusion), channel_id=1, source_target_pairs={{0,6},{1,7},{2,4},{3,5},{4,2},{5,3},{6,0},{7,1},{8,14},{9,15},{10,... | collective-permute-start | bytes 196616 | tf_op jit(solution)/shard_map/ppermute | solution.py:147
  54.3 6.1 %collective-permute-start.3 = (f32[2,64,128]{2,1,0:T(8,128)S(1)}, f32[2,64,128]{2,1,0:T(8,128)S(1)}, u32[]{:S(2)}, u32[]{:S(2)}) collective-permute-start(f32[2,64,128]{2,1,0:T(8,128)S(1)} %pad_maximum_fusion), channel_id=1, source_target_pairs={{0,4},{1,5},{2,6},{3,7},{4,0},{5,1},{6,2},{7,3},{8,12},{9,13},{10,... | collective-permute-start | bytes 196616 | tf_op jit(solution)/shard_map/ppermute | solution.py:147
  55.4 4.4 %collective-permute-start.2 = (f32[2,64,128]{2,1,0:T(8,128)S(1)}, f32[2,64,128]{2,1,0:T(8,128)S(1)}, u32[]{:S(2)}, u32[]{:S(2)}) collective-permute-start(f32[2,64,128]{2,1,0:T(8,128)S(1)} %pad_maximum_fusion), channel_id=1, source_target_pairs={{0,2},{1,3},{2,0},{3,1},{4,6},{5,7},{6,4},{7,5},{8,10},{9,11},{10,... | collective-permute-start | bytes 196616 | tf_op jit(solution)/shard_map/ppermute | solution.py:147
  60.4 12.2 %collective-permute-start.12 = (f32[64,128]{1,0:T(8,128)S(1)}, f32[64,128]{1,0:T(8,128)S(1)}, u32[]{:S(2)}, u32[]{:S(2)}) collective-permute-start(f32[64,128]{1,0:T(8,128)S(1)} %reduce_sum.27), channel_id=1, source_target_pairs={{0,0},{1,16},{2,32},{3,48},{4,64},{5,80},{6,96},{7,112},{8,128},{9... | collective-permute-start | bytes 98312 | tf_op jit(solution)/shard_map/ppermute | solution.py:167
  65.2 19.9 %collective-permute-start.5 = (f32[8,64,128]{2,1,0:T(8,128)S(1)}, f32[8,64,128]{2,1,0:T(8,128)S(1)}, u32[]{:S(2)}, u32[]{:S(2)}) collective-permute-start(f32[8,64,128]{2,1,0:T(8,128)S(1)} %get-tuple-element.28), channel_id=1, source_target_pairs={{0,1},{1,0},{2,3},{3,2},{4,5},{5,4},{6,7},{7,6},{8,9},{9,8},{10,11... | collective-permute-start | bytes 786440 | tf_op jit(solution)/shard_map/ppermute | solution.py:147
  65.3 11.8 %collective-permute-start.7 = (f32[1,64,128]{2,1,0:T(8,128)S(1)}, f32[1,64,128]{2,1,0:T(8,128)S(1)}, u32[]{:S(2)}, u32[]{:S(2)}) collective-permute-start(f32[1,64,128]{2,1,0:T(8,128)S(1)} %bitcast.16), channel_id=1, source_target_pairs={{0,8},{1,9},{2,10},{3,11},{4,12},{5,13},{6,14},{7,15},{8,0},{9,1},... | collective-permute-start | bytes 98312 | tf_op jit(solution)/shard_map/ppermute | solution.py:147
  73.5 19.6 %all-to-all-start.2 = ((f32[16,64,128]{2,1,0:T(8,128)}), f32[16,64,128]{2,1,0:T(8,128)S(1)}, u32[]{:S(2)}, u32[]{:S(2)}) async-start(f32[16,64,128]{2,1,0:T(8,128)} %broadcast_in_dim.27), calls=%async_computation.2 | async-start | bytes 1048576 | tf_op jit(solution)/shard_map/all_to_all | solution.py:168
  77.1 7.9 %collective-permute-start.10 = (f32[2,64,128]{2,1,0:T(8,128)S(1)}, f32[2,64,128]{2,1,0:T(8,128)S(1)}, u32[]{:S(2)}, u32[]{:S(2)}) collective-permute-start(f32[2,64,128]{2,1,0:T(8,128)S(1)} %pad_maximum_fusion.1), channel_id=1, source_target_pairs={{0,6},{1,7},{2,4},{3,5},{4,2},{5,3},{6,0},{7,1},{8,14},{9,15},{10,... | collective-permute-start | bytes 196616 | tf_op jit(solution)/shard_map/ppermute | solution.py:147
  78.8 6.2 %collective-permute-start.9 = (f32[2,64,128]{2,1,0:T(8,128)S(1)}, f32[2,64,128]{2,1,0:T(8,128)S(1)}, u32[]{:S(2)}, u32[]{:S(2)}) collective-permute-start(f32[2,64,128]{2,1,0:T(8,128)S(1)} %pad_maximum_fusion.1), channel_id=1, source_target_pairs={{0,4},{1,5},{2,6},{3,7},{4,0},{5,1},{6,2},{7,3},{8,12},{9,13},{10,... | collective-permute-start | bytes 196616 | tf_op jit(solution)/shard_map/ppermute | solution.py:147
  115.8 12.1 %collective-permute-start.19 = (f32[64,128]{1,0:T(8,128)S(1)}, f32[64,128]{1,0:T(8,128)S(1)}, u32[]{:S(2)}, u32[]{:S(2)}) collective-permute-start(f32[64,128]{1,0:T(8,128)S(1)} %reduce_sum.28), channel_id=1, source_target_pairs={{0,0},{1,16},{2,32},{3,48},{4,64},{5,80},{6,96},{7,112},{8,128},{9... | collective-permute-start | bytes 98312 | tf_op jit(solution)/shard_map/ppermute | solution.py:167
  120.7 11.6 %collective-permute-start.14 = (f32[1,64,128]{2,1,0:T(8,128)S(1)}, f32[1,64,128]{2,1,0:T(8,128)S(1)}, u32[]{:S(2)}, u32[]{:S(2)}) collective-permute-start(f32[1,64,128]{2,1,0:T(8,128)S(1)} %bitcast.20), channel_id=1, source_target_pairs={{0,8},{1,9},{2,10},{3,11},{4,12},{5,13},{6,14},{7,15},{8,0},{9,1},... | collective-permute-start | bytes 98312 | tf_op jit(solution)/shard_map/ppermute | solution.py:147
  128.8 20.6 %all-to-all-start.4 = ((f32[16,64,128]{2,1,0:T(8,128)}), f32[16,64,128]{2,1,0:T(8,128)S(1)}, u32[]{:S(2)}, u32[]{:S(2)}) async-start(f32[16,64,128]{2,1,0:T(8,128)} %broadcast_in_dim.29), calls=%async_computation.4 | async-start | bytes 1048576 | tf_op jit(solution)/shard_map/all_to_all | solution.py:168
  132.4 7.2 %collective-permute-start.17 = (f32[2,64,128]{2,1,0:T(8,128)S(1)}, f32[2,64,128]{2,1,0:T(8,128)S(1)}, u32[]{:S(2)}, u32[]{:S(2)}) collective-permute-start(f32[2,64,128]{2,1,0:T(8,128)S(1)} %pad_maximum_fusion.2), channel_id=1, source_target_pairs={{0,6},{1,7},{2,4},{3,5},{4,2},{5,3},{6,0},{7,1},{8,14},{9,15},{10,... | collective-permute-start | bytes 196616 | tf_op jit(solution)/shard_map/ppermute | solution.py:147
  132.6 7.0 %collective-permute-start.16 = (f32[2,64,128]{2,1,0:T(8,128)S(1)}, f32[2,64,128]{2,1,0:T(8,128)S(1)}, u32[]{:S(2)}, u32[]{:S(2)}) collective-permute-start(f32[2,64,128]{2,1,0:T(8,128)S(1)} %pad_maximum_fusion.2), channel_id=1, source_target_pairs={{0,4},{1,5},{2,6},{3,7},{4,0},{5,1},{6,2},{7,3},{8,12},{9,13},{10,... | collective-permute-start | bytes 196616 | tf_op jit(solution)/shard_map/ppermute | solution.py:147
  171.0 12.1 %collective-permute-start.26 = (f32[64,128]{1,0:T(8,128)S(1)}, f32[64,128]{1,0:T(8,128)S(1)}, u32[]{:S(2)}, u32[]{:S(2)}) collective-permute-start(f32[64,128]{1,0:T(8,128)S(1)} %reduce_sum.29), channel_id=1, source_target_pairs={{0,0},{1,16},{2,32},{3,48},{4,64},{5,80},{6,96},{7,112},{8,128},{9... | collective-permute-start | bytes 98312 | tf_op jit(solution)/shard_map/ppermute | solution.py:167
  176.3 11.2 %collective-permute-start.21 = (f32[1,64,128]{2,1,0:T(8,128)S(1)}, f32[1,64,128]{2,1,0:T(8,128)S(1)}, u32[]{:S(2)}, u32[]{:S(2)}) collective-permute-start(f32[1,64,128]{2,1,0:T(8,128)S(1)} %bitcast.18), channel_id=1, source_target_pairs={{0,8},{1,9},{2,10},{3,11},{4,12},{5,13},{6,14},{7,15},{8,0},{9,1},... | collective-permute-start | bytes 98312 | tf_op jit(solution)/shard_map/ppermute | solution.py:147
  183.9 20.9 %all-to-all-start.6 = ((f32[16,64,128]{2,1,0:T(8,128)}), f32[16,64,128]{2,1,0:T(8,128)S(1)}, u32[]{:S(2)}, u32[]{:S(2)}) async-start(f32[16,64,128]{2,1,0:T(8,128)} %broadcast_in_dim.31), calls=%async_computation.6 | async-start | bytes 1048576 | tf_op jit(solution)/shard_map/all_to_all | solution.py:168
  187.5 7.7 %collective-permute-start.24 = (f32[2,64,128]{2,1,0:T(8,128)S(1)}, f32[2,64,128]{2,1,0:T(8,128)S(1)}, u32[]{:S(2)}, u32[]{:S(2)}) collective-permute-start(f32[2,64,128]{2,1,0:T(8,128)S(1)} %pad_maximum_fusion.3), channel_id=1, source_target_pairs={{0,6},{1,7},{2,4},{3,5},{4,2},{5,3},{6,0},{7,1},{8,14},{9,15},{10,... | collective-permute-start | bytes 196616 | tf_op jit(solution)/shard_map/ppermute | solution.py:147
  188.3 7.0 %collective-permute-start.23 = (f32[2,64,128]{2,1,0:T(8,128)S(1)}, f32[2,64,128]{2,1,0:T(8,128)S(1)}, u32[]{:S(2)}, u32[]{:S(2)}) collective-permute-start(f32[2,64,128]{2,1,0:T(8,128)S(1)} %pad_maximum_fusion.3), channel_id=1, source_target_pairs={{0,4},{1,5},{2,6},{3,7},{4,0},{5,1},{6,2},{7,3},{8,12},{9,13},{10,... | collective-permute-start | bytes 196616 | tf_op jit(solution)/shard_map/ppermute | solution.py:147
  (15 other events, 73.9 us)

commit v2 on v1

--- a/solution.py
+++ b/solution.py
@@ -2,6 +2,7 @@
 
 import jax
 import jax.numpy as jnp
+import numpy as np
 from jax import lax
 from jax.experimental import pallas as pl
 from jax.experimental.pallas import tpu as pltpu
@@ -51,22 +52,20 @@
     def _():
         for q in range(SIDE):
             span = pl.ds(q * PIECE, PIECE)
-            high, low = split(xc[q])
+            high, low = split(xc[place[2 + q]])
             if emit_sums:
                 xx[span, :frame_count] = high
                 xx[span, frame_count:] = low
             if update:
                 bh[span, :frame_count] = high
                 bl[span, :frame_count] = low
-                high, low = split(yc[q])
+                high, low = split(yc[place[34 + q]])
                 bh[span, frame_count:] = high
                 bl[span, frame_count:] = low
-                d = q ^ col
-                slot = (d & 1) * 8 + ((d >> 1) & 3) * 2 + (d >> 3)
-                high, low = split(yr[slot])
+                high, low = split(yr[place[50 + q]])
                 ah[span, :frame_count] = high
                 al[span, :frame_count] = low
-                high, low = split(xr[slot])
+                high, low = split(xr[place[18 + q]])
                 ah[span, frame_count:] = high
                 al[span, frame_count:] = low
 
@@ -103,7 +102,7 @@
         total = both[:, :frame_count] + both[:, frame_count:] + rest
         for s in range(TILE // PIECE):
             q = tile * (TILE // PIECE) + s
-            slot = ((q ^ col) & 1) * 8 + (q >> 3) * 4 + ((q >> 1) & 3)
+            slot = ((q ^ col) & 1) * 8 + ((q ^ col) >> 3) * 4 + ((q >> 1) & 3)
             sums[slot] = total[s * PIECE : (s + 1) * PIECE]
 
 
@@ -113,7 +112,7 @@
     frame_count = xc.shape[-1]
     block = pl.BlockSpec((TILE, rows), lambda i, *_: (i, 0))
     whole = pl.BlockSpec((SIDE, PIECE, frame_count), lambda i, *_: (0, 0, 0))
-    matrix = jax.ShapeDtypeStruct(omega.shape, jnp.float32)
+    matrix = pltpu.HBM(omega.shape, jnp.float32)
     shapes, specs, scratch = [], [], []
     if update:
         shapes.append(matrix)
@@ -140,45 +139,79 @@
         ),
         compiler_params=pltpu.CompilerParams(vmem_limit_bytes=28 * 1024 * 1024),
         cost_estimate=pl.CostEstimate(flops=4 * rows * rows * frame_count * 3, bytes_accessed=8 * rows * rows, transcendentals=0),
-    )(place, omega, xc, *panels)
+    )(place, pltpu.with_memory_space_constraint(omega, pltpu.HBM), xc, *panels)
 
 
 def swap_cols(value, mask):
     return lax.ppermute(value, "cols", [(i, i ^ mask) for i in range(SIDE)])
 
 
-EIGHTS = [[k + 2 * y + 8 * z for z in range(2) for y in range(4)] for k in range(2)]
-
-
-def scatter_sum(sums):
-    near = sums[:8] + swap_cols(sums[8:], 1)
-    return lax.all_to_all(near, "cols", 0, 0, axis_index_groups=EIGHTS).sum(0)
-
-
-def gather_cols(piece):
+def swap_rows(value, mask):
+    return lax.ppermute(value, "rows", [(i, i ^ mask) for i in range(SIDE)])
+
+
+def landing(r, c):
+    high, x = r >> 2, r & 3
+    low, y, core = c >> 3, (c >> 1) & 3, c & 1
+    off = (2, 1, 0, 3)[(y - ((r >> 1) & 3)) % 4]
+    far = [min(d % 8, -d % 8) for d in (2 * off + (r >> 3), 2 * off + (r >> 3) - 1)]
+    if far[low] > far[1 - low] or (far[0] == far[1] and low == 0):
+        step = (0, 1)[core]
+    else:
+        step = (3, 2)[core]
+    return ((high + off) % 4) * 4 + (x + step) % 4, r
+
+
+LANDING = {(r, c): landing(r, c) for r in range(SIDE) for c in range(SIDE)}
+SOURCE = {there: here for here, there in LANDING.items()}
+
+
+def slots():
+    table = np.zeros((SIDE, SIDE, 4, SIDE), np.int32)
+    for r in range(SIDE):
+        for c in range(SIDE):
+            for q in range(SIDE):
+                lands = LANDING[c, (q & 9) | (SOURCE[r, c][1] & 6)][0]
+                hop = (lands ^ r) & 3
+                y, mine = (q >> 1) & 3, (SOURCE[r, c][1] >> 1) & 3
+                side = ((q ^ c) & 1) * 8 + ((q ^ c) >> 3) * 4
+                table[r, c, 0, q] = hop * 4 + (y ^ mine)
+                table[r, c, 1, q] = side + (y ^ ((c >> 1) & 3))
+                table[r, c, 2, q] = hop * 4 + y
+                table[r, c, 3, q] = side + y
+    return table.reshape(SIDE, SIDE, 4 * SIDE)
+
+
+def sum_near(sums):
+    value = sums[:8] + swap_cols(sums[8:], 1)
+    value = value[:4] + swap_cols(value[4:], 8)
+    others = [swap_cols(value, 2 * m) for m in (1, 2, 3)]
+    return (value + others[0]) + (others[1] + others[2])
+
+
+def gather_near(piece):
     value = piece[None]
-    value = jnp.concatenate([value, swap_cols(value, 8)], 0)
-    value = jnp.concatenate([value] + [swap_cols(value, 2 * m) for m in (1, 2, 3)], 0)
-    return jnp.concatenate([value, swap_cols(value, 1)], 0)
-
-
-def gather_turned(piece):
-    turn = [(r * SIDE + c, c * SIDE + r) for r in range(SIDE) for c in range(SIDE)]
-    turned = lax.ppermute(piece, ("rows", "cols"), turn)
-    return lax.all_to_all(jnp.broadcast_to(turned, (SIDE,) + piece.shape), "rows", 0, 0)
+    return jnp.concatenate([value] + [swap_cols(value, 2 * m) for m in (1, 2, 3)], 0)
+
+
+def panels_of(four):
+    pairs = [(r * SIDE + c, LANDING[r, c][0] * SIDE + LANDING[r, c][1]) for r in range(SIDE) for c in range(SIDE)]
+    turned = lax.ppermute(four, ("rows", "cols"), pairs)
+    across = jnp.concatenate([turned] + [swap_rows(turned, m) for m in (1, 2, 3)], 0)
+    along = jnp.concatenate([four, swap_cols(four, 8)], 0)
+    along = jnp.concatenate([along, swap_cols(along, 1)], 0)
+    return across, along
 
 
 def on_device(frames, precision):
-    place = jnp.stack([lax.axis_index("rows"), lax.axis_index("cols")]).astype(jnp.int32)
-    own = frames.T
-    xc = gather_turned(own)
-    xr = gather_cols(own)
+    row, col = lax.axis_index("rows"), lax.axis_index("cols")
+    table = lax.dynamic_slice(jnp.asarray(slots()), (row, col, 0), (1, 1, 4 * SIDE)).reshape(-1)
+    place = jnp.concatenate([jnp.stack([row, col]).astype(jnp.int32), table])
+    xc, xr = panels_of(gather_near(frames.T))
     (sums,) = sweep(place, precision, xc, (), True, False)
     current = precision
     for index in range(ITERS):
-        piece = scatter_sum(sums)
-        yc = gather_turned(piece)
-        yr = gather_cols(piece)
+        yc, yr = panels_of(sum_near(sums))
         if index < ITERS - 1:
             current, sums = sweep(place, current, xc, (xr, yr, yc), True, False)
         else:

time: 214 us -> 184 us (0.86)
  blocking collectives: 21.7 us -> 0 us
  local copies, waits for them, and re-layouts: 16.5 us -> 0.89 us
  starting transfers between devices: 72.4 us -> 61.3 us
  waiting for transfers between devices: 81 us -> 91.1 us
  Pallas kernels: 18.8 us -> 26.9 us
    all_to_all x5 -> x0, waiting for transfers between devices: 37.5 us -> none  [the longest x4 37.5 us: gather_turned(): lax.all_to_all(jnp.broadcast_to(turned, (SIDE,) + piece.shape), 'rows', 0...]
    ppermute x4 -> x16, waiting for transfers between devices: 22.5 us -> 52.2 us  [the longest x4 30.6 us: panels_of(): turned = lax.ppermute(four, ('rows', 'cols'), pairs)]
    all_to_all x5 -> x0, starting transfers between devices: 23.3 us -> none  [the longest x4 17.4 us: gather_turned(): lax.all_to_all(jnp.broadcast_to(turned, (SIDE,) + piece.shape), 'rows', 0...]
    all_to_all x2 -> x0, blocking collectives: 21.7 us -> none  [scatter_sum(): return lax.all_to_all(near, 'cols', 0, 0, axis_index_groups=EIGHTS).sum(0)]
    ppermute x23 -> x26, waiting for transfers between devices: 20.9 us -> 38.9 us  [swap_cols(): return lax.ppermute(value, 'cols', [(i, i ^ mask) for i in range(SIDE)])]
    unnamed x30 -> x9, local copies, waits for them, and re-layouts: 12.9 us -> 0.06 us
    ppermute x4 -> x16, starting transfers between devices: 25.1 us -> 36.8 us  [the longest x4 18.9 us: panels_of(): turned = lax.ppermute(four, ('rows', 'cols'), pairs)]
    pallas_call x4, Pallas kernels: 18.8 us -> 26.9 us  [sweep(): pl.pallas_call(functools.partial(kernel, update, emit_sums, emit_grad, fr...]
  transfers between devices with their start and end apart: 32 -> 42, of which waited for: 18 -> 30; matrix products, arithmetic and copies ran while one was open for 2% -> 1% of each run, Pallas kernels for 0% -> 0%
where the time goes in v2:
time: 184 us; the launch traced here: 183 us
  waiting for transfers between devices  91.1 us (50%)
  starting transfers between devices  61.3 us (33%)
  Pallas kernels  26.9 us (15%)
    ppermute x26, waiting for transfers between devices, swap_cols(): return lax.ppermute(value, 'cols', [(i, i ^ mask) for i in range(SIDE)])  38.9 us
    ppermute x4, waiting for transfers between devices, panels_of(): turned = lax.ppermute(four, ('rows', 'cols'), pairs)  30.6 us
    pallas_call x4, Pallas kernels, sweep(): pl.pallas_call(functools.partial(kernel, update, emit_sums, emit_grad, fr...  26.9 us
    ppermute x26, starting transfers between devices, swap_cols(): return lax.ppermute(value, 'cols', [(i, i ^ mask) for i in range(SIDE)])  24.5 us
    ppermute x12, waiting for transfers between devices, swap_rows(): return lax.ppermute(value, 'rows', [(i, i ^ mask) for i in range(SIDE)])  21.6 us
    ppermute x4, starting transfers between devices, panels_of(): turned = lax.ppermute(four, ('rows', 'cols'), pairs)  18.9 us
    ppermute x12, starting transfers between devices, swap_rows(): return lax.ppermute(value, 'rows', [(i, i ^ mask) for i in range(SIDE)])  17.9 us
  transfers between devices with their start and end apart: 42, of which 30 were waited for; matrix products, arithmetic and copies ran while one was open for 1% of the time, Pallas kernels for 0%

profile of v2, /device:TPU:40, one launch (start us, length us, event | category | flops | bytes accessed | tf_op | source)
XLA Modules:
  0.0 182.6 jit_solution(293702937737854417)
XLA Ops:
  4.8 3.1 %collective-permute-done.1 = f32[1,64,128]{2,1,0:T(8,128)S(1)} collective-permute-done((f32[1,64,128]{2,1,0:T(8,128)}, f32[1,64,128]{2,1,0:T(8,128)S(1)}, u32[]{:S(2)}, u32[]{:S(2)}) %collective-permute-start.1) | collective-permute-done | bytes 32800 | tf_op jit(solution)/shard_map/ppermute | solution.py:146
  8.7 5.5 %collective-permute-start.3 = (f32[4,64,128]{2,1,0:T(8,128)S(1)}, f32[4,64,128]{2,1,0:T(8,128)S(1)}, u32[]{:S(2)}, u32[]{:S(2)}) collective-permute-start(f32[4,64,128]{2,1,0:T(8,128)S(1)} %pad_maximum_fusion.9), channel_id=1, source_target_pairs={{0,128},{1,144},{2,64},{3,80},{4,48},{5,32},{6,240},{7,224},{8,176... | collective-permute-start | bytes 393224 | tf_op jit(solution)/shard_map/ppermute | solution.py:199
  14.9 4.7 %collective-permute-done.3 = f32[4,64,128]{2,1,0:T(8,128)S(1)} collective-permute-done((f32[4,64,128]{2,1,0:T(8,128)S(1)}, f32[4,64,128]{2,1,0:T(8,128)S(1)}, u32[]{:S(2)}, u32[]{:S(2)}) %collective-permute-start.3) | collective-permute-done | bytes 131104 | tf_op jit(solution)/shard_map/ppermute | solution.py:199
  19.6 3.2 %collective-permute-start.4 = (f32[4,64,128]{2,1,0:T(8,128)S(1)}, f32[4,64,128]{2,1,0:T(8,128)S(1)}, u32[]{:S(2)}, u32[]{:S(2)}) collective-permute-start(f32[4,64,128]{2,1,0:T(8,128)S(1)} %collective-permute-done.3), channel_id=1, source_target_pairs={{0,16},{16,0},{32,48},{48,32},{64,80},{80,64},{96,112},{112,96},{1... | collective-permute-start | bytes 393224 | tf_op jit(solution)/shard_map/ppermute | solution.py:150
  26.8 4.1 %collective-permute-done.5 = f32[4,64,128]{2,1,0:T(8,128)S(1)} collective-permute-done((f32[4,64,128]{2,1,0:T(8,128)S(1)}, f32[4,64,128]{2,1,0:T(8,128)S(1)}, u32[]{:S(2)}, u32[]{:S(2)}) %collective-permute-start.5) | collective-permute-done | bytes 131104 | tf_op jit(solution)/shard_map/ppermute | solution.py:150
  31.6 4.5 %shard_map.50 = f32[16,64,128]{2,1,0:T(8,128)S(1)} custom-call(s32[66]{0:T(128)S(1)} %pad_add_fusion.refs_0_, f32[1024,1024]{1,0:T(8,128)} %refs_1_.3, f32[16,64,128]{2,1,0:T(8,128)S(1)} %constant_dynamic-update-slice_fusion.refs_2_), custom_call_target="tpu_custom_call" | custom-call | flops 1610612736 | bytes 8388608 | tf_op jit(solution)/shard_map/pallas_call | solution.py:130
  40.0 4.2 %collective-permute-done.10 = f32[4,64,128]{2,1,0:T(8,128)S(1)} collective-permute-done((f32[4,64,128]{2,1,0:T(8,128)S(1)}, f32[4,64,128]{2,1,0:T(8,128)S(1)}, u32[]{:S(2)}, u32[]{:S(2)}) %collective-permute-start.10) | collective-permute-done | bytes 131104 | tf_op jit(solution)/shard_map/ppermute | solution.py:146
  54.8 4.9 %collective-permute-start.16 = (f32[4,64,128]{2,1,0:T(8,128)S(1)}, f32[4,64,128]{2,1,0:T(8,128)S(1)}, u32[]{:S(2)}, u32[]{:S(2)}) collective-permute-start(f32[4,64,128]{2,1,0:T(8,128)S(1)} %add_add_fusion.2), channel_id=1, source_target_pairs={{0,128},{1,144},{2,64},{3,80},{4,48},{5,32},{6,240},{7,224},{8,176... | collective-permute-start | bytes 393224 | tf_op jit(solution)/shard_map/ppermute | solution.py:199
  59.7 9.4 %collective-permute-done.16 = f32[4,64,128]{2,1,0:T(8,128)S(1)} collective-permute-done((f32[4,64,128]{2,1,0:T(8,128)S(1)}, f32[4,64,128]{2,1,0:T(8,128)S(1)}, u32[]{:S(2)}, u32[]{:S(2)}) %collective-permute-start.16) | collective-permute-done | bytes 131104 | tf_op jit(solution)/shard_map/ppermute | solution.py:199
  73.2 4.6 %collective-permute-done.19 = f32[4,64,128]{2,1,0:T(8,128)S(1)} collective-permute-done((f32[4,64,128]{2,1,0:T(8,128)S(1)}, f32[4,64,128]{2,1,0:T(8,128)S(1)}, u32[]{:S(2)}, u32[]{:S(2)}) %collective-permute-start.19) | collective-permute-done | bytes 131104 | tf_op jit(solution)/shard_map/ppermute | solution.py:150
  78.7 7.3 %shard_map.51 = (f32[1024,1024]{1,0:T(8,128)}, f32[16,64,128]{2,1,0:T(8,128)S(1)}) custom-call(s32[66]{0:T(128)S(1)} %pad_add_fusion.refs_0_, f32[1024,1024]{1,0:T(8,128)} %refs_1_.3, f32[16,64,128]{2,1,0:T(8,128)S(1)} %constant_dynamic-update-slice_fusion.refs_2_, f32[16,64,128]{2,1,0:T(8,128)S(1)} %constant_dynamic-update-slice_fusion.9.refs_3_, ...), custom_call_target="tpu_custom_call" | custom-call | flops 1610612736 | bytes 8388608 | tf_op jit(solution)/shard_map/pallas_call | solution.py:130
  87.7 5.5 %collective-permute-done.21 = f32[4,64,128]{2,1,0:T(8,128)S(1)} collective-permute-done((f32[4,64,128]{2,1,0:T(8,128)S(1)}, f32[4,64,128]{2,1,0:T(8,128)S(1)}, u32[]{:S(2)}, u32[]{:S(2)}) %collective-permute-start.21) | collective-permute-done | bytes 131104 | tf_op jit(solution)/shard_map/ppermute | solution.py:146
  97.8 2.6 %collective-permute-done.24 = f32[4,64,128]{2,1,0:T(8,128)S(1)} collective-permute-done((f32[4,64,128]{2,1,0:T(8,128)S(1)}, f32[4,64,128]{2,1,0:T(8,128)S(1)}, u32[]{:S(2)}, u32[]{:S(2)}) %collective-permute-start.24) | collective-permute-done | bytes 131104 | tf_op jit(solution)/shard_map/ppermute | solution.py:146
  104.0 4.5 %collective-permute-start.27 = (f32[4,64,128]{2,1,0:T(8,128)S(1)}, f32[4,64,128]{2,1,0:T(8,128)S(1)}, u32[]{:S(2)}, u32[]{:S(2)}) collective-permute-start(f32[4,64,128]{2,1,0:T(8,128)S(1)} %add_add_fusion.1), channel_id=1, source_target_pairs={{0,128},{1,144},{2,64},{3,80},{4,48},{5,32},{6,240},{7,224},{8,176... | collective-permute-start | bytes 393224 | tf_op jit(solution)/shard_map/ppermute | solution.py:199
  108.9 6.9 %collective-permute-done.27 = f32[4,64,128]{2,1,0:T(8,128)S(1)} collective-permute-done((f32[4,64,128]{2,1,0:T(8,128)S(1)}, f32[4,64,128]{2,1,0:T(8,128)S(1)}, u32[]{:S(2)}, u32[]{:S(2)}) %collective-permute-start.27) | collective-permute-done | bytes 131104 | tf_op jit(solution)/shard_map/ppermute | solution.py:199
  116.8 3.4 %collective-permute-start.29 = (f32[4,64,128]{2,1,0:T(8,128)S(1)}, f32[4,64,128]{2,1,0:T(8,128)S(1)}, u32[]{:S(2)}, u32[]{:S(2)}) collective-permute-start(f32[4,64,128]{2,1,0:T(8,128)S(1)} %collective-permute-done.27), channel_id=1, source_target_pairs={{0,32},{16,48},{32,0},{48,16},{64,96},{80,112},{96,64},{112,80},{1... | collective-permute-start | bytes 393224 | tf_op jit(solution)/shard_map/ppermute | solution.py:150
  120.2 4.5 %collective-permute-done.30 = f32[4,64,128]{2,1,0:T(8,128)S(1)} collective-permute-done((f32[4,64,128]{2,1,0:T(8,128)S(1)}, f32[4,64,128]{2,1,0:T(8,128)S(1)}, u32[]{:S(2)}, u32[]{:S(2)}) %collective-permute-start.30) | collective-permute-done | bytes 131104 | tf_op jit(solution)/shard_map/ppermute | solution.py:150
  125.7 7.3 %shard_map.52 = (f32[1024,1024]{1,0:T(8,128)}, f32[16,64,128]{2,1,0:T(8,128)S(1)}) custom-call(s32[66]{0:T(128)S(1)} %pad_add_fusion.refs_0_, f32[1024,1024]{1,0:T(8,128)} %get-tuple-element.6.refs_1_, f32[16,64,128]{2,1,0:T(8,128)S(1)} %constant_dynamic-update-slice_fusion.refs_2_, f32[16,64,128]{2,1,0:T(8,128)S(1)} %constant_dynamic-update-slice_fusion.9.refs_3_, ...), custom_call_target="tpu_custom_call" | custom-call | flops 1610612736 | bytes 8388608 | tf_op jit(solution)/shard_map/pallas_call | solution.py:130
  134.8 5.5 %collective-permute-done.32 = f32[4,64,128]{2,1,0:T(8,128)S(1)} collective-permute-done((f32[4,64,128]{2,1,0:T(8,128)S(1)}, f32[4,64,128]{2,1,0:T(8,128)S(1)}, u32[]{:S(2)}, u32[]{:S(2)}) %collective-permute-start.32) | collective-permute-done | bytes 131104 | tf_op jit(solution)/shard_map/ppermute | solution.py:146
  141.9 3.4 %collective-permute-start.34 = (f32[4,64,128]{2,1,0:T(8,128)S(1)}, f32[4,64,128]{2,1,0:T(8,128)S(1)}, u32[]{:S(2)}, u32[]{:S(2)}) collective-permute-start(f32[4,64,128]{2,1,0:T(8,128)S(1)} %slice_add_fusion.3), channel_id=1, source_target_pairs={{0,4},{1,5},{2,6},{3,7},{4,0},{5,1},{6,2},{7,3},{8,12},{9,13},{10,... | collective-permute-start | bytes 393224 | tf_op jit(solution)/shard_map/ppermute | solution.py:146
  152.3 4.0 %collective-permute-start.38 = (f32[4,64,128]{2,1,0:T(8,128)S(1)}, f32[4,64,128]{2,1,0:T(8,128)S(1)}, u32[]{:S(2)}, u32[]{:S(2)}) collective-permute-start(f32[4,64,128]{2,1,0:T(8,128)S(1)} %add_add_fusion), channel_id=1, source_target_pairs={{0,128},{1,144},{2,64},{3,80},{4,48},{5,32},{6,240},{7,224},{8,176... | collective-permute-start | bytes 393224 | tf_op jit(solution)/shard_map/ppermute | solution.py:199
  156.5 9.6 %collective-permute-done.38 = f32[4,64,128]{2,1,0:T(8,128)S(1)} collective-permute-done((f32[4,64,128]{2,1,0:T(8,128)S(1)}, f32[4,64,128]{2,1,0:T(8,128)S(1)}, u32[]{:S(2)}, u32[]{:S(2)}) %collective-permute-start.38) | collective-permute-done | bytes 131104 | tf_op jit(solution)/shard_map/ppermute | solution.py:199
  170.2 3.3 %collective-permute-done.41 = f32[4,64,128]{2,1,0:T(8,128)S(1)} collective-permute-done((f32[4,64,128]{2,1,0:T(8,128)S(1)}, f32[4,64,128]{2,1,0:T(8,128)S(1)}, u32[]{:S(2)}, u32[]{:S(2)}) %collective-permute-start.41) | collective-permute-done | bytes 131104 | tf_op jit(solution)/shard_map/ppermute | solution.py:150
  174.7 7.9 %shard_map.53 = (f32[1024,1024]{1,0:T(8,128)}, f32[1024,1024]{1,0:T(8,128)}) custom-call(s32[66]{0:T(128)S(1)} %pad_add_fusion.refs_0_, f32[1024,1024]{1,0:T(8,128)} %get-tuple-element.8.refs_1_, f32[16,64,128]{2,1,0:T(8,128)S(1)} %constant_dynamic-update-slice_fusion.refs_2_, f32[16,64,128]{2,1,0:T(8,128)S(1)} %constant_dynamic-update-slice_fusion.9.refs_3_, ...), custom_call_target="tpu_custom_call" | custom-call | flops 1610612736 | bytes 8388608 | tf_op jit(solution)/shard_map/pallas_call | solution.py:130
  (103 shorter events, 57.6 us)
Async XLA Ops:
  8.7 10.9 %collective-permute-start.3 = (f32[4,64,128]{2,1,0:T(8,128)S(1)}, f32[4,64,128]{2,1,0:T(8,128)S(1)}, u32[]{:S(2)}, u32[]{:S(2)}) collective-permute-start(f32[4,64,128]{2,1,0:T(8,128)S(1)} %pad_maximum_fusion.9), channel_id=1, source_target_pairs={{0,128},{1,144},{2,64},{3,80},{4,48},{5,32},{6,240},{7,224},{8,176... | collective-permute-start | bytes 393224 | tf_op jit(solution)/shard_map/ppermute | solution.py:199
  19.6 7.1 %collective-permute-start.4 = (f32[4,64,128]{2,1,0:T(8,128)S(1)}, f32[4,64,128]{2,1,0:T(8,128)S(1)}, u32[]{:S(2)}, u32[]{:S(2)}) collective-permute-start(f32[4,64,128]{2,1,0:T(8,128)S(1)} %collective-permute-done.3), channel_id=1, source_target_pairs={{0,16},{16,0},{32,48},{48,32},{64,80},{80,64},{96,112},{112,96},{1... | collective-permute-start | bytes 393224 | tf_op jit(solution)/shard_map/ppermute | solution.py:150
  22.9 8.6 %collective-permute-start.6 = (f32[4,64,128]{2,1,0:T(8,128)S(1)}, f32[4,64,128]{2,1,0:T(8,128)S(1)}, u32[]{:S(2)}, u32[]{:S(2)}) collective-permute-start(f32[4,64,128]{2,1,0:T(8,128)S(1)} %collective-permute-done.3), channel_id=1, source_target_pairs={{0,48},{16,32},{32,16},{48,0},{64,112},{80,96},{96,80},{112,64},{1... | collective-permute-start | bytes 393224 | tf_op jit(solution)/shard_map/ppermute | solution.py:150
  24.4 6.5 %collective-permute-start.5 = (f32[4,64,128]{2,1,0:T(8,128)S(1)}, f32[4,64,128]{2,1,0:T(8,128)S(1)}, u32[]{:S(2)}, u32[]{:S(2)}) collective-permute-start(f32[4,64,128]{2,1,0:T(8,128)S(1)} %collective-permute-done.3), channel_id=1, source_target_pairs={{0,32},{16,48},{32,0},{48,16},{64,96},{80,112},{96,64},{112,80},{1... | collective-permute-start | bytes 393224 | tf_op jit(solution)/shard_map/ppermute | solution.py:150
  37.9 16.7 %collective-permute-start.7 = (f32[4,64,128]{2,1,0:T(8,128)S(1)}, f32[4,64,128]{2,1,0:T(8,128)S(1)}, u32[]{:S(2)}, u32[]{:S(2)}) collective-permute-start(f32[4,64,128]{2,1,0:T(8,128)S(1)} %pad_maximum_fusion.9), channel_id=1, source_target_pairs={{0,8},{1,9},{2,10},{3,11},{4,12},{5,13},{6,14},{7,15},{8,0},{9,1},... | collective-permute-start | bytes 393224 | tf_op jit(solution)/shard_map/ppermute | solution.py:146
  44.2 6.8 %collective-permute-start.13 = (f32[4,64,128]{2,1,0:T(8,128)S(1)}, f32[4,64,128]{2,1,0:T(8,128)S(1)}, u32[]{:S(2)}, u32[]{:S(2)}) collective-permute-start(f32[4,64,128]{2,1,0:T(8,128)S(1)} %slice_add_fusion.5), channel_id=1, source_target_pairs={{0,6},{1,7},{2,4},{3,5},{4,2},{5,3},{6,0},{7,1},{8,14},{9,15},{10,... | collective-permute-start | bytes 393224 | tf_op jit(solution)/shard_map/ppermute | solution.py:146
  46.7 6.6 %collective-permute-start.12 = (f32[4,64,128]{2,1,0:T(8,128)S(1)}, f32[4,64,128]{2,1,0:T(8,128)S(1)}, u32[]{:S(2)}, u32[]{:S(2)}) collective-permute-start(f32[4,64,128]{2,1,0:T(8,128)S(1)} %slice_add_fusion.5), channel_id=1, source_target_pairs={{0,4},{1,5},{2,6},{3,7},{4,0},{5,1},{6,2},{7,3},{8,12},{9,13},{10,... | collective-permute-start | bytes 393224 | tf_op jit(solution)/shard_map/ppermute | solution.py:146
  54.7 18.5 %collective-permute-start.8 = (f32[8,64,128]{2,1,0:T(8,128)S(1)}, f32[8,64,128]{2,1,0:T(8,128)S(1)}, u32[]{:S(2)}, u32[]{:S(2)}) collective-permute-start(f32[8,64,128]{2,1,0:T(8,128)S(1)} %get-tuple-element.10), channel_id=1, source_target_pairs={{0,1},{1,0},{2,3},{3,2},{4,5},{5,4},{6,7},{7,6},{8,9},{9,8},{10,11... | collective-permute-start | bytes 786440 | tf_op jit(solution)/shard_map/ppermute | solution.py:146
  54.8 14.3 %collective-permute-start.16 = (f32[4,64,128]{2,1,0:T(8,128)S(1)}, f32[4,64,128]{2,1,0:T(8,128)S(1)}, u32[]{:S(2)}, u32[]{:S(2)}) collective-permute-start(f32[4,64,128]{2,1,0:T(8,128)S(1)} %add_add_fusion.2), channel_id=1, source_target_pairs={{0,128},{1,144},{2,64},{3,80},{4,48},{5,32},{6,240},{7,224},{8,176... | collective-permute-start | bytes 393224 | tf_op jit(solution)/shard_map/ppermute | solution.py:199
  59.6 19.0 %collective-permute-start.15 = (f32[8,64,128]{2,1,0:T(8,128)S(1)}, f32[8,64,128]{2,1,0:T(8,128)S(1)}, u32[]{:S(2)}, u32[]{:S(2)}) collective-permute-start(f32[8,64,128]{2,1,0:T(8,128)S(1)} %pad_maximum_fusion.6), channel_id=1, source_target_pairs={{0,1},{1,0},{2,3},{3,2},{4,5},{5,4},{6,7},{7,6},{8,9},{9,8},{10,11... | collective-permute-start | bytes 786440 | tf_op jit(solution)/shard_map/ppermute | solution.py:146
  69.1 8.7 %collective-permute-start.19 = (f32[4,64,128]{2,1,0:T(8,128)S(1)}, f32[4,64,128]{2,1,0:T(8,128)S(1)}, u32[]{:S(2)}, u32[]{:S(2)}) collective-permute-start(f32[4,64,128]{2,1,0:T(8,128)S(1)} %collective-permute-done.16), channel_id=1, source_target_pairs={{0,48},{16,32},{32,16},{48,0},{64,112},{80,96},{96,80},{112,64},{1... | collective-permute-start | bytes 393224 | tf_op jit(solution)/shard_map/ppermute | solution.py:150
  69.1 8.7 %collective-permute-start.18 = (f32[4,64,128]{2,1,0:T(8,128)S(1)}, f32[4,64,128]{2,1,0:T(8,128)S(1)}, u32[]{:S(2)}, u32[]{:S(2)}) collective-permute-start(f32[4,64,128]{2,1,0:T(8,128)S(1)} %collective-permute-done.16), channel_id=1, source_target_pairs={{0,32},{16,48},{32,0},{48,16},{64,96},{80,112},{96,64},{112,80},{1... | collective-permute-start | bytes 393224 | tf_op jit(solution)/shard_map/ppermute | solution.py:150
  71.5 7.1 %collective-permute-start.17 = (f32[4,64,128]{2,1,0:T(8,128)S(1)}, f32[4,64,128]{2,1,0:T(8,128)S(1)}, u32[]{:S(2)}, u32[]{:S(2)}) collective-permute-start(f32[4,64,128]{2,1,0:T(8,128)S(1)} %collective-permute-done.16), channel_id=1, source_target_pairs={{0,16},{16,0},{32,48},{48,32},{64,80},{80,64},{96,112},{112,96},{1... | collective-permute-start | bytes 393224 | tf_op jit(solution)/shard_map/ppermute | solution.py:150
  93.3 7.1 %collective-permute-start.24 = (f32[4,64,128]{2,1,0:T(8,128)S(1)}, f32[4,64,128]{2,1,0:T(8,128)S(1)}, u32[]{:S(2)}, u32[]{:S(2)}) collective-permute-start(f32[4,64,128]{2,1,0:T(8,128)S(1)} %slice_add_fusion.4), channel_id=1, source_target_pairs={{0,6},{1,7},{2,4},{3,5},{4,2},{5,3},{6,0},{7,1},{8,14},{9,15},{10,... | collective-permute-start | bytes 393224 | tf_op jit(solution)/shard_map/ppermute | solution.py:146
  95.6 7.3 %collective-permute-start.23 = (f32[4,64,128]{2,1,0:T(8,128)S(1)}, f32[4,64,128]{2,1,0:T(8,128)S(1)}, u32[]{:S(2)}, u32[]{:S(2)}) collective-permute-start(f32[4,64,128]{2,1,0:T(8,128)S(1)} %slice_add_fusion.4), channel_id=1, source_target_pairs={{0,4},{1,5},{2,6},{3,7},{4,0},{5,1},{6,2},{7,3},{8,12},{9,13},{10,... | collective-permute-start | bytes 393224 | tf_op jit(solution)/shard_map/ppermute | solution.py:146
  104.0 11.7 %collective-permute-start.27 = (f32[4,64,128]{2,1,0:T(8,128)S(1)}, f32[4,64,128]{2,1,0:T(8,128)S(1)}, u32[]{:S(2)}, u32[]{:S(2)}) collective-permute-start(f32[4,64,128]{2,1,0:T(8,128)S(1)} %add_add_fusion.1), channel_id=1, source_target_pairs={{0,128},{1,144},{2,64},{3,80},{4,48},{5,32},{6,240},{7,224},{8,176... | collective-permute-start | bytes 393224 | tf_op jit(solution)/shard_map/ppermute | solution.py:199
  108.6 17.1 %collective-permute-start.26 = (f32[8,64,128]{2,1,0:T(8,128)S(1)}, f32[8,64,128]{2,1,0:T(8,128)S(1)}, u32[]{:S(2)}, u32[]{:S(2)}) collective-permute-start(f32[8,64,128]{2,1,0:T(8,128)S(1)} %pad_maximum_fusion.7), channel_id=1, source_target_pairs={{0,1},{1,0},{2,3},{3,2},{4,5},{5,4},{6,7},{7,6},{8,9},{9,8},{10,11... | collective-permute-start | bytes 786440 | tf_op jit(solution)/shard_map/ppermute | solution.py:146
  115.8 8.9 %collective-permute-start.30 = (f32[4,64,128]{2,1,0:T(8,128)S(1)}, f32[4,64,128]{2,1,0:T(8,128)S(1)}, u32[]{:S(2)}, u32[]{:S(2)}) collective-permute-start(f32[4,64,128]{2,1,0:T(8,128)S(1)} %collective-permute-done.27), channel_id=1, source_target_pairs={{0,48},{16,32},{32,16},{48,0},{64,112},{80,96},{96,80},{112,64},{1... | collective-permute-start | bytes 393224 | tf_op jit(solution)/shard_map/ppermute | solution.py:150
  116.8 7.9 %collective-permute-start.29 = (f32[4,64,128]{2,1,0:T(8,128)S(1)}, f32[4,64,128]{2,1,0:T(8,128)S(1)}, u32[]{:S(2)}, u32[]{:S(2)}) collective-permute-start(f32[4,64,128]{2,1,0:T(8,128)S(1)} %collective-permute-done.27), channel_id=1, source_target_pairs={{0,32},{16,48},{32,0},{48,16},{64,96},{80,112},{96,64},{112,80},{1... | collective-permute-start | bytes 393224 | tf_op jit(solution)/shard_map/ppermute | solution.py:150
  141.9 7.2 %collective-permute-start.34 = (f32[4,64,128]{2,1,0:T(8,128)S(1)}, f32[4,64,128]{2,1,0:T(8,128)S(1)}, u32[]{:S(2)}, u32[]{:S(2)}) collective-permute-start(f32[4,64,128]{2,1,0:T(8,128)S(1)} %slice_add_fusion.3), channel_id=1, source_target_pairs={{0,4},{1,5},{2,6},{3,7},{4,0},{5,1},{6,2},{7,3},{8,12},{9,13},{10,... | collective-permute-start | bytes 393224 | tf_op jit(solution)/shard_map/ppermute | solution.py:146
  152.3 13.9 %collective-permute-start.38 = (f32[4,64,128]{2,1,0:T(8,128)S(1)}, f32[4,64,128]{2,1,0:T(8,128)S(1)}, u32[]{:S(2)}, u32[]{:S(2)}) collective-permute-start(f32[4,64,128]{2,1,0:T(8,128)S(1)} %add_add_fusion), channel_id=1, source_target_pairs={{0,128},{1,144},{2,64},{3,80},{4,48},{5,32},{6,240},{7,224},{8,176... | collective-permute-start | bytes 393224 | tf_op jit(solution)/shard_map/ppermute | solution.py:199
  156.3 18.3 %collective-permute-start.37 = (f32[8,64,128]{2,1,0:T(8,128)S(1)}, f32[8,64,128]{2,1,0:T(8,128)S(1)}, u32[]{:S(2)}, u32[]{:S(2)}) collective-permute-start(f32[8,64,128]{2,1,0:T(8,128)S(1)} %pad_maximum_fusion.8), channel_id=1, source_target_pairs={{0,1},{1,0},{2,3},{3,2},{4,5},{5,4},{6,7},{7,6},{8,9},{9,8},{10,11... | collective-permute-start | bytes 786440 | tf_op jit(solution)/shard_map/ppermute | solution.py:146
  166.1 7.4 %collective-permute-start.41 = (f32[4,64,128]{2,1,0:T(8,128)S(1)}, f32[4,64,128]{2,1,0:T(8,128)S(1)}, u32[]{:S(2)}, u32[]{:S(2)}) collective-permute-start(f32[4,64,128]{2,1,0:T(8,128)S(1)} %collective-permute-done.38), channel_id=1, source_target_pairs={{0,48},{16,32},{32,16},{48,0},{64,112},{80,96},{96,80},{112,64},{1... | collective-permute-start | bytes 393224 | tf_op jit(solution)/shard_map/ppermute | solution.py:150
  166.1 7.7 %collective-permute-start.40 = (f32[4,64,128]{2,1,0:T(8,128)S(1)}, f32[4,64,128]{2,1,0:T(8,128)S(1)}, u32[]{:S(2)}, u32[]{:S(2)}) collective-permute-start(f32[4,64,128]{2,1,0:T(8,128)S(1)} %collective-permute-done.38), channel_id=1, source_target_pairs={{0,32},{16,48},{32,0},{48,16},{64,96},{80,112},{96,64},{112,80},{1... | collective-permute-start | bytes 393224 | tf_op jit(solution)/shard_map/ppermute | solution.py:150
  (19 other events, 100.5 us)

commit v3 on v0

v3 whole, which is shorter than its diff:
```python
import functools

import jax
import jax.numpy as jnp
import numpy as np
from jax import lax
from jax.experimental import pallas as pl
from jax.experimental.pallas import tpu as pltpu
from jax.sharding import PartitionSpec as P

ITERS = 3

step_size = 0.005
penalty = 4.0

SIDE = 16
PIECE = 64
TILE = 512
FETCHES = 8
NT = (((1,), (1,)), ((), ()))


def split(value):
    high = value.astype(jnp.bfloat16)
    low = (value - high.astype(jnp.float32)).astype(jnp.bfloat16)
    return high, low


def dot(a, b, dims=(((1,), (0,)), ((), ()))):
    return lax.dot_general(a, b, dims, preferred_element_type=jnp.float32)


def load_panels(update, emit_sums, frame_count, place, xc, xr, yr, yc, ah, al, bh, bl, xx):
    for q in range(SIDE):
        span = pl.ds(q * PIECE, PIECE)
        high, low = split(xc[place[2 + q]])
        if emit_sums:
            xx[span, :frame_count] = high
            xx[span, frame_count:] = low
        if update:
            bh[span, :frame_count] = high
            bl[span, :frame_count] = low
            high, low = split(yc[place[34 + q]])
            bh[span, frame_count:] = high
            bl[span, frame_count:] = low
            high, low = split(yr[place[50 + q]])
            ah[span, :frame_count] = high
            al[span, :frame_count] = low
            high, low = split(xr[place[18 + q]])
            ah[span, frame_count:] = high
            al[span, frame_count:] = low


def gradient_part(frame_count, a_high, a_low, b_high, b_low):
    return (dot(a_high, b_high, NT) + dot(a_high, b_low, NT) + dot(a_low, b_high, NT)) * (0.5 / frame_count)


def step(old, g, eye):
    bound = step_size * penalty
    if eye is not None:
        g = g - jnp.where(eye, 1.0 / jnp.where(eye, old, 1.0), 0.0)
    moved = old - step_size * g
    cut = jnp.clip(moved, -bound, bound)
    if eye is not None:
        cut = jnp.where(eye, 0.0, cut)
    return g, moved - cut


def diagonal(on):
    eye = lax.broadcasted_iota(jnp.int32, (TILE, TILE), 0) == lax.broadcasted_iota(jnp.int32, (TILE, TILE), 1)
    return jnp.logical_and(eye, on)


def sweep_kernel(update, frame_count, *refs):
    if update:
        place, omega, xc, xr, yr, yc, out, sums, ah, al, bh, bl, xx = refs
        load_panels(True, True, frame_count, place, xc, xr, yr, yc, ah, al, bh, bl, xx)
    else:
        place, whole, xc, omega, sums, xx, arrived = refs
        step_rows = whole.shape[0] // FETCHES
        fetches = []
        for n in range(FETCHES):
            part = pl.ds(n * step_rows, step_rows)
            fetches.append(pltpu.make_async_copy(whole.at[part, :], omega.at[part, :], arrived.at[n]))
            fetches[-1].start()
        load_panels(False, True, frame_count, place, xc, None, None, None, None, None, None, None, xx)
    rows = omega.shape[0]
    col = place[1]
    here = place[0] == col
    for t in range(rows // TILE):
        mine = slice(t * TILE, t * TILE + TILE)
        both = rest = None
        if not update:
            for n in range(t * TILE // step_rows, (t + 1) * TILE // step_rows):
                fetches[n].wait()
        for j in range(rows // TILE):
            span = slice(j * TILE, j * TILE + TILE)
            value = omega[mine, span]
            if update:
                g = gradient_part(frame_count, ah[mine, :], al[mine, :], bh[span, :], bl[span, :])
                _, value = step(value, g, diagonal(here) if j == t else None)
                out[mine, span] = value
            high, low = split(value)
            first = dot(high, xx[span, :])
            second = dot(low, xx[span, :frame_count])
            both = first if both is None else both + first
            rest = second if rest is None else rest + second
        total = both[:, :frame_count] + both[:, frame_count:] + rest
        for s in range(TILE // PIECE):
            q = t * (TILE // PIECE) + s
            slot = ((q ^ col) & 1) * 8 + ((q ^ col) >> 3) * 4 + ((q >> 1) & 3)
            sums[slot] = total[s * PIECE : (s + 1) * PIECE]


def sweep(place, omega, xc, panels):
    update = bool(panels)
    rows = omega.shape[0]
    frame_count = xc.shape[-1]
    wide = pltpu.VMEM((rows, 2 * frame_count), jnp.bfloat16)
    vmem = pl.BlockSpec(memory_space=pltpu.VMEM)
    shapes = [pltpu.VMEM(omega.shape, jnp.float32), jax.ShapeDtypeStruct((SIDE, PIECE, frame_count), jnp.float32)]
    home = pltpu.VMEM if update else pltpu.HBM
    return pl.pallas_call(
        functools.partial(sweep_kernel, update, frame_count),
        out_shape=shapes,
        in_specs=[pl.BlockSpec(memory_space=pltpu.SMEM), pl.BlockSpec(memory_space=home)] + [vmem] * (1 + len(panels)),
        out_specs=[vmem] * 2,
        scratch_shapes=[wide] * 5 if update else [wide, pltpu.SemaphoreType.DMA((FETCHES,))],
        compiler_params=pltpu.CompilerParams(vmem_limit_bytes=28 * 1024 * 1024),
        cost_estimate=pl.CostEstimate(flops=4 * rows * rows * frame_count * 3, bytes_accessed=8 * rows * rows, transcendentals=0),
    )(place, pltpu.with_memory_space_constraint(omega, home), xc, *panels)


def final_kernel(frame_count, place, omega, xc, xr, yr, yc, out, grad, ah, al, bh, bl, values, grads, sent):
    load_panels(True, False, frame_count, place, xc, xr, yr, yc, ah, al, bh, bl, None)
    rows = omega.shape[0]
    here = place[0] == place[1]
    copies = []
    for t in range(rows // TILE):
        mine = slice(t * TILE, t * TILE + TILE)
        for j in range(rows // TILE):
            span = slice(j * TILE, j * TILE + TILE)
            g = gradient_part(frame_count, ah[mine, :], al[mine, :], bh[span, :], bl[span, :])
            g, value = step(omega[mine, span], g, diagonal(here) if j == t else None)
            grads[mine, span] = g
            values[mine, span] = value
            for held, there in ((grads, grad), (values, out)):
                block = (pl.ds(t * TILE, TILE), pl.ds(j * TILE, TILE))
                copies.append(pltpu.make_async_copy(held.at[block], there.at[block], sent.at[len(copies)]))
                copies[-1].start()
    for copy in copies:
        copy.wait()


def final_sweep(place, omega, xc, panels):
    rows = omega.shape[0]
    frame_count = xc.shape[-1]
    wide = pltpu.VMEM((rows, 2 * frame_count), jnp.bfloat16)
    vmem = pl.BlockSpec(memory_space=pltpu.VMEM)
    return pl.pallas_call(
        functools.partial(final_kernel, frame_count),
        out_shape=[pltpu.HBM(omega.shape, jnp.float32)] * 2,
        in_specs=[pl.BlockSpec(memory_space=pltpu.SMEM)] + [vmem] * (2 + len(panels)),
        out_specs=[pl.BlockSpec(memory_space=pltpu.HBM)] * 2,
        scratch_shapes=[wide] * 4
        + [pltpu.VMEM(omega.shape, jnp.float32)] * 2
        + [pltpu.SemaphoreType.DMA((2 * (rows // TILE) ** 2,))],
        compiler_params=pltpu.CompilerParams(vmem_limit_bytes=28 * 1024 * 1024),
        cost_estimate=pl.CostEstimate(flops=4 * rows * rows * frame_count * 3, bytes_accessed=12 * rows * rows, transcendentals=0),
    )(place, pltpu.with_memory_space_constraint(omega, pltpu.VMEM), xc, *panels)


def swap_cols(value, mask):
    return lax.ppermute(value, "cols", [(i, i ^ mask) for i in range(SIDE)])


def swap_rows(value, mask):
    return lax.ppermute(value, "rows", [(i, i ^ mask) for i in range(SIDE)])


ROWS = (
    "b9f71c52ea83046d",
    "a864d20fcb1e5397",
    "5ca9e4128bf07d36",
    "6fd8b3071a9ce542",
    "70259fcb68ade134",
    "4187ea2d950cf36b",
    "e075398f42abd61c",
    "b1264acd5f8739e0",
    "d23f58b4610a9ce7",
    "7ea018d6235fcb94",
    "a4c0296ed7135fb8",
    "35d18f7bac2460e9",
    "9fe4601bcd2875a3",
    "ca5d3782efb14609",
    "17e8ad43f92c60b5",
    "60fb9c25e83d71a4",
)


LANDING = {(r, c): (int(ROWS[r][c], SIDE), r) for r in range(SIDE) for c in range(SIDE)}
SOURCE = {there: here for here, there in LANDING.items()}


def slots():
    table = np.zeros((SIDE, SIDE, 4, SIDE), np.int32)
    for r in range(SIDE):
        for c in range(SIDE):
            found = {}
            for hop in range(4):
                near = SOURCE[r ^ hop, c][1]
                for y in range(4):
                    found[near & 9 | y << 1] = hop * 4 + y, hop * 4 + (y ^ (near >> 1 & 3))
            for q in range(SIDE):
                y = (q >> 1) & 3
                side = ((q ^ c) & 1) * 8 + ((q ^ c) >> 3) * 4
                table[r, c, 0, q] = found[q][1]
                table[r, c, 1, q] = side + (y ^ ((c >> 1) & 3))
                table[r, c, 2, q] = found[q][0]
                table[r, c, 3, q] = side + y
    return table.reshape(SIDE, SIDE, 4 * SIDE)


def sum_near(sums):
    value = sums[:8] + swap_cols(sums[8:], 1)
    value = value[:4] + swap_cols(value[4:], 8)
    others = [swap_cols(value, 2 * m) for m in (1, 2, 3)]
    return (value + others[0]) + (others[1] + others[2])


def gather_near(piece):
    value = piece[None]
    return jnp.concatenate([value] + [swap_cols(value, 2 * m) for m in (1, 2, 3)], 0)


def turn(four):
    pairs = [(r * SIDE + c, LANDING[r, c][0] * SIDE + LANDING[r, c][1]) for r in range(SIDE) for c in range(SIDE)]
    turned = lax.ppermute(four, ("rows", "cols"), pairs)
    return jnp.concatenate([turned] + [swap_rows(turned, m) for m in (1, 2, 3)], 0)


def along(four):
    value = jnp.concatenate([four, swap_cols(four, 8)], 0)
    return jnp.concatenate([value, swap_cols(value, 1)], 0)


def on_device(frames, precision):
    row, col = lax.axis_index("rows"), lax.axis_index("cols")
    table = lax.dynamic_slice(jnp.asarray(slots()), (row, col, 0), (1, 1, 4 * SIDE)).reshape(-1)
    place = jnp.concatenate([jnp.stack([row, col]).astype(jnp.int32), table])
    own = gather_near(frames.T)
    xc = turn(own)
    xr = along(own)
    current, sums = sweep(place, precision, xc, ())
    for index in range(ITERS):
        four = sum_near(sums)
        yc = turn(four)
        yr = along(four)
        if index < ITERS - 1:
            current, sums = sweep(place, current, xc, (xr, yr, yc))
        else:
            current, gradient = final_sweep(place, current, xc, (xr, yr, yc))
    return (current, gradient)


def solution(mesh):
    placed = (P(None, ("rows", "cols")), P("rows", "cols"))
    return jax.shard_map(
        on_device,
        mesh=mesh,
        in_specs=placed,
        out_specs=(P("rows", "cols"), P("rows", "cols")),
        check_vma=False,
    )
```

time: 1380 us -> 168 us (0.12)
  waiting for transfers between devices: 1250 us -> 83.5 us
  matrix products: 106 us -> 0 us
  starting transfers between devices: 0.54 us -> 63.6 us
  Pallas kernels: 0 us -> 16.6 us
    psum x6 -> x0, waiting for transfers between devices: 829 us -> none  [the longest x3 498 us: on_device(): weighted = lax.psum(local_cols, 'rows')]
    all_gather x1 -> x0, waiting for transfers between devices: 420 us -> none  [on_device(): everything = lax.all_gather(frames, ('rows', 'cols'), axis=1, tiled=True)]
    dot_general x12 -> x0, matrix products: 106 us -> none  [the longest x3 31 us: on_device(): lax.dot_general(current, col_panel, (((1,), (1,)), ((), ())), precision=h...]
    ppermute x0 -> x42, waiting for transfers between devices: none -> 83.5 us  [the longest x26 38.2 us: swap_cols(): return lax.ppermute(value, 'cols', [(i, i ^ mask) for i in range(SIDE)])]
    ppermute x0 -> x42, starting transfers between devices: none -> 63.6 us  [the longest x4 23.5 us: turn(): turned = lax.ppermute(four, ('rows', 'cols'), pairs)]
    pallas_call x0 -> x4, Pallas kernels: none -> 16.6 us  [the longest x3 11.8 us: sweep(): pl.pallas_call(functools.partial(sweep_kernel, update, frame_count), out_...]
  transfers between devices with their start and end apart: 7 -> 42, of which waited for: 7 -> 28; matrix products, arithmetic and copies ran while one was open for 3% -> 1% of each run, Pallas kernels for 0% -> 0%
where the time goes in v3:
time: 168 us; the launch traced here: 167 us
  waiting for transfers between devices  83.5 us (50%)
  starting transfers between devices  63.6 us (38%)
  Pallas kernels  16.6 us (10%)
    ppermute x26, waiting for transfers between devices, swap_cols(): return lax.ppermute(value, 'cols', [(i, i ^ mask) for i in range(SIDE)])  38.2 us
    ppermute x4, starting transfers between devices, turn(): turned = lax.ppermute(four, ('rows', 'cols'), pairs)  23.5 us
    ppermute x4, waiting for transfers between devices, turn(): turned = lax.ppermute(four, ('rows', 'cols'), pairs)  23 us
    ppermute x26, starting transfers between devices, swap_cols(): return lax.ppermute(value, 'cols', [(i, i ^ mask) for i in range(SIDE)])  22.5 us
    ppermute x12, waiting for transfers between devices, swap_rows(): return lax.ppermute(value, 'rows', [(i, i ^ mask) for i in range(SIDE)])  22.3 us
    ppermute x12, starting transfers between devices, swap_rows(): return lax.ppermute(value, 'rows', [(i, i ^ mask) for i in range(SIDE)])  17.6 us
    pallas_call x3, Pallas kernels, sweep(): pl.pallas_call(functools.partial(sweep_kernel, update, frame_count), out_...  11.8 us
    pallas_call x1, Pallas kernels, final_sweep(): pl.pallas_call(functools.partial(final_kernel, frame_count), out_shape=[p...  4.81 us
  transfers between devices with their start and end apart: 42, of which 28 were waited for; matrix products, arithmetic and copies ran while one was open for 1% of the time, Pallas kernels for 0%

profile of v3, /device:TPU:40, one launch (start us, length us, event | category | flops | bytes accessed | tf_op | source)
XLA Modules:
  0.0 167.0 jit_solution(5338493127206344298)
XLA Ops:
  4.8 3.1 %collective-permute-done.1 = f32[1,64,128]{2,1,0:T(8,128)S(1)} collective-permute-done((f32[1,64,128]{2,1,0:T(8,128)}, f32[1,64,128]{2,1,0:T(8,128)S(1)}, u32[]{:S(2)}, u32[]{:S(2)}) %collective-permute-start.1) | collective-permute-done | bytes 32800 | tf_op jit(solution)/shard_map/ppermute | solution.py:174
  8.7 7.2 %collective-permute-start.3 = (f32[4,64,128]{2,1,0:T(8,128)S(1)}, f32[4,64,128]{2,1,0:T(8,128)S(1)}, u32[]{:S(2)}, u32[]{:S(2)}) collective-permute-start(f32[4,64,128]{2,1,0:T(8,128)S(1)} %pad_maximum_fusion.9), channel_id=1, source_target_pairs={{0,176},{1,144},{2,240},{3,112},{4,16},{5,192},{6,80},{7,32},{8,22... | collective-permute-start | bytes 393224 | tf_op jit(solution)/shard_map/ppermute | solution.py:238
  18.6 3.0 %collective-permute-start.4 = (f32[4,64,128]{2,1,0:T(8,128)S(1)}, f32[4,64,128]{2,1,0:T(8,128)S(1)}, u32[]{:S(2)}, u32[]{:S(2)}) collective-permute-start(f32[4,64,128]{2,1,0:T(8,128)S(1)} %collective-permute-done.3), channel_id=1, source_target_pairs={{0,16},{16,0},{32,48},{48,32},{64,80},{80,64},{96,112},{112,96},{1... | collective-permute-start | bytes 393224 | tf_op jit(solution)/shard_map/ppermute | solution.py:178
  25.9 4.6 %collective-permute-done.5 = f32[4,64,128]{2,1,0:T(8,128)S(1)} collective-permute-done((f32[4,64,128]{2,1,0:T(8,128)S(1)}, f32[4,64,128]{2,1,0:T(8,128)S(1)}, u32[]{:S(2)}, u32[]{:S(2)}) %collective-permute-start.5) | collective-permute-done | bytes 131104 | tf_op jit(solution)/shard_map/ppermute | solution.py:178
  30.5 3.6 %shard_map.50 = (f32[1024,1024]{1,0:T(8,128)S(1)}, f32[16,64,128]{2,1,0:T(8,128)S(1)}) custom-call(s32[66]{0:T(128)S(1)} %pad_add_fusion.refs_0_.place, f32[1024,1024]{1,0:T(8,128)} %refs_1_.1, f32[16,64,128]{2,1,0:T(8,128)S(1)} %constant_dynamic-update-slice_fusion.refs_2_.xc), custom_call_target="tpu_custom_call" | custom-call | flops 1610612736 | bytes 8388608 | tf_op jit(solution)/shard_map/pallas_call | solution.py:123
  38.0 4.2 %collective-permute-done.10 = f32[4,64,128]{2,1,0:T(8,128)S(1)} collective-permute-done((f32[4,64,128]{2,1,0:T(8,128)S(1)}, f32[4,64,128]{2,1,0:T(8,128)S(1)}, u32[]{:S(2)}, u32[]{:S(2)}) %collective-permute-start.10) | collective-permute-done | bytes 131104 | tf_op jit(solution)/shard_map/ppermute | solution.py:174
  43.8 3.9 %collective-permute-start.12 = (f32[4,64,128]{2,1,0:T(8,128)S(1)}, f32[4,64,128]{2,1,0:T(8,128)S(1)}, u32[]{:S(2)}, u32[]{:S(2)}) collective-permute-start(f32[4,64,128]{2,1,0:T(8,128)S(1)} %slice_add_fusion.5), channel_id=1, source_target_pairs={{0,4},{1,5},{2,6},{3,7},{4,0},{5,1},{6,2},{7,3},{8,12},{9,13},{10,... | collective-permute-start | bytes 393224 | tf_op jit(solution)/shard_map/ppermute | solution.py:174
  52.9 6.7 %collective-permute-start.16 = (f32[4,64,128]{2,1,0:T(8,128)S(1)}, f32[4,64,128]{2,1,0:T(8,128)S(1)}, u32[]{:S(2)}, u32[]{:S(2)}) collective-permute-start(f32[4,64,128]{2,1,0:T(8,128)S(1)} %add_add_fusion.2), channel_id=1, source_target_pairs={{0,176},{1,144},{2,240},{3,112},{4,16},{5,192},{6,80},{7,32},{8,22... | collective-permute-start | bytes 393224 | tf_op jit(solution)/shard_map/ppermute | solution.py:238
  59.7 5.9 %collective-permute-done.16 = f32[4,64,128]{2,1,0:T(8,128)S(1)} collective-permute-done((f32[4,64,128]{2,1,0:T(8,128)S(1)}, f32[4,64,128]{2,1,0:T(8,128)S(1)}, u32[]{:S(2)}, u32[]{:S(2)}) %collective-permute-start.16) | collective-permute-done | bytes 131104 | tf_op jit(solution)/shard_map/ppermute | solution.py:238
  69.7 5.9 %collective-permute-done.19 = f32[4,64,128]{2,1,0:T(8,128)S(1)} collective-permute-done((f32[4,64,128]{2,1,0:T(8,128)S(1)}, f32[4,64,128]{2,1,0:T(8,128)S(1)}, u32[]{:S(2)}, u32[]{:S(2)}) %collective-permute-start.19) | collective-permute-done | bytes 131104 | tf_op jit(solution)/shard_map/ppermute | solution.py:178
  76.9 4.1 %shard_map.51 = (f32[1024,1024]{1,0:T(8,128)S(1)}, f32[16,64,128]{2,1,0:T(8,128)S(1)}) custom-call(s32[66]{0:T(128)S(1)} %pad_add_fusion.refs_0_.place, f32[1024,1024]{1,0:T(8,128)S(1)} %get-tuple-element.8.refs_1_, f32[16,64,128]{2,1,0:T(8,128)S(1)} %constant_dynamic-update-slice_fusion.refs_2_.xc, ...), custom_call_target="tpu_custom_call" | custom-call | flops 1610612736 | bytes 8388608 | tf_op jit(solution)/shard_map/pallas_call | solution.py:123
  82.8 5.5 %collective-permute-done.21 = f32[4,64,128]{2,1,0:T(8,128)S(1)} collective-permute-done((f32[4,64,128]{2,1,0:T(8,128)S(1)}, f32[4,64,128]{2,1,0:T(8,128)S(1)}, u32[]{:S(2)}, u32[]{:S(2)}) %collective-permute-start.21) | collective-permute-done | bytes 131104 | tf_op jit(solution)/shard_map/ppermute | solution.py:174
  92.5 3.3 %collective-permute-done.24 = f32[4,64,128]{2,1,0:T(8,128)S(1)} collective-permute-done((f32[4,64,128]{2,1,0:T(8,128)S(1)}, f32[4,64,128]{2,1,0:T(8,128)S(1)}, u32[]{:S(2)}, u32[]{:S(2)}) %collective-permute-start.24) | collective-permute-done | bytes 131104 | tf_op jit(solution)/shard_map/ppermute | solution.py:174
  98.4 4.4 %collective-permute-start.27 = (f32[4,64,128]{2,1,0:T(8,128)S(1)}, f32[4,64,128]{2,1,0:T(8,128)S(1)}, u32[]{:S(2)}, u32[]{:S(2)}) collective-permute-start(f32[4,64,128]{2,1,0:T(8,128)S(1)} %add_add_fusion.1), channel_id=1, source_target_pairs={{0,176},{1,144},{2,240},{3,112},{4,16},{5,192},{6,80},{7,32},{8,22... | collective-permute-start | bytes 393224 | tf_op jit(solution)/shard_map/ppermute | solution.py:238
  103.0 7.8 %collective-permute-done.27 = f32[4,64,128]{2,1,0:T(8,128)S(1)} collective-permute-done((f32[4,64,128]{2,1,0:T(8,128)S(1)}, f32[4,64,128]{2,1,0:T(8,128)S(1)}, u32[]{:S(2)}, u32[]{:S(2)}) %collective-permute-start.27) | collective-permute-done | bytes 131104 | tf_op jit(solution)/shard_map/ppermute | solution.py:238
  114.9 3.5 %collective-permute-done.30 = f32[4,64,128]{2,1,0:T(8,128)S(1)} collective-permute-done((f32[4,64,128]{2,1,0:T(8,128)S(1)}, f32[4,64,128]{2,1,0:T(8,128)S(1)}, u32[]{:S(2)}, u32[]{:S(2)}) %collective-permute-start.30) | collective-permute-done | bytes 131104 | tf_op jit(solution)/shard_map/ppermute | solution.py:178
  119.3 4.1 %shard_map.52 = (f32[1024,1024]{1,0:T(8,128)S(1)}, f32[16,64,128]{2,1,0:T(8,128)S(1)}) custom-call(s32[66]{0:T(128)S(1)} %pad_add_fusion.refs_0_.place, f32[1024,1024]{1,0:T(8,128)S(1)} %get-tuple-element.10.refs_1_, f32[16,64,128]{2,1,0:T(8,128)S(1)} %constant_dynamic-update-slice_fusion.refs_2_.xc, ...), custom_call_target="tpu_custom_call" | custom-call | flops 1610612736 | bytes 8388608 | tf_op jit(solution)/shard_map/pallas_call | solution.py:123
  125.2 5.5 %collective-permute-done.32 = f32[4,64,128]{2,1,0:T(8,128)S(1)} collective-permute-done((f32[4,64,128]{2,1,0:T(8,128)S(1)}, f32[4,64,128]{2,1,0:T(8,128)S(1)}, u32[]{:S(2)}, u32[]{:S(2)}) %collective-permute-start.32) | collective-permute-done | bytes 131104 | tf_op jit(solution)/shard_map/ppermute | solution.py:174
  130.9 3.2 %collective-permute-start.34 = (f32[4,64,128]{2,1,0:T(8,128)S(1)}, f32[4,64,128]{2,1,0:T(8,128)S(1)}, u32[]{:S(2)}, u32[]{:S(2)}) collective-permute-start(f32[4,64,128]{2,1,0:T(8,128)S(1)} %slice_add_fusion.3), channel_id=1, source_target_pairs={{0,4},{1,5},{2,6},{3,7},{4,0},{5,1},{6,2},{7,3},{8,12},{9,13},{10,... | collective-permute-start | bytes 393224 | tf_op jit(solution)/shard_map/ppermute | solution.py:174
  134.9 3.4 %collective-permute-done.35 = f32[4,64,128]{2,1,0:T(8,128)S(1)} collective-permute-done((f32[4,64,128]{2,1,0:T(8,128)S(1)}, f32[4,64,128]{2,1,0:T(8,128)S(1)}, u32[]{:S(2)}, u32[]{:S(2)}) %collective-permute-start.35) | collective-permute-done | bytes 131104 | tf_op jit(solution)/shard_map/ppermute | solution.py:174
  140.9 5.1 %collective-permute-start.38 = (f32[4,64,128]{2,1,0:T(8,128)S(1)}, f32[4,64,128]{2,1,0:T(8,128)S(1)}, u32[]{:S(2)}, u32[]{:S(2)}) collective-permute-start(f32[4,64,128]{2,1,0:T(8,128)S(1)} %add_add_fusion), channel_id=1, source_target_pairs={{0,176},{1,144},{2,240},{3,112},{4,16},{5,192},{6,80},{7,32},{8,22... | collective-permute-start | bytes 393224 | tf_op jit(solution)/shard_map/ppermute | solution.py:238
  146.1 7.4 %collective-permute-done.38 = f32[4,64,128]{2,1,0:T(8,128)S(1)} collective-permute-done((f32[4,64,128]{2,1,0:T(8,128)S(1)}, f32[4,64,128]{2,1,0:T(8,128)S(1)}, u32[]{:S(2)}, u32[]{:S(2)}) %collective-permute-start.38) | collective-permute-done | bytes 131104 | tf_op jit(solution)/shard_map/ppermute | solution.py:238
  157.6 3.5 %collective-permute-done.41 = f32[4,64,128]{2,1,0:T(8,128)S(1)} collective-permute-done((f32[4,64,128]{2,1,0:T(8,128)S(1)}, f32[4,64,128]{2,1,0:T(8,128)S(1)}, u32[]{:S(2)}, u32[]{:S(2)}) %collective-permute-start.41) | collective-permute-done | bytes 131104 | tf_op jit(solution)/shard_map/ppermute | solution.py:178
  162.0 4.8 %shard_map.53 = (f32[1024,1024]{1,0:T(8,128)}, f32[1024,1024]{1,0:T(8,128)}) custom-call(s32[66]{0:T(128)S(1)} %pad_add_fusion.refs_0_.place, f32[1024,1024]{1,0:T(8,128)S(1)} %get-tuple-element.12.omega, f32[16,64,128]{2,1,0:T(8,128)S(1)} %constant_dynamic-update-slice_fusion.refs_2_.xc, f32[16,64,128]{2,1,0:T(8,128)S(1)} %constant_dynamic-update-slice_fusion.9.refs_3_.xr, ...), custom_call_target="tpu_custom_call" | custom-call | flops 1610612736 | bytes 12582912 | tf_op jit(solution)/shard_map/pallas_call | solution.py:160
  (103 shorter events, 52.3 us)
Async XLA Ops:
  8.7 9.9 %collective-permute-start.3 = (f32[4,64,128]{2,1,0:T(8,128)S(1)}, f32[4,64,128]{2,1,0:T(8,128)S(1)}, u32[]{:S(2)}, u32[]{:S(2)}) collective-permute-start(f32[4,64,128]{2,1,0:T(8,128)S(1)} %pad_maximum_fusion.9), channel_id=1, source_target_pairs={{0,176},{1,144},{2,240},{3,112},{4,16},{5,192},{6,80},{7,32},{8,22... | collective-permute-start | bytes 393224 | tf_op jit(solution)/shard_map/ppermute | solution.py:238
  18.6 7.3 %collective-permute-start.4 = (f32[4,64,128]{2,1,0:T(8,128)S(1)}, f32[4,64,128]{2,1,0:T(8,128)S(1)}, u32[]{:S(2)}, u32[]{:S(2)}) collective-permute-start(f32[4,64,128]{2,1,0:T(8,128)S(1)} %collective-permute-done.3), channel_id=1, source_target_pairs={{0,16},{16,0},{32,48},{48,32},{64,80},{80,64},{96,112},{112,96},{1... | collective-permute-start | bytes 393224 | tf_op jit(solution)/shard_map/ppermute | solution.py:178
  21.6 8.9 %collective-permute-start.6 = (f32[4,64,128]{2,1,0:T(8,128)S(1)}, f32[4,64,128]{2,1,0:T(8,128)S(1)}, u32[]{:S(2)}, u32[]{:S(2)}) collective-permute-start(f32[4,64,128]{2,1,0:T(8,128)S(1)} %collective-permute-done.3), channel_id=1, source_target_pairs={{0,48},{16,32},{32,16},{48,0},{64,112},{80,96},{96,80},{112,64},{1... | collective-permute-start | bytes 393224 | tf_op jit(solution)/shard_map/ppermute | solution.py:178
  35.9 16.8 %collective-permute-start.7 = (f32[4,64,128]{2,1,0:T(8,128)S(1)}, f32[4,64,128]{2,1,0:T(8,128)S(1)}, u32[]{:S(2)}, u32[]{:S(2)}) collective-permute-start(f32[4,64,128]{2,1,0:T(8,128)S(1)} %pad_maximum_fusion.9), channel_id=1, source_target_pairs={{0,8},{1,9},{2,10},{3,11},{4,12},{5,13},{6,14},{7,15},{8,0},{9,1},... | collective-permute-start | bytes 393224 | tf_op jit(solution)/shard_map/ppermute | solution.py:174
  43.8 7.7 %collective-permute-start.12 = (f32[4,64,128]{2,1,0:T(8,128)S(1)}, f32[4,64,128]{2,1,0:T(8,128)S(1)}, u32[]{:S(2)}, u32[]{:S(2)}) collective-permute-start(f32[4,64,128]{2,1,0:T(8,128)S(1)} %slice_add_fusion.5), channel_id=1, source_target_pairs={{0,4},{1,5},{2,6},{3,7},{4,0},{5,1},{6,2},{7,3},{8,12},{9,13},{10,... | collective-permute-start | bytes 393224 | tf_op jit(solution)/shard_map/ppermute | solution.py:174
  52.8 16.9 %collective-permute-start.8 = (f32[8,64,128]{2,1,0:T(8,128)S(1)}, f32[8,64,128]{2,1,0:T(8,128)S(1)}, u32[]{:S(2)}, u32[]{:S(2)}) collective-permute-start(f32[8,64,128]{2,1,0:T(8,128)S(1)} %get-tuple-element.14), channel_id=1, source_target_pairs={{0,1},{1,0},{2,3},{3,2},{4,5},{5,4},{6,7},{7,6},{8,9},{9,8},{10,11... | collective-permute-start | bytes 786440 | tf_op jit(solution)/shard_map/ppermute | solution.py:174
  52.9 12.7 %collective-permute-start.16 = (f32[4,64,128]{2,1,0:T(8,128)S(1)}, f32[4,64,128]{2,1,0:T(8,128)S(1)}, u32[]{:S(2)}, u32[]{:S(2)}) collective-permute-start(f32[4,64,128]{2,1,0:T(8,128)S(1)} %add_add_fusion.2), channel_id=1, source_target_pairs={{0,176},{1,144},{2,240},{3,112},{4,16},{5,192},{6,80},{7,32},{8,22... | collective-permute-start | bytes 393224 | tf_op jit(solution)/shard_map/ppermute | solution.py:238
  59.6 17.2 %collective-permute-start.15 = (f32[8,64,128]{2,1,0:T(8,128)S(1)}, f32[8,64,128]{2,1,0:T(8,128)S(1)}, u32[]{:S(2)}, u32[]{:S(2)}) collective-permute-start(f32[8,64,128]{2,1,0:T(8,128)S(1)} %pad_maximum_fusion.6), channel_id=1, source_target_pairs={{0,1},{1,0},{2,3},{3,2},{4,5},{5,4},{6,7},{7,6},{8,9},{9,8},{10,11... | collective-permute-start | bytes 786440 | tf_op jit(solution)/shard_map/ppermute | solution.py:174
  65.6 10.0 %collective-permute-start.19 = (f32[4,64,128]{2,1,0:T(8,128)S(1)}, f32[4,64,128]{2,1,0:T(8,128)S(1)}, u32[]{:S(2)}, u32[]{:S(2)}) collective-permute-start(f32[4,64,128]{2,1,0:T(8,128)S(1)} %collective-permute-done.16), channel_id=1, source_target_pairs={{0,48},{16,32},{32,16},{48,0},{64,112},{80,96},{96,80},{112,64},{1... | collective-permute-start | bytes 393224 | tf_op jit(solution)/shard_map/ppermute | solution.py:178
  65.9 9.8 %collective-permute-start.18 = (f32[4,64,128]{2,1,0:T(8,128)S(1)}, f32[4,64,128]{2,1,0:T(8,128)S(1)}, u32[]{:S(2)}, u32[]{:S(2)}) collective-permute-start(f32[4,64,128]{2,1,0:T(8,128)S(1)} %collective-permute-done.16), channel_id=1, source_target_pairs={{0,32},{16,48},{32,0},{48,16},{64,96},{80,112},{96,64},{112,80},{1... | collective-permute-start | bytes 393224 | tf_op jit(solution)/shard_map/ppermute | solution.py:178
  67.2 9.5 %collective-permute-start.17 = (f32[4,64,128]{2,1,0:T(8,128)S(1)}, f32[4,64,128]{2,1,0:T(8,128)S(1)}, u32[]{:S(2)}, u32[]{:S(2)}) collective-permute-start(f32[4,64,128]{2,1,0:T(8,128)S(1)} %collective-permute-done.16), channel_id=1, source_target_pairs={{0,16},{16,0},{32,48},{48,32},{64,80},{80,64},{96,112},{112,96},{1... | collective-permute-start | bytes 393224 | tf_op jit(solution)/shard_map/ppermute | solution.py:178
  88.3 7.5 %collective-permute-start.24 = (f32[4,64,128]{2,1,0:T(8,128)S(1)}, f32[4,64,128]{2,1,0:T(8,128)S(1)}, u32[]{:S(2)}, u32[]{:S(2)}) collective-permute-start(f32[4,64,128]{2,1,0:T(8,128)S(1)} %slice_add_fusion.4), channel_id=1, source_target_pairs={{0,6},{1,7},{2,4},{3,5},{4,2},{5,3},{6,0},{7,1},{8,14},{9,15},{10,... | collective-permute-start | bytes 393224 | tf_op jit(solution)/shard_map/ppermute | solution.py:174
  88.4 7.7 %collective-permute-start.23 = (f32[4,64,128]{2,1,0:T(8,128)S(1)}, f32[4,64,128]{2,1,0:T(8,128)S(1)}, u32[]{:S(2)}, u32[]{:S(2)}) collective-permute-start(f32[4,64,128]{2,1,0:T(8,128)S(1)} %slice_add_fusion.4), channel_id=1, source_target_pairs={{0,4},{1,5},{2,6},{3,7},{4,0},{5,1},{6,2},{7,3},{8,12},{9,13},{10,... | collective-permute-start | bytes 393224 | tf_op jit(solution)/shard_map/ppermute | solution.py:174
  98.4 12.3 %collective-permute-start.27 = (f32[4,64,128]{2,1,0:T(8,128)S(1)}, f32[4,64,128]{2,1,0:T(8,128)S(1)}, u32[]{:S(2)}, u32[]{:S(2)}) collective-permute-start(f32[4,64,128]{2,1,0:T(8,128)S(1)} %add_add_fusion.1), channel_id=1, source_target_pairs={{0,176},{1,144},{2,240},{3,112},{4,16},{5,192},{6,80},{7,32},{8,22... | collective-permute-start | bytes 393224 | tf_op jit(solution)/shard_map/ppermute | solution.py:238
  102.9 16.4 %collective-permute-start.26 = (f32[8,64,128]{2,1,0:T(8,128)S(1)}, f32[8,64,128]{2,1,0:T(8,128)S(1)}, u32[]{:S(2)}, u32[]{:S(2)}) collective-permute-start(f32[8,64,128]{2,1,0:T(8,128)S(1)} %pad_maximum_fusion.7), channel_id=1, source_target_pairs={{0,1},{1,0},{2,3},{3,2},{4,5},{5,4},{6,7},{7,6},{8,9},{9,8},{10,11... | collective-permute-start | bytes 786440 | tf_op jit(solution)/shard_map/ppermute | solution.py:174
  110.8 7.6 %collective-permute-start.30 = (f32[4,64,128]{2,1,0:T(8,128)S(1)}, f32[4,64,128]{2,1,0:T(8,128)S(1)}, u32[]{:S(2)}, u32[]{:S(2)}) collective-permute-start(f32[4,64,128]{2,1,0:T(8,128)S(1)} %collective-permute-done.27), channel_id=1, source_target_pairs={{0,48},{16,32},{32,16},{48,0},{64,112},{80,96},{96,80},{112,64},{1... | collective-permute-start | bytes 393224 | tf_op jit(solution)/shard_map/ppermute | solution.py:178
  110.8 7.6 %collective-permute-start.29 = (f32[4,64,128]{2,1,0:T(8,128)S(1)}, f32[4,64,128]{2,1,0:T(8,128)S(1)}, u32[]{:S(2)}, u32[]{:S(2)}) collective-permute-start(f32[4,64,128]{2,1,0:T(8,128)S(1)} %collective-permute-done.27), channel_id=1, source_target_pairs={{0,32},{16,48},{32,0},{48,16},{64,96},{80,112},{96,64},{112,80},{1... | collective-permute-start | bytes 393224 | tf_op jit(solution)/shard_map/ppermute | solution.py:178
  130.8 7.5 %collective-permute-start.35 = (f32[4,64,128]{2,1,0:T(8,128)S(1)}, f32[4,64,128]{2,1,0:T(8,128)S(1)}, u32[]{:S(2)}, u32[]{:S(2)}) collective-permute-start(f32[4,64,128]{2,1,0:T(8,128)S(1)} %slice_add_fusion.3), channel_id=1, source_target_pairs={{0,6},{1,7},{2,4},{3,5},{4,2},{5,3},{6,0},{7,1},{8,14},{9,15},{10,... | collective-permute-start | bytes 393224 | tf_op jit(solution)/shard_map/ppermute | solution.py:174
  130.9 7.9 %collective-permute-start.34 = (f32[4,64,128]{2,1,0:T(8,128)S(1)}, f32[4,64,128]{2,1,0:T(8,128)S(1)}, u32[]{:S(2)}, u32[]{:S(2)}) collective-permute-start(f32[4,64,128]{2,1,0:T(8,128)S(1)} %slice_add_fusion.3), channel_id=1, source_target_pairs={{0,4},{1,5},{2,6},{3,7},{4,0},{5,1},{6,2},{7,3},{8,12},{9,13},{10,... | collective-permute-start | bytes 393224 | tf_op jit(solution)/shard_map/ppermute | solution.py:174
  140.9 12.6 %collective-permute-start.38 = (f32[4,64,128]{2,1,0:T(8,128)S(1)}, f32[4,64,128]{2,1,0:T(8,128)S(1)}, u32[]{:S(2)}, u32[]{:S(2)}) collective-permute-start(f32[4,64,128]{2,1,0:T(8,128)S(1)} %add_add_fusion), channel_id=1, source_target_pairs={{0,176},{1,144},{2,240},{3,112},{4,16},{5,192},{6,80},{7,32},{8,22... | collective-permute-start | bytes 393224 | tf_op jit(solution)/shard_map/ppermute | solution.py:238
  146.0 15.9 %collective-permute-start.37 = (f32[8,64,128]{2,1,0:T(8,128)S(1)}, f32[8,64,128]{2,1,0:T(8,128)S(1)}, u32[]{:S(2)}, u32[]{:S(2)}) collective-permute-start(f32[8,64,128]{2,1,0:T(8,128)S(1)} %pad_maximum_fusion.8), channel_id=1, source_target_pairs={{0,1},{1,0},{2,3},{3,2},{4,5},{5,4},{6,7},{7,6},{8,9},{9,8},{10,11... | collective-permute-start | bytes 786440 | tf_op jit(solution)/shard_map/ppermute | solution.py:174
  153.5 7.6 %collective-permute-start.41 = (f32[4,64,128]{2,1,0:T(8,128)S(1)}, f32[4,64,128]{2,1,0:T(8,128)S(1)}, u32[]{:S(2)}, u32[]{:S(2)}) collective-permute-start(f32[4,64,128]{2,1,0:T(8,128)S(1)} %collective-permute-done.38), channel_id=1, source_target_pairs={{0,48},{16,32},{32,16},{48,0},{64,112},{80,96},{96,80},{112,64},{1... | collective-permute-start | bytes 393224 | tf_op jit(solution)/shard_map/ppermute | solution.py:178
  153.5 7.6 %collective-permute-start.40 = (f32[4,64,128]{2,1,0:T(8,128)S(1)}, f32[4,64,128]{2,1,0:T(8,128)S(1)}, u32[]{:S(2)}, u32[]{:S(2)}) collective-permute-start(f32[4,64,128]{2,1,0:T(8,128)S(1)} %collective-permute-done.38), channel_id=1, source_target_pairs={{0,32},{16,48},{32,0},{48,16},{64,96},{80,112},{96,64},{112,80},{1... | collective-permute-start | bytes 393224 | tf_op jit(solution)/shard_map/ppermute | solution.py:178
  155.0 7.0 %collective-permute-start.39 = (f32[4,64,128]{2,1,0:T(8,128)S(1)}, f32[4,64,128]{2,1,0:T(8,128)S(1)}, u32[]{:S(2)}, u32[]{:S(2)}) collective-permute-start(f32[4,64,128]{2,1,0:T(8,128)S(1)} %collective-permute-done.38), channel_id=1, source_target_pairs={{0,16},{16,0},{32,48},{48,32},{64,80},{80,64},{96,112},{112,96},{1... | collective-permute-start | bytes 393224 | tf_op jit(solution)/shard_map/ppermute | solution.py:178
  (19 other events, 104.4 us)

commit v4 on v3

--- a/solution.py
+++ b/solution.py
@@ -76,13 +76,7 @@
         place, omega, xc, xr, yr, yc, out, sums, ah, al, bh, bl, xx = refs
         load_panels(True, True, frame_count, place, xc, xr, yr, yc, ah, al, bh, bl, xx)
     else:
-        place, whole, xc, omega, sums, xx, arrived = refs
-        step_rows = whole.shape[0] // FETCHES
-        fetches = []
-        for n in range(FETCHES):
-            part = pl.ds(n * step_rows, step_rows)
-            fetches.append(pltpu.make_async_copy(whole.at[part, :], omega.at[part, :], arrived.at[n]))
-            fetches[-1].start()
+        place, omega, xc, sums, xx = refs
         load_panels(False, True, frame_count, place, xc, None, None, None, None, None, None, None, xx)
     rows = omega.shape[0]
     col = place[1]
@@ -90,9 +84,6 @@
     for t in range(rows // TILE):
         mine = slice(t * TILE, t * TILE + TILE)
         both = rest = None
-        if not update:
-            for n in range(t * TILE // step_rows, (t + 1) * TILE // step_rows):
-                fetches[n].wait()
         for j in range(rows // TILE):
             span = slice(j * TILE, j * TILE + TILE)
             value = omega[mine, span]
@@ -118,17 +109,41 @@
     frame_count = xc.shape[-1]
     wide = pltpu.VMEM((rows, 2 * frame_count), jnp.bfloat16)
     vmem = pl.BlockSpec(memory_space=pltpu.VMEM)
-    shapes = [pltpu.VMEM(omega.shape, jnp.float32), jax.ShapeDtypeStruct((SIDE, PIECE, frame_count), jnp.float32)]
-    home = pltpu.VMEM if update else pltpu.HBM
+    shapes = [jax.ShapeDtypeStruct((SIDE, PIECE, frame_count), jnp.float32)]
+    if update:
+        shapes = [pltpu.VMEM(omega.shape, jnp.float32)] + shapes
     return pl.pallas_call(
         functools.partial(sweep_kernel, update, frame_count),
         out_shape=shapes,
-        in_specs=[pl.BlockSpec(memory_space=pltpu.SMEM), pl.BlockSpec(memory_space=home)] + [vmem] * (1 + len(panels)),
-        out_specs=[vmem] * 2,
-        scratch_shapes=[wide] * 5 if update else [wide, pltpu.SemaphoreType.DMA((FETCHES,))],
+        in_specs=[pl.BlockSpec(memory_space=pltpu.SMEM)] + [vmem] * (2 + len(panels)),
+        out_specs=[vmem] * len(shapes),
+        scratch_shapes=[wide] * (5 if update else 1),
         compiler_params=pltpu.CompilerParams(vmem_limit_bytes=28 * 1024 * 1024),
         cost_estimate=pl.CostEstimate(flops=4 * rows * rows * frame_count * 3, bytes_accessed=8 * rows * rows, transcendentals=0),
-    )(place, pltpu.with_memory_space_constraint(omega, home), xc, *panels)
+    )(place, pltpu.with_memory_space_constraint(omega, pltpu.VMEM), xc, *panels)
+
+
+def stage_kernel(whole, held, arrived):
+    step_rows = whole.shape[0] // FETCHES
+    copies = []
+    for n in range(FETCHES):
+        part = pl.ds(n * step_rows, step_rows)
+        copies.append(pltpu.make_async_copy(whole.at[part, :], held.at[part, :], arrived.at[n]))
+        copies[-1].start()
+    for copy in copies:
+        copy.wait()
+
+
+def staged(omega):
+    return pl.pallas_call(
+        stage_kernel,
+        out_shape=pltpu.VMEM(omega.shape, jnp.float32),
+        in_specs=[pl.BlockSpec(memory_space=pltpu.HBM)],
+        out_specs=pl.BlockSpec(memory_space=pltpu.VMEM),
+        scratch_shapes=[pltpu.SemaphoreType.DMA((FETCHES,))],
+        compiler_params=pltpu.CompilerParams(vmem_limit_bytes=4 * 1024 * 1024),
+        cost_estimate=pl.CostEstimate(flops=0, bytes_accessed=8 * omega.size, transcendentals=0),
+    )(pltpu.with_memory_space_constraint(omega, pltpu.HBM))
 
 
 def final_kernel(frame_count, place, omega, xc, xr, yr, yc, out, grad, ah, al, bh, bl, values, grads, sent):
@@ -179,22 +194,22 @@
 
 
 ROWS = (
-    "b9f71c52ea83046d",
-    "a864d20fcb1e5397",
-    "5ca9e4128bf07d36",
-    "6fd8b3071a9ce542",
-    "70259fcb68ade134",
-    "4187ea2d950cf36b",
-    "e075398f42abd61c",
-    "b1264acd5f8739e0",
-    "d23f58b4610a9ce7",
-    "7ea018d6235fcb94",
-    "a4c0296ed7135fb8",
-    "35d18f7bac2460e9",
-    "9fe4601bcd2875a3",
-    "ca5d3782efb14609",
-    "17e8ad43f92c60b5",
-    "60fb9c25e83d71a4",
+    "8bf5137eda064c92",
+    "a9c6104efb7d2583",
+    "7ca9f6134ed8b025",
+    "db854e20f69c1a73",
+    "46b1fa3c85d02e79",
+    "7582de094ab13fc6",
+    "a07539ed4fb628c1",
+    "b16428cfe5a3790d",
+    "2f68b5c031e49a7d",
+    "e3ad4917205f8bc6",
+    "38f04e97c5216dab",
+    "28d15fa67e0493cb",
+    "c9ad3650fe2b4781",
+    "8ef4721bdc90563a",
+    "7cdb821409efa356",
+    "e9af365072bcd814",
 )
 
 
@@ -233,10 +248,13 @@
     return jnp.concatenate([value] + [swap_cols(value, 2 * m) for m in (1, 2, 3)], 0)
 
 
-def turn(four):
+def turn(four, beside=None):
     pairs = [(r * SIDE + c, LANDING[r, c][0] * SIDE + LANDING[r, c][1]) for r in range(SIDE) for c in range(SIDE)]
     turned = lax.ppermute(four, ("rows", "cols"), pairs)
-    return jnp.concatenate([turned] + [swap_rows(turned, m) for m in (1, 2, 3)], 0)
+    if beside is not None:
+        turned, beside = lax.optimization_barrier((turned, beside))
+    panel = jnp.concatenate([turned] + [swap_rows(turned, m) for m in (1, 2, 3)], 0)
+    return panel if beside is None else (panel, beside)
 
 
 def along(four):
@@ -249,9 +267,10 @@
     table = lax.dynamic_slice(jnp.asarray(slots()), (row, col, 0), (1, 1, 4 * SIDE)).reshape(-1)
     place = jnp.concatenate([jnp.stack([row, col]).astype(jnp.int32), table])
     own = gather_near(frames.T)
-    xc = turn(own)
+    own, begun = lax.optimization_barrier((own, precision))
+    xc, current = turn(own, staged(begun))
     xr = along(own)
-    current, sums = sweep(place, precision, xc, ())
+    (sums,) = sweep(place, current, xc, ())
     for index in range(ITERS):
         four = sum_near(sums)
         yc = turn(four)

time: 168 us -> 166 us (0.988)
  starting transfers between devices: 63.6 us -> 44.3 us
  waiting for transfers between devices: 83.5 us -> 101 us
    ppermute x4, starting transfers between devices: 23.5 us -> 6.26 us  [turn(): turned = lax.ppermute(four, ('rows', 'cols'), pairs)]
    ppermute x26, waiting for transfers between devices: 38.2 us -> 47.7 us  [swap_cols(): return lax.ppermute(value, 'cols', [(i, i ^ mask) for i in range(SIDE)])]
    ppermute x4, waiting for transfers between devices: 23 us -> 28.9 us  [turn(): turned = lax.ppermute(four, ('rows', 'cols'), pairs)]
    pallas_call x0 -> x1, Pallas kernels: none -> 2.21 us  [staged(): pl.pallas_call(stage_kernel, out_shape=pltpu.VMEM(omega.shape, jnp.float3...]
    ppermute x12, waiting for transfers between devices: 22.3 us -> 24.1 us  [swap_rows(): return lax.ppermute(value, 'rows', [(i, i ^ mask) for i in range(SIDE)])]
  transfers between devices with their start and end apart: 42 -> 42, of which waited for: 28 -> 32; matrix products, arithmetic and copies ran while one was open for 1% -> 1% of each run, Pallas kernels for 0% -> 1%
where the time goes in v4:
time: 166 us; the launch traced here: 165 us
  waiting for transfers between devices  101 us (61%)
  starting transfers between devices  44.3 us (27%)
  Pallas kernels  17.1 us (10%)
    ppermute x26, waiting for transfers between devices, swap_cols(): return lax.ppermute(value, 'cols', [(i, i ^ mask) for i in range(SIDE)])  47.7 us
    ppermute x4, waiting for transfers between devices, turn(): turned = lax.ppermute(four, ('rows', 'cols'), pairs)  28.9 us
    ppermute x12, waiting for transfers between devices, swap_rows(): return lax.ppermute(value, 'rows', [(i, i ^ mask) for i in range(SIDE)])  24.1 us
    ppermute x26, starting transfers between devices, swap_cols(): return lax.ppermute(value, 'cols', [(i, i ^ mask) for i in range(SIDE)])  21.6 us
    ppermute x12, starting transfers between devices, swap_rows(): return lax.ppermute(value, 'rows', [(i, i ^ mask) for i in range(SIDE)])  16.4 us
    pallas_call x3, Pallas kernels, sweep(): pl.pallas_call(functools.partial(sweep_kernel, update, frame_count), out_...  10.1 us
    ppermute x4, starting transfers between devices, turn(): turned = lax.ppermute(four, ('rows', 'cols'), pairs)  6.26 us
    pallas_call x1, Pallas kernels, final_sweep(): pl.pallas_call(functools.partial(final_kernel, frame_count), out_shape=[p...  4.81 us
  transfers between devices with their start and end apart: 42, of which 32 were waited for; matrix products, arithmetic and copies ran while one was open for 1% of the time, Pallas kernels for 1%

profile of v4, /device:TPU:40, one launch (start us, length us, event | category | flops | bytes accessed | tf_op | source)
XLA Modules:
  0.0 165.4 jit_solution(10029854738240210289)
XLA Ops:
  4.8 3.1 %collective-permute-done.1 = f32[1,64,128]{2,1,0:T(8,128)S(1)} collective-permute-done((f32[1,64,128]{2,1,0:T(8,128)}, f32[1,64,128]{2,1,0:T(8,128)S(1)}, u32[]{:S(2)}, u32[]{:S(2)}) %collective-permute-start.1) | collective-permute-done | bytes 32800 | tf_op jit(solution)/shard_map/ppermute | solution.py:189
  13.1 8.4 %collective-permute-done.3 = f32[4,64,128]{2,1,0:T(8,128)S(1)} collective-permute-done((f32[4,64,128]{2,1,0:T(8,128)S(1)}, f32[4,64,128]{2,1,0:T(8,128)S(1)}, u32[]{:S(2)}, u32[]{:S(2)}) %collective-permute-start.3) | collective-permute-done | bytes 131104 | tf_op jit(solution)/shard_map/ppermute | solution.py:253
  26.5 4.7 %collective-permute-done.5 = f32[4,64,128]{2,1,0:T(8,128)S(1)} collective-permute-done((f32[4,64,128]{2,1,0:T(8,128)S(1)}, f32[4,64,128]{2,1,0:T(8,128)S(1)}, u32[]{:S(2)}, u32[]{:S(2)}) %collective-permute-start.5) | collective-permute-done | bytes 131104 | tf_op jit(solution)/shard_map/ppermute | solution.py:193
  35.7 5.5 %collective-permute-done.10 = f32[4,64,128]{2,1,0:T(8,128)S(1)} collective-permute-done((f32[4,64,128]{2,1,0:T(8,128)S(1)}, f32[4,64,128]{2,1,0:T(8,128)S(1)}, u32[]{:S(2)}, u32[]{:S(2)}) %collective-permute-start.10) | collective-permute-done | bytes 131104 | tf_op jit(solution)/shard_map/ppermute | solution.py:189
  41.3 3.3 %collective-permute-start.12 = (f32[4,64,128]{2,1,0:T(8,128)S(1)}, f32[4,64,128]{2,1,0:T(8,128)S(1)}, u32[]{:S(2)}, u32[]{:S(2)}) collective-permute-start(f32[4,64,128]{2,1,0:T(8,128)S(1)} %slice_add_fusion.5), channel_id=1, source_target_pairs={{0,4},{1,5},{2,6},{3,7},{4,0},{5,1},{6,2},{7,3},{8,12},{9,13},{10,... | collective-permute-start | bytes 393224 | tf_op jit(solution)/shard_map/ppermute | solution.py:189
  45.7 3.0 %collective-permute-done.13 = f32[4,64,128]{2,1,0:T(8,128)S(1)} collective-permute-done((f32[4,64,128]{2,1,0:T(8,128)S(1)}, f32[4,64,128]{2,1,0:T(8,128)S(1)}, u32[]{:S(2)}, u32[]{:S(2)}) %collective-permute-start.13) | collective-permute-done | bytes 131104 | tf_op jit(solution)/shard_map/ppermute | solution.py:189
  57.2 6.7 %collective-permute-done.16 = f32[4,64,128]{2,1,0:T(8,128)S(1)} collective-permute-done((f32[4,64,128]{2,1,0:T(8,128)S(1)}, f32[4,64,128]{2,1,0:T(8,128)S(1)}, u32[]{:S(2)}, u32[]{:S(2)}) %collective-permute-start.16) | collective-permute-done | bytes 131104 | tf_op jit(solution)/shard_map/ppermute | solution.py:253
  64.6 3.4 %collective-permute-start.17 = (f32[4,64,128]{2,1,0:T(8,128)S(1)}, f32[4,64,128]{2,1,0:T(8,128)S(1)}, u32[]{:S(2)}, u32[]{:S(2)}) collective-permute-start(f32[4,64,128]{2,1,0:T(8,128)S(1)} %collective-permute-done.16), channel_id=1, source_target_pairs={{0,16},{16,0},{32,48},{48,32},{64,80},{80,64},{96,112},{112,96},{1... | collective-permute-start | bytes 393224 | tf_op jit(solution)/shard_map/ppermute | solution.py:193
  68.0 5.2 %collective-permute-done.19 = f32[4,64,128]{2,1,0:T(8,128)S(1)} collective-permute-done((f32[4,64,128]{2,1,0:T(8,128)S(1)}, f32[4,64,128]{2,1,0:T(8,128)S(1)}, u32[]{:S(2)}, u32[]{:S(2)}) %collective-permute-start.19) | collective-permute-done | bytes 131104 | tf_op jit(solution)/shard_map/ppermute | solution.py:193
  73.9 4.1 %shard_map.52 = (f32[1024,1024]{1,0:T(8,128)S(1)}, f32[16,64,128]{2,1,0:T(8,128)S(1)}) custom-call(s32[66]{0:T(128)S(1)} %pad_add_fusion.refs_0_.place, f32[1024,1024]{1,0:T(8,128)S(1)} %shard_map.50.refs_1_, f32[16,64,128]{2,1,0:T(8,128)S(1)} %constant_dynamic-update-slice_fusion.refs_2_.xc, ...), custom_call_target="tpu_custom_call" | custom-call | flops 1610612736 | bytes 8388608 | tf_op jit(solution)/shard_map/pallas_call | solution.py:115
  79.8 5.5 %collective-permute-done.21 = f32[4,64,128]{2,1,0:T(8,128)S(1)} collective-permute-done((f32[4,64,128]{2,1,0:T(8,128)S(1)}, f32[4,64,128]{2,1,0:T(8,128)S(1)}, u32[]{:S(2)}, u32[]{:S(2)}) %collective-permute-start.21) | collective-permute-done | bytes 131104 | tf_op jit(solution)/shard_map/ppermute | solution.py:189
  89.6 3.3 %collective-permute-done.24 = f32[4,64,128]{2,1,0:T(8,128)S(1)} collective-permute-done((f32[4,64,128]{2,1,0:T(8,128)S(1)}, f32[4,64,128]{2,1,0:T(8,128)S(1)}, u32[]{:S(2)}, u32[]{:S(2)}) %collective-permute-start.24) | collective-permute-done | bytes 131104 | tf_op jit(solution)/shard_map/ppermute | solution.py:189
  96.7 3.2 %collective-permute-done.25 = f32[4,64,128]{2,1,0:T(8,128)S(1)} collective-permute-done((f32[4,64,128]{2,1,0:T(8,128)S(1)}, f32[4,64,128]{2,1,0:T(8,128)S(1)}, u32[]{:S(2)}, u32[]{:S(2)}) %collective-permute-start.25) | collective-permute-done | bytes 131104 | tf_op jit(solution)/shard_map/ppermute | solution.py:189
  100.1 6.0 %collective-permute-done.27 = f32[4,64,128]{2,1,0:T(8,128)S(1)} collective-permute-done((f32[4,64,128]{2,1,0:T(8,128)S(1)}, f32[4,64,128]{2,1,0:T(8,128)S(1)}, u32[]{:S(2)}, u32[]{:S(2)}) %collective-permute-start.27) | collective-permute-done | bytes 131104 | tf_op jit(solution)/shard_map/ppermute | solution.py:253
  110.2 6.1 %collective-permute-done.30 = f32[4,64,128]{2,1,0:T(8,128)S(1)} collective-permute-done((f32[4,64,128]{2,1,0:T(8,128)S(1)}, f32[4,64,128]{2,1,0:T(8,128)S(1)}, u32[]{:S(2)}, u32[]{:S(2)}) %collective-permute-start.30) | collective-permute-done | bytes 131104 | tf_op jit(solution)/shard_map/ppermute | solution.py:193
  117.4 4.1 %shard_map.53 = (f32[1024,1024]{1,0:T(8,128)S(1)}, f32[16,64,128]{2,1,0:T(8,128)S(1)}) custom-call(s32[66]{0:T(128)S(1)} %pad_add_fusion.refs_0_.place, f32[1024,1024]{1,0:T(8,128)S(1)} %get-tuple-element.14.refs_1_, f32[16,64,128]{2,1,0:T(8,128)S(1)} %constant_dynamic-update-slice_fusion.refs_2_.xc, ...), custom_call_target="tpu_custom_call" | custom-call | flops 1610612736 | bytes 8388608 | tf_op jit(solution)/shard_map/pallas_call | solution.py:115
  123.3 5.5 %collective-permute-done.32 = f32[4,64,128]{2,1,0:T(8,128)S(1)} collective-permute-done((f32[4,64,128]{2,1,0:T(8,128)S(1)}, f32[4,64,128]{2,1,0:T(8,128)S(1)}, u32[]{:S(2)}, u32[]{:S(2)}) %collective-permute-start.32) | collective-permute-done | bytes 131104 | tf_op jit(solution)/shard_map/ppermute | solution.py:189
  128.9 2.5 %collective-permute-start.34 = (f32[4,64,128]{2,1,0:T(8,128)S(1)}, f32[4,64,128]{2,1,0:T(8,128)S(1)}, u32[]{:S(2)}, u32[]{:S(2)}) collective-permute-start(f32[4,64,128]{2,1,0:T(8,128)S(1)} %slice_add_fusion.3), channel_id=1, source_target_pairs={{0,4},{1,5},{2,6},{3,7},{4,0},{5,1},{6,2},{7,3},{8,12},{9,13},{10,... | collective-permute-start | bytes 393224 | tf_op jit(solution)/shard_map/ppermute | solution.py:189
  133.0 3.3 %collective-permute-done.35 = f32[4,64,128]{2,1,0:T(8,128)S(1)} collective-permute-done((f32[4,64,128]{2,1,0:T(8,128)S(1)}, f32[4,64,128]{2,1,0:T(8,128)S(1)}, u32[]{:S(2)}, u32[]{:S(2)}) %collective-permute-start.35) | collective-permute-done | bytes 131104 | tf_op jit(solution)/shard_map/ppermute | solution.py:189
  140.3 3.0 %collective-permute-done.36 = f32[4,64,128]{2,1,0:T(8,128)S(1)} collective-permute-done((f32[4,64,128]{2,1,0:T(8,128)S(1)}, f32[4,64,128]{2,1,0:T(8,128)S(1)}, u32[]{:S(2)}, u32[]{:S(2)}) %collective-permute-start.36) | collective-permute-done | bytes 131104 | tf_op jit(solution)/shard_map/ppermute | solution.py:189
  143.4 7.8 %collective-permute-done.38 = f32[4,64,128]{2,1,0:T(8,128)S(1)} collective-permute-done((f32[4,64,128]{2,1,0:T(8,128)S(1)}, f32[4,64,128]{2,1,0:T(8,128)S(1)}, u32[]{:S(2)}, u32[]{:S(2)}) %collective-permute-start.38) | collective-permute-done | bytes 131104 | tf_op jit(solution)/shard_map/ppermute | solution.py:253
  151.6 3.8 %collective-permute-start.39 = (f32[4,64,128]{2,1,0:T(8,128)S(1)}, f32[4,64,128]{2,1,0:T(8,128)S(1)}, u32[]{:S(2)}, u32[]{:S(2)}) collective-permute-start(f32[4,64,128]{2,1,0:T(8,128)S(1)} %collective-permute-done.38), channel_id=1, source_target_pairs={{0,16},{16,0},{32,48},{48,32},{64,80},{80,64},{96,112},{112,96},{1... | collective-permute-start | bytes 393224 | tf_op jit(solution)/shard_map/ppermute | solution.py:193
  155.4 4.4 %collective-permute-done.41 = f32[4,64,128]{2,1,0:T(8,128)S(1)} collective-permute-done((f32[4,64,128]{2,1,0:T(8,128)S(1)}, f32[4,64,128]{2,1,0:T(8,128)S(1)}, u32[]{:S(2)}, u32[]{:S(2)}) %collective-permute-start.41) | collective-permute-done | bytes 131104 | tf_op jit(solution)/shard_map/ppermute | solution.py:193
  160.4 4.8 %shard_map.54 = (f32[1024,1024]{1,0:T(8,128)}, f32[1024,1024]{1,0:T(8,128)}) custom-call(s32[66]{0:T(128)S(1)} %pad_add_fusion.refs_0_.place, f32[1024,1024]{1,0:T(8,128)S(1)} %get-tuple-element.16.omega, f32[16,64,128]{2,1,0:T(8,128)S(1)} %constant_dynamic-update-slice_fusion.refs_2_.xc, f32[16,64,128]{2,1,0:T(8,128)S(1)} %constant_dynamic-update-slice_fusion.4.refs_3_.xr, ...), custom_call_target="tpu_custom_call" | custom-call | flops 1610612736 | bytes 12582912 | tf_op jit(solution)/shard_map/pallas_call | solution.py:175
  (100 shorter events, 53.7 us)
Async XLA Ops:
  8.7 12.8 %collective-permute-start.3 = (f32[4,64,128]{2,1,0:T(8,128)S(1)}, f32[4,64,128]{2,1,0:T(8,128)S(1)}, u32[]{:S(2)}, u32[]{:S(2)}) collective-permute-start(f32[4,64,128]{2,1,0:T(8,128)S(1)} %pad_maximum_fusion.10), channel_id=1, source_target_pairs={{0,128},{1,176},{2,240},{3,80},{4,16},{5,48},{6,112},{7,224},{8,20... | collective-permute-start | bytes 393224 | tf_op jit(solution)/shard_map/ppermute | solution.py:253
  21.6 10.4 %collective-permute-start.6 = (f32[4,64,128]{2,1,0:T(8,128)S(1)}, f32[4,64,128]{2,1,0:T(8,128)S(1)}, u32[]{:S(2)}, u32[]{:S(2)}) collective-permute-start(f32[4,64,128]{2,1,0:T(8,128)S(1)} %collective-permute-done.3), channel_id=1, source_target_pairs={{0,48},{16,32},{32,16},{48,0},{64,112},{80,96},{96,80},{112,64},{1... | collective-permute-start | bytes 393224 | tf_op jit(solution)/shard_map/ppermute | solution.py:193
  23.4 7.7 %collective-permute-start.5 = (f32[4,64,128]{2,1,0:T(8,128)S(1)}, f32[4,64,128]{2,1,0:T(8,128)S(1)}, u32[]{:S(2)}, u32[]{:S(2)}) collective-permute-start(f32[4,64,128]{2,1,0:T(8,128)S(1)} %collective-permute-done.3), channel_id=1, source_target_pairs={{0,32},{16,48},{32,0},{48,16},{64,96},{80,112},{96,64},{112,80},{1... | collective-permute-start | bytes 393224 | tf_op jit(solution)/shard_map/ppermute | solution.py:193
  41.2 7.5 %collective-permute-start.13 = (f32[4,64,128]{2,1,0:T(8,128)S(1)}, f32[4,64,128]{2,1,0:T(8,128)S(1)}, u32[]{:S(2)}, u32[]{:S(2)}) collective-permute-start(f32[4,64,128]{2,1,0:T(8,128)S(1)} %slice_add_fusion.5), channel_id=1, source_target_pairs={{0,6},{1,7},{2,4},{3,5},{4,2},{5,3},{6,0},{7,1},{8,14},{9,15},{10,... | collective-permute-start | bytes 393224 | tf_op jit(solution)/shard_map/ppermute | solution.py:189
  41.3 7.7 %collective-permute-start.12 = (f32[4,64,128]{2,1,0:T(8,128)S(1)}, f32[4,64,128]{2,1,0:T(8,128)S(1)}, u32[]{:S(2)}, u32[]{:S(2)}) collective-permute-start(f32[4,64,128]{2,1,0:T(8,128)S(1)} %slice_add_fusion.5), channel_id=1, source_target_pairs={{0,4},{1,5},{2,6},{3,7},{4,0},{5,1},{6,2},{7,3},{8,12},{9,13},{10,... | collective-permute-start | bytes 393224 | tf_op jit(solution)/shard_map/ppermute | solution.py:189
  51.4 16.6 %collective-permute-start.8 = (f32[8,64,128]{2,1,0:T(8,128)S(1)}, f32[8,64,128]{2,1,0:T(8,128)S(1)}, u32[]{:S(2)}, u32[]{:S(2)}) collective-permute-start(f32[8,64,128]{2,1,0:T(8,128)S(1)} %pad_maximum_fusion.6), channel_id=1, source_target_pairs={{0,1},{1,0},{2,3},{3,2},{4,5},{5,4},{6,7},{7,6},{8,9},{9,8},{10,11... | collective-permute-start | bytes 786440 | tf_op jit(solution)/shard_map/ppermute | solution.py:189
  51.5 12.4 %collective-permute-start.16 = (f32[4,64,128]{2,1,0:T(8,128)S(1)}, f32[4,64,128]{2,1,0:T(8,128)S(1)}, u32[]{:S(2)}, u32[]{:S(2)}) collective-permute-start(f32[4,64,128]{2,1,0:T(8,128)S(1)} %add_add_fusion.2), channel_id=1, source_target_pairs={{0,128},{1,176},{2,240},{3,80},{4,16},{5,48},{6,112},{7,224},{8,20... | collective-permute-start | bytes 393224 | tf_op jit(solution)/shard_map/ppermute | solution.py:253
  55.7 18.1 %collective-permute-start.15 = (f32[8,64,128]{2,1,0:T(8,128)S(1)}, f32[8,64,128]{2,1,0:T(8,128)S(1)}, u32[]{:S(2)}, u32[]{:S(2)}) collective-permute-start(f32[8,64,128]{2,1,0:T(8,128)S(1)} %pad_maximum_fusion.7), channel_id=1, source_target_pairs={{0,1},{1,0},{2,3},{3,2},{4,5},{5,4},{6,7},{7,6},{8,9},{9,8},{10,11... | collective-permute-start | bytes 786440 | tf_op jit(solution)/shard_map/ppermute | solution.py:189
  63.9 9.3 %collective-permute-start.19 = (f32[4,64,128]{2,1,0:T(8,128)S(1)}, f32[4,64,128]{2,1,0:T(8,128)S(1)}, u32[]{:S(2)}, u32[]{:S(2)}) collective-permute-start(f32[4,64,128]{2,1,0:T(8,128)S(1)} %collective-permute-done.16), channel_id=1, source_target_pairs={{0,48},{16,32},{32,16},{48,0},{64,112},{80,96},{96,80},{112,64},{1... | collective-permute-start | bytes 393224 | tf_op jit(solution)/shard_map/ppermute | solution.py:193
  64.5 8.7 %collective-permute-start.18 = (f32[4,64,128]{2,1,0:T(8,128)S(1)}, f32[4,64,128]{2,1,0:T(8,128)S(1)}, u32[]{:S(2)}, u32[]{:S(2)}) collective-permute-start(f32[4,64,128]{2,1,0:T(8,128)S(1)} %collective-permute-done.16), channel_id=1, source_target_pairs={{0,32},{16,48},{32,0},{48,16},{64,96},{80,112},{96,64},{112,80},{1... | collective-permute-start | bytes 393224 | tf_op jit(solution)/shard_map/ppermute | solution.py:193
  64.6 9.2 %collective-permute-start.17 = (f32[4,64,128]{2,1,0:T(8,128)S(1)}, f32[4,64,128]{2,1,0:T(8,128)S(1)}, u32[]{:S(2)}, u32[]{:S(2)}) collective-permute-start(f32[4,64,128]{2,1,0:T(8,128)S(1)} %collective-permute-done.16), channel_id=1, source_target_pairs={{0,16},{16,0},{32,48},{48,32},{64,80},{80,64},{96,112},{112,96},{1... | collective-permute-start | bytes 393224 | tf_op jit(solution)/shard_map/ppermute | solution.py:193
  85.4 7.5 %collective-permute-start.24 = (f32[4,64,128]{2,1,0:T(8,128)S(1)}, f32[4,64,128]{2,1,0:T(8,128)S(1)}, u32[]{:S(2)}, u32[]{:S(2)}) collective-permute-start(f32[4,64,128]{2,1,0:T(8,128)S(1)} %slice_add_fusion.4), channel_id=1, source_target_pairs={{0,6},{1,7},{2,4},{3,5},{4,2},{5,3},{6,0},{7,1},{8,14},{9,15},{10,... | collective-permute-start | bytes 393224 | tf_op jit(solution)/shard_map/ppermute | solution.py:189
  85.5 7.7 %collective-permute-start.23 = (f32[4,64,128]{2,1,0:T(8,128)S(1)}, f32[4,64,128]{2,1,0:T(8,128)S(1)}, u32[]{:S(2)}, u32[]{:S(2)}) collective-permute-start(f32[4,64,128]{2,1,0:T(8,128)S(1)} %slice_add_fusion.4), channel_id=1, source_target_pairs={{0,4},{1,5},{2,6},{3,7},{4,0},{5,1},{6,2},{7,3},{8,12},{9,13},{10,... | collective-permute-start | bytes 393224 | tf_op jit(solution)/shard_map/ppermute | solution.py:189
  95.5 10.6 %collective-permute-start.27 = (f32[4,64,128]{2,1,0:T(8,128)S(1)}, f32[4,64,128]{2,1,0:T(8,128)S(1)}, u32[]{:S(2)}, u32[]{:S(2)}) collective-permute-start(f32[4,64,128]{2,1,0:T(8,128)S(1)} %add_add_fusion.1), channel_id=1, source_target_pairs={{0,128},{1,176},{2,240},{3,80},{4,16},{5,48},{6,112},{7,224},{8,20... | collective-permute-start | bytes 393224 | tf_op jit(solution)/shard_map/ppermute | solution.py:253
  99.9 17.4 %collective-permute-start.26 = (f32[8,64,128]{2,1,0:T(8,128)S(1)}, f32[8,64,128]{2,1,0:T(8,128)S(1)}, u32[]{:S(2)}, u32[]{:S(2)}) collective-permute-start(f32[8,64,128]{2,1,0:T(8,128)S(1)} %pad_maximum_fusion.8), channel_id=1, source_target_pairs={{0,1},{1,0},{2,3},{3,2},{4,5},{5,4},{6,7},{7,6},{8,9},{9,8},{10,11... | collective-permute-start | bytes 786440 | tf_op jit(solution)/shard_map/ppermute | solution.py:189
  106.1 10.2 %collective-permute-start.30 = (f32[4,64,128]{2,1,0:T(8,128)S(1)}, f32[4,64,128]{2,1,0:T(8,128)S(1)}, u32[]{:S(2)}, u32[]{:S(2)}) collective-permute-start(f32[4,64,128]{2,1,0:T(8,128)S(1)} %collective-permute-done.27), channel_id=1, source_target_pairs={{0,48},{16,32},{32,16},{48,0},{64,112},{80,96},{96,80},{112,64},{1... | collective-permute-start | bytes 393224 | tf_op jit(solution)/shard_map/ppermute | solution.py:193
  107.7 8.5 %collective-permute-start.29 = (f32[4,64,128]{2,1,0:T(8,128)S(1)}, f32[4,64,128]{2,1,0:T(8,128)S(1)}, u32[]{:S(2)}, u32[]{:S(2)}) collective-permute-start(f32[4,64,128]{2,1,0:T(8,128)S(1)} %collective-permute-done.27), channel_id=1, source_target_pairs={{0,32},{16,48},{32,0},{48,16},{64,96},{80,112},{96,64},{112,80},{1... | collective-permute-start | bytes 393224 | tf_op jit(solution)/shard_map/ppermute | solution.py:193
  108.0 9.3 %collective-permute-start.28 = (f32[4,64,128]{2,1,0:T(8,128)S(1)}, f32[4,64,128]{2,1,0:T(8,128)S(1)}, u32[]{:S(2)}, u32[]{:S(2)}) collective-permute-start(f32[4,64,128]{2,1,0:T(8,128)S(1)} %collective-permute-done.27), channel_id=1, source_target_pairs={{0,16},{16,0},{32,48},{48,32},{64,80},{80,64},{96,112},{112,96},{1... | collective-permute-start | bytes 393224 | tf_op jit(solution)/shard_map/ppermute | solution.py:193
  128.9 7.7 %collective-permute-start.34 = (f32[4,64,128]{2,1,0:T(8,128)S(1)}, f32[4,64,128]{2,1,0:T(8,128)S(1)}, u32[]{:S(2)}, u32[]{:S(2)}) collective-permute-start(f32[4,64,128]{2,1,0:T(8,128)S(1)} %slice_add_fusion.3), channel_id=1, source_target_pairs={{0,4},{1,5},{2,6},{3,7},{4,0},{5,1},{6,2},{7,3},{8,12},{9,13},{10,... | collective-permute-start | bytes 393224 | tf_op jit(solution)/shard_map/ppermute | solution.py:189
  138.9 12.3 %collective-permute-start.38 = (f32[4,64,128]{2,1,0:T(8,128)S(1)}, f32[4,64,128]{2,1,0:T(8,128)S(1)}, u32[]{:S(2)}, u32[]{:S(2)}) collective-permute-start(f32[4,64,128]{2,1,0:T(8,128)S(1)} %add_add_fusion), channel_id=1, source_target_pairs={{0,128},{1,176},{2,240},{3,80},{4,16},{5,48},{6,112},{7,224},{8,20... | collective-permute-start | bytes 393224 | tf_op jit(solution)/shard_map/ppermute | solution.py:253
  143.3 17.1 %collective-permute-start.37 = (f32[8,64,128]{2,1,0:T(8,128)S(1)}, f32[8,64,128]{2,1,0:T(8,128)S(1)}, u32[]{:S(2)}, u32[]{:S(2)}) collective-permute-start(f32[8,64,128]{2,1,0:T(8,128)S(1)} %pad_maximum_fusion.9), channel_id=1, source_target_pairs={{0,1},{1,0},{2,3},{3,2},{4,5},{5,4},{6,7},{7,6},{8,9},{9,8},{10,11... | collective-permute-start | bytes 786440 | tf_op jit(solution)/shard_map/ppermute | solution.py:189
  151.3 8.5 %collective-permute-start.41 = (f32[4,64,128]{2,1,0:T(8,128)S(1)}, f32[4,64,128]{2,1,0:T(8,128)S(1)}, u32[]{:S(2)}, u32[]{:S(2)}) collective-permute-start(f32[4,64,128]{2,1,0:T(8,128)S(1)} %collective-permute-done.38), channel_id=1, source_target_pairs={{0,48},{16,32},{32,16},{48,0},{64,112},{80,96},{96,80},{112,64},{1... | collective-permute-start | bytes 393224 | tf_op jit(solution)/shard_map/ppermute | solution.py:193
  151.3 8.5 %collective-permute-start.40 = (f32[4,64,128]{2,1,0:T(8,128)S(1)}, f32[4,64,128]{2,1,0:T(8,128)S(1)}, u32[]{:S(2)}, u32[]{:S(2)}) collective-permute-start(f32[4,64,128]{2,1,0:T(8,128)S(1)} %collective-permute-done.38), channel_id=1, source_target_pairs={{0,32},{16,48},{32,0},{48,16},{64,96},{80,112},{96,64},{112,80},{1... | collective-permute-start | bytes 393224 | tf_op jit(solution)/shard_map/ppermute | solution.py:193
  151.6 8.7 %collective-permute-start.39 = (f32[4,64,128]{2,1,0:T(8,128)S(1)}, f32[4,64,128]{2,1,0:T(8,128)S(1)}, u32[]{:S(2)}, u32[]{:S(2)}) collective-permute-start(f32[4,64,128]{2,1,0:T(8,128)S(1)} %collective-permute-done.38), channel_id=1, source_target_pairs={{0,16},{16,0},{32,48},{48,32},{64,80},{80,64},{96,112},{112,96},{1... | collective-permute-start | bytes 393224 | tf_op jit(solution)/shard_map/ppermute | solution.py:193
  (18 other events, 89.9 us)

commit v5 on v4

--- a/solution.py
+++ b/solution.py
@@ -31,24 +31,26 @@
 
 
 def load_panels(update, emit_sums, frame_count, place, xc, xr, yr, yc, ah, al, bh, bl, xx):
-    for q in range(SIDE):
-        span = pl.ds(q * PIECE, PIECE)
-        high, low = split(xc[place[2 + q]])
+    for slot in range(SIDE):
+        q = place[2 + slot]
+        span = pl.ds(pl.multiple_of(q * PIECE, PIECE), PIECE)
+        high, low = split(xc[slot // 4][slot % 4])
         if emit_sums:
             xx[span, :frame_count] = high
             xx[span, frame_count:] = low
         if update:
             bh[span, :frame_count] = high
             bl[span, :frame_count] = low
-            high, low = split(yc[place[34 + q]])
-            bh[span, frame_count:] = high
-            bl[span, frame_count:] = low
-            high, low = split(yr[place[50 + q]])
-            ah[span, :frame_count] = high
-            al[span, :frame_count] = low
-            high, low = split(xr[place[18 + q]])
-            ah[span, frame_count:] = high
-            al[span, frame_count:] = low
+            for panel, first, left, right, columns, width in (
+                (yc, 34, bh, bl, slice(frame_count, None), 4),
+                (yr, 50, ah, al, slice(None, frame_count), 8),
+                (xr, 18, ah, al, slice(frame_count, None), 8),
+            ):
+                q = place[first + slot]
+                span = pl.ds(pl.multiple_of(q * PIECE, PIECE), PIECE)
+                high, low = split(panel[slot // width][slot % width])
+                left[span, columns] = high
+                right[span, columns] = low
 
 
 def gradient_part(frame_count, a_high, a_low, b_high, b_low):
@@ -73,10 +75,11 @@
 
 def sweep_kernel(update, frame_count, *refs):
     if update:
-        place, omega, xc, xr, yr, yc, out, sums, ah, al, bh, bl, xx = refs
+        place, omega, *panels, out, sums, ah, al, bh, bl, xx = refs
+        xc, xr, yr, yc = panels[:4], panels[4:6], panels[6:8], panels[8:]
         load_panels(True, True, frame_count, place, xc, xr, yr, yc, ah, al, bh, bl, xx)
     else:
-        place, omega, xc, sums, xx = refs
+        place, omega, *xc, sums, xx = refs
         load_panels(False, True, frame_count, place, xc, None, None, None, None, None, None, None, xx)
     rows = omega.shape[0]
     col = place[1]
@@ -106,7 +109,7 @@
 def sweep(place, omega, xc, panels):
     update = bool(panels)
     rows = omega.shape[0]
-    frame_count = xc.shape[-1]
+    frame_count = xc[0].shape[-1]
     wide = pltpu.VMEM((rows, 2 * frame_count), jnp.bfloat16)
     vmem = pl.BlockSpec(memory_space=pltpu.VMEM)
     shapes = [jax.ShapeDtypeStruct((SIDE, PIECE, frame_count), jnp.float32)]
@@ -115,12 +118,12 @@
     return pl.pallas_call(
         functools.partial(sweep_kernel, update, frame_count),
         out_shape=shapes,
-        in_specs=[pl.BlockSpec(memory_space=pltpu.SMEM)] + [vmem] * (2 + len(panels)),
+        in_specs=[pl.BlockSpec(memory_space=pltpu.SMEM)] + [vmem] * (1 + len(xc) + len(panels)),
         out_specs=[vmem] * len(shapes),
         scratch_shapes=[wide] * (5 if update else 1),
         compiler_params=pltpu.CompilerParams(vmem_limit_bytes=28 * 1024 * 1024),
         cost_estimate=pl.CostEstimate(flops=4 * rows * rows * frame_count * 3, bytes_accessed=8 * rows * rows, transcendentals=0),
-    )(place, pltpu.with_memory_space_constraint(omega, pltpu.VMEM), xc, *panels)
+    )(place, pltpu.with_memory_space_constraint(omega, pltpu.VMEM), *xc, *panels)
 
 
 def stage_kernel(whole, held, arrived):
@@ -146,7 +149,9 @@
     )(pltpu.with_memory_space_constraint(omega, pltpu.HBM))
 
 
-def final_kernel(frame_count, place, omega, xc, xr, yr, yc, out, grad, ah, al, bh, bl, values, grads, sent):
+def final_kernel(frame_count, place, omega, *refs):
+    *panels, out, grad, ah, al, bh, bl, values, grads, sent = refs
+    xc, xr, yr, yc = panels[:4], panels[4:6], panels[6:8], panels[8:]
     load_panels(True, False, frame_count, place, xc, xr, yr, yc, ah, al, bh, bl, None)
     rows = omega.shape[0]
     here = place[0] == place[1]
@@ -169,20 +174,20 @@
 
 def final_sweep(place, omega, xc, panels):
     rows = omega.shape[0]
-    frame_count = xc.shape[-1]
+    frame_count = xc[0].shape[-1]
     wide = pltpu.VMEM((rows, 2 * frame_count), jnp.bfloat16)
     vmem = pl.BlockSpec(memory_space=pltpu.VMEM)
     return pl.pallas_call(
         functools.partial(final_kernel, frame_count),
         out_shape=[pltpu.HBM(omega.shape, jnp.float32)] * 2,
-        in_specs=[pl.BlockSpec(memory_space=pltpu.SMEM)] + [vmem] * (2 + len(panels)),
+        in_specs=[pl.BlockSpec(memory_space=pltpu.SMEM)] + [vmem] * (1 + len(xc) + len(panels)),
         out_specs=[pl.BlockSpec(memory_space=pltpu.HBM)] * 2,
         scratch_shapes=[wide] * 4
         + [pltpu.VMEM(omega.shape, jnp.float32)] * 2
         + [pltpu.SemaphoreType.DMA((2 * (rows // TILE) ** 2,))],
         compiler_params=pltpu.CompilerParams(vmem_limit_bytes=28 * 1024 * 1024),
         cost_estimate=pl.CostEstimate(flops=4 * rows * rows * frame_count * 3, bytes_accessed=12 * rows * rows, transcendentals=0),
-    )(place, pltpu.with_memory_space_constraint(omega, pltpu.VMEM), xc, *panels)
+    )(place, pltpu.with_memory_space_constraint(omega, pltpu.VMEM), *xc, *panels)
 
 
 def swap_cols(value, mask):
@@ -233,7 +238,7 @@
                 table[r, c, 1, q] = side + (y ^ ((c >> 1) & 3))
                 table[r, c, 2, q] = found[q][0]
                 table[r, c, 3, q] = side + y
-    return table.reshape(SIDE, SIDE, 4 * SIDE)
+    return np.argsort(table, -1).astype(np.int32).reshape(SIDE, SIDE, 4 * SIDE)
 
 
 def sum_near(sums):
@@ -253,13 +258,13 @@
     turned = lax.ppermute(four, ("rows", "cols"), pairs)
     if beside is not None:
         turned, beside = lax.optimization_barrier((turned, beside))
-    panel = jnp.concatenate([turned] + [swap_rows(turned, m) for m in (1, 2, 3)], 0)
+    panel = [turned] + [swap_rows(turned, m) for m in (1, 2, 3)]
     return panel if beside is None else (panel, beside)
 
 
 def along(four):
     value = jnp.concatenate([four, swap_cols(four, 8)], 0)
-    return jnp.concatenate([value, swap_cols(value, 1)], 0)
+    return [value, swap_cols(value, 1)]
 
 
 def on_device(frames, precision):
@@ -276,9 +281,9 @@
         yc = turn(four)
         yr = along(four)
         if index < ITERS - 1:
-            current, sums = sweep(place, current, xc, (xr, yr, yc))
+            current, sums = sweep(place, current, xc, (*xr, *yr, *yc))
         else:
-            current, gradient = final_sweep(place, current, xc, (xr, yr, yc))
+            current, gradient = final_sweep(place, current, xc, (*xr, *yr, *yc))
     return (current, gradient)
 
 

time: 166 us -> 167 us (level)
  waiting for transfers between devices: 101 us -> 97.7 us
  starting transfers between devices: 44.3 us -> 47.5 us
    ppermute x4, starting transfers between devices: 6.26 us -> 8.15 us  [turn(): turned = lax.ppermute(four, ('rows', 'cols'), pairs)]
  transfers between devices with their start and end apart: 42 -> 42, of which waited for: 32 -> 33; matrix products, arithmetic and copies ran while one was open for 1% -> 1% of each run, Pallas kernels for 1% -> 1%
where the time goes in v5:
time: 167 us; the launch traced here: 166 us
  waiting for transfers between devices  97.7 us (59%)
  starting transfers between devices  47.5 us (28%)
  Pallas kernels  17.6 us (11%)
    ppermute x26, waiting for transfers between devices, swap_cols(): return lax.ppermute(value, 'cols', [(i, i ^ mask) for i in range(SIDE)])  46.4 us
    ppermute x4, waiting for transfers between devices, turn(): turned = lax.ppermute(four, ('rows', 'cols'), pairs)  28.4 us
    ppermute x26, starting transfers between devices, swap_cols(): return lax.ppermute(value, 'cols', [(i, i ^ mask) for i in range(SIDE)])  23 us
    ppermute x12, waiting for transfers between devices, swap_rows(): return lax.ppermute(value, 'rows', [(i, i ^ mask) for i in range(SIDE)])  22.9 us
    ppermute x12, starting transfers between devices, swap_rows(): return lax.ppermute(value, 'rows', [(i, i ^ mask) for i in range(SIDE)])  16.4 us
    pallas_call x3, Pallas kernels, sweep(): pl.pallas_call(functools.partial(sweep_kernel, update, frame_count), out_...  10.4 us
    ppermute x4, starting transfers between devices, turn(): turned = lax.ppermute(four, ('rows', 'cols'), pairs)  8.15 us
    pallas_call x1, Pallas kernels, final_sweep(): pl.pallas_call(functools.partial(final_kernel, frame_count), out_shape=[p...  4.96 us
  transfers between devices with their start and end apart: 42, of which 33 were waited for; matrix products, arithmetic and copies ran while one was open for 1% of the time, Pallas kernels for 1%

profile of v5, /device:TPU:40, one launch (start us, length us, event | category | flops | bytes accessed | tf_op | source)
XLA Modules:
  0.0 165.9 jit_solution(1500181848405375279)
XLA Ops:
  4.8 3.1 %collective-permute-done.1 = f32[1,64,128]{2,1,0:T(8,128)S(1)} collective-permute-done((f32[1,64,128]{2,1,0:T(8,128)}, f32[1,64,128]{2,1,0:T(8,128)S(1)}, u32[]{:S(2)}, u32[]{:S(2)}) %collective-permute-start.1) | collective-permute-done | bytes 32800 | tf_op jit(solution)/shard_map/ppermute | solution.py:194
  12.4 9.1 %collective-permute-done.3.refs_2_.refs_0_ = f32[4,64,128]{2,1,0:T(8,128)S(1)} collective-permute-done((f32[4,64,128]{2,1,0:T(8,128)S(1)}, f32[4,64,128]{2,1,0:T(8,128)S(1)}, u32[]{:S(2)}, u32[]{:S(2)}) %collective-permute-start.3) | collective-permute-done | bytes 131104 | tf_op jit(solution)/shard_map/ppermute | solution.py:258
  26.4 3.8 %collective-permute-done.6.refs_5_.refs_3_ = f32[4,64,128]{2,1,0:T(8,128)S(1)} collective-permute-done((f32[4,64,128]{2,1,0:T(8,128)S(1)}, f32[4,64,128]{2,1,0:T(8,128)S(1)}, u32[]{:S(2)}, u32[]{:S(2)}) %collective-permute-start.6) | collective-permute-done | bytes 131104 | tf_op jit(solution)/shard_map/ppermute | solution.py:198
  35.1 5.5 %collective-permute-done.10 = f32[4,64,128]{2,1,0:T(8,128)S(1)} collective-permute-done((f32[4,64,128]{2,1,0:T(8,128)S(1)}, f32[4,64,128]{2,1,0:T(8,128)S(1)}, u32[]{:S(2)}, u32[]{:S(2)}) %collective-permute-start.10) | collective-permute-done | bytes 131104 | tf_op jit(solution)/shard_map/ppermute | solution.py:194
  40.7 3.6 %collective-permute-start.12 = (f32[4,64,128]{2,1,0:T(8,128)S(1)}, f32[4,64,128]{2,1,0:T(8,128)S(1)}, u32[]{:S(2)}, u32[]{:S(2)}) collective-permute-start(f32[4,64,128]{2,1,0:T(8,128)S(1)} %slice_add_fusion.5), channel_id=1, source_target_pairs={{0,4},{1,5},{2,6},{3,7},{4,0},{5,1},{6,2},{7,3},{8,12},{9,13},{10,... | collective-permute-start | bytes 393224 | tf_op jit(solution)/shard_map/ppermute | solution.py:194
  45.1 3.0 %collective-permute-done.13 = f32[4,64,128]{2,1,0:T(8,128)S(1)} collective-permute-done((f32[4,64,128]{2,1,0:T(8,128)S(1)}, f32[4,64,128]{2,1,0:T(8,128)S(1)}, u32[]{:S(2)}, u32[]{:S(2)}) %collective-permute-start.13) | collective-permute-done | bytes 131104 | tf_op jit(solution)/shard_map/ppermute | solution.py:194
  50.9 2.5 %collective-permute-start.16 = (f32[4,64,128]{2,1,0:T(8,128)S(1)}, f32[4,64,128]{2,1,0:T(8,128)S(1)}, u32[]{:S(2)}, u32[]{:S(2)}) collective-permute-start(f32[4,64,128]{2,1,0:T(8,128)S(1)} %add_add_fusion.2), channel_id=1, source_target_pairs={{0,128},{1,176},{2,240},{3,80},{4,16},{5,48},{6,112},{7,224},{8,20... | collective-permute-start | bytes 393224 | tf_op jit(solution)/shard_map/ppermute | solution.py:258
  56.5 5.3 %collective-permute-done.16.refs_10_ = f32[4,64,128]{2,1,0:T(8,128)S(1)} collective-permute-done((f32[4,64,128]{2,1,0:T(8,128)S(1)}, f32[4,64,128]{2,1,0:T(8,128)S(1)}, u32[]{:S(2)}, u32[]{:S(2)}) %collective-permute-start.16) | collective-permute-done | bytes 131104 | tf_op jit(solution)/shard_map/ppermute | solution.py:258
  65.9 5.4 %collective-permute-done.19.refs_13_ = f32[4,64,128]{2,1,0:T(8,128)S(1)} collective-permute-done((f32[4,64,128]{2,1,0:T(8,128)S(1)}, f32[4,64,128]{2,1,0:T(8,128)S(1)}, u32[]{:S(2)}, u32[]{:S(2)}) %collective-permute-start.19) | collective-permute-done | bytes 131104 | tf_op jit(solution)/shard_map/ppermute | solution.py:198
  72.8 4.3 %shard_map.52 = (f32[1024,1024]{1,0:T(8,128)S(1)}, f32[16,64,128]{2,1,0:T(8,128)S(1)}) custom-call(s32[66]{0:T(128)S(1)} %pad_add_fusion.refs_0_.place, f32[1024,1024]{1,0:T(8,128)S(1)} %shard_map.50.refs_1_, f32[4,64,128]{2,1,0:T(8,128)S(1)} %collective-permute-done.3.refs_2_.refs_0_, f32[4,64,128]{2,1,0:T(8,128)S(1)} %collective-permute-done.4.refs_3_.refs_1_, ...), custom_call_target="tpu_custom_call" | custom-call | flops 1610612736 | bytes 8388608 | tf_op jit(solution)/shard_map/pallas_call | solution.py:118
  78.9 5.5 %collective-permute-done.21 = f32[4,64,128]{2,1,0:T(8,128)S(1)} collective-permute-done((f32[4,64,128]{2,1,0:T(8,128)S(1)}, f32[4,64,128]{2,1,0:T(8,128)S(1)}, u32[]{:S(2)}, u32[]{:S(2)}) %collective-permute-start.21) | collective-permute-done | bytes 131104 | tf_op jit(solution)/shard_map/ppermute | solution.py:194
  84.5 4.4 %collective-permute-start.23 = (f32[4,64,128]{2,1,0:T(8,128)S(1)}, f32[4,64,128]{2,1,0:T(8,128)S(1)}, u32[]{:S(2)}, u32[]{:S(2)}) collective-permute-start(f32[4,64,128]{2,1,0:T(8,128)S(1)} %slice_add_fusion.4), channel_id=1, source_target_pairs={{0,4},{1,5},{2,6},{3,7},{4,0},{5,1},{6,2},{7,3},{8,12},{9,13},{10,... | collective-permute-start | bytes 393224 | tf_op jit(solution)/shard_map/ppermute | solution.py:194
  94.8 2.9 %collective-permute-start.27 = (f32[4,64,128]{2,1,0:T(8,128)S(1)}, f32[4,64,128]{2,1,0:T(8,128)S(1)}, u32[]{:S(2)}, u32[]{:S(2)}) collective-permute-start(f32[4,64,128]{2,1,0:T(8,128)S(1)} %add_add_fusion.1), channel_id=1, source_target_pairs={{0,128},{1,176},{2,240},{3,80},{4,16},{5,48},{6,112},{7,224},{8,20... | collective-permute-start | bytes 393224 | tf_op jit(solution)/shard_map/ppermute | solution.py:258
  100.8 6.8 %collective-permute-done.27.refs_10_ = f32[4,64,128]{2,1,0:T(8,128)S(1)} collective-permute-done((f32[4,64,128]{2,1,0:T(8,128)S(1)}, f32[4,64,128]{2,1,0:T(8,128)S(1)}, u32[]{:S(2)}, u32[]{:S(2)}) %collective-permute-start.27) | collective-permute-done | bytes 131104 | tf_op jit(solution)/shard_map/ppermute | solution.py:258
  108.5 3.1 %collective-permute-start.28 = (f32[4,64,128]{2,1,0:T(8,128)S(1)}, f32[4,64,128]{2,1,0:T(8,128)S(1)}, u32[]{:S(2)}, u32[]{:S(2)}) collective-permute-start(f32[4,64,128]{2,1,0:T(8,128)S(1)} %collective-permute-done.27.refs_10_), channel_id=1, source_target_pairs={{0,16},{16,0},{32,48},{48,32},{64,80},{80,64},{96,112},{112,96},{1... | collective-permute-start | bytes 393224 | tf_op jit(solution)/shard_map/ppermute | solution.py:198
  111.6 5.3 %collective-permute-done.30.refs_13_ = f32[4,64,128]{2,1,0:T(8,128)S(1)} collective-permute-done((f32[4,64,128]{2,1,0:T(8,128)S(1)}, f32[4,64,128]{2,1,0:T(8,128)S(1)}, u32[]{:S(2)}, u32[]{:S(2)}) %collective-permute-start.30) | collective-permute-done | bytes 131104 | tf_op jit(solution)/shard_map/ppermute | solution.py:198
  117.5 4.3 %shard_map.53 = (f32[1024,1024]{1,0:T(8,128)S(1)}, f32[16,64,128]{2,1,0:T(8,128)S(1)}) custom-call(s32[66]{0:T(128)S(1)} %pad_add_fusion.refs_0_.place, f32[1024,1024]{1,0:T(8,128)S(1)} %get-tuple-element.14.refs_1_, f32[4,64,128]{2,1,0:T(8,128)S(1)} %collective-permute-done.3.refs_2_.refs_0_, f32[4,64,128]{2,1,0:T(8,128)S(1)} %collective-permute-done.4.refs_3_.refs_1_, ...), custom_call_target="tpu_custom_call" | custom-call | flops 1610612736 | bytes 8388608 | tf_op jit(solution)/shard_map/pallas_call | solution.py:118
  123.6 5.5 %collective-permute-done.32 = f32[4,64,128]{2,1,0:T(8,128)S(1)} collective-permute-done((f32[4,64,128]{2,1,0:T(8,128)S(1)}, f32[4,64,128]{2,1,0:T(8,128)S(1)}, u32[]{:S(2)}, u32[]{:S(2)}) %collective-permute-start.32) | collective-permute-done | bytes 131104 | tf_op jit(solution)/shard_map/ppermute | solution.py:194
  133.3 3.3 %collective-permute-done.35 = f32[4,64,128]{2,1,0:T(8,128)S(1)} collective-permute-done((f32[4,64,128]{2,1,0:T(8,128)S(1)}, f32[4,64,128]{2,1,0:T(8,128)S(1)}, u32[]{:S(2)}, u32[]{:S(2)}) %collective-permute-start.35) | collective-permute-done | bytes 131104 | tf_op jit(solution)/shard_map/ppermute | solution.py:194
  140.4 3.2 %collective-permute-done.36 = f32[4,64,128]{2,1,0:T(8,128)S(1)} collective-permute-done((f32[4,64,128]{2,1,0:T(8,128)S(1)}, f32[4,64,128]{2,1,0:T(8,128)S(1)}, u32[]{:S(2)}, u32[]{:S(2)}) %collective-permute-start.36) | collective-permute-done | bytes 131104 | tf_op jit(solution)/shard_map/ppermute | solution.py:194
  144.2 7.3 %collective-permute-done.38.refs_8_ = f32[4,64,128]{2,1,0:T(8,128)S(1)} collective-permute-done((f32[4,64,128]{2,1,0:T(8,128)S(1)}, f32[4,64,128]{2,1,0:T(8,128)S(1)}, u32[]{:S(2)}, u32[]{:S(2)}) %collective-permute-start.38) | collective-permute-done | bytes 131104 | tf_op jit(solution)/shard_map/ppermute | solution.py:258
  151.7 3.8 %collective-permute-start.39 = (f32[4,64,128]{2,1,0:T(8,128)S(1)}, f32[4,64,128]{2,1,0:T(8,128)S(1)}, u32[]{:S(2)}, u32[]{:S(2)}) collective-permute-start(f32[4,64,128]{2,1,0:T(8,128)S(1)} %collective-permute-done.38.refs_8_), channel_id=1, source_target_pairs={{0,16},{16,0},{32,48},{48,32},{64,80},{80,64},{96,112},{112,96},{1... | collective-permute-start | bytes 393224 | tf_op jit(solution)/shard_map/ppermute | solution.py:198
  155.5 4.6 %collective-permute-done.41.refs_11_ = f32[4,64,128]{2,1,0:T(8,128)S(1)} collective-permute-done((f32[4,64,128]{2,1,0:T(8,128)S(1)}, f32[4,64,128]{2,1,0:T(8,128)S(1)}, u32[]{:S(2)}, u32[]{:S(2)}) %collective-permute-start.41) | collective-permute-done | bytes 131104 | tf_op jit(solution)/shard_map/ppermute | solution.py:198
  160.7 5.0 %shard_map.54 = (f32[1024,1024]{1,0:T(8,128)}, f32[1024,1024]{1,0:T(8,128)}) custom-call(s32[66]{0:T(128)S(1)} %pad_add_fusion.refs_0_.place, f32[1024,1024]{1,0:T(8,128)S(1)} %get-tuple-element.16.omega, f32[4,64,128]{2,1,0:T(8,128)S(1)} %collective-permute-done.3.refs_2_.refs_0_, f32[4,64,128]{2,1,0:T(8,128)S(1)} %collective-permute-done.4.refs_3_.refs_1_, ...), custom_call_target="tpu_custom_call" | custom-call | flops 1610612736 | bytes 12582912 | tf_op jit(solution)/shard_map/pallas_call | solution.py:180
  (88 shorter events, 54.5 us)
Async XLA Ops:
  8.7 12.8 %collective-permute-start.3 = (f32[4,64,128]{2,1,0:T(8,128)S(1)}, f32[4,64,128]{2,1,0:T(8,128)S(1)}, u32[]{:S(2)}, u32[]{:S(2)}) collective-permute-start(f32[4,64,128]{2,1,0:T(8,128)S(1)} %pad_maximum_fusion.3), channel_id=1, source_target_pairs={{0,128},{1,176},{2,240},{3,80},{4,16},{5,48},{6,112},{7,224},{8,20... | collective-permute-start | bytes 393224 | tf_op jit(solution)/shard_map/ppermute | solution.py:258
  21.5 8.7 %collective-permute-start.6 = (f32[4,64,128]{2,1,0:T(8,128)S(1)}, f32[4,64,128]{2,1,0:T(8,128)S(1)}, u32[]{:S(2)}, u32[]{:S(2)}) collective-permute-start(f32[4,64,128]{2,1,0:T(8,128)S(1)} %collective-permute-done.3.refs_2_.refs_0_), channel_id=1, source_target_pairs={{0,48},{16,32},{32,16},{48,0},{64,112},{80,96},{96,80},{112,64},{1... | collective-permute-start | bytes 393224 | tf_op jit(solution)/shard_map/ppermute | solution.py:198
  23.3 8.1 %collective-permute-start.4 = (f32[4,64,128]{2,1,0:T(8,128)S(1)}, f32[4,64,128]{2,1,0:T(8,128)S(1)}, u32[]{:S(2)}, u32[]{:S(2)}) collective-permute-start(f32[4,64,128]{2,1,0:T(8,128)S(1)} %collective-permute-done.3.refs_2_.refs_0_), channel_id=1, source_target_pairs={{0,16},{16,0},{32,48},{48,32},{64,80},{80,64},{96,112},{112,96},{1... | collective-permute-start | bytes 393224 | tf_op jit(solution)/shard_map/ppermute | solution.py:198
  40.6 7.5 %collective-permute-start.13 = (f32[4,64,128]{2,1,0:T(8,128)S(1)}, f32[4,64,128]{2,1,0:T(8,128)S(1)}, u32[]{:S(2)}, u32[]{:S(2)}) collective-permute-start(f32[4,64,128]{2,1,0:T(8,128)S(1)} %slice_add_fusion.5), channel_id=1, source_target_pairs={{0,6},{1,7},{2,4},{3,5},{4,2},{5,3},{6,0},{7,1},{8,14},{9,15},{10,... | collective-permute-start | bytes 393224 | tf_op jit(solution)/shard_map/ppermute | solution.py:194
  40.7 7.7 %collective-permute-start.12 = (f32[4,64,128]{2,1,0:T(8,128)S(1)}, f32[4,64,128]{2,1,0:T(8,128)S(1)}, u32[]{:S(2)}, u32[]{:S(2)}) collective-permute-start(f32[4,64,128]{2,1,0:T(8,128)S(1)} %slice_add_fusion.5), channel_id=1, source_target_pairs={{0,4},{1,5},{2,6},{3,7},{4,0},{5,1},{6,2},{7,3},{8,12},{9,13},{10,... | collective-permute-start | bytes 393224 | tf_op jit(solution)/shard_map/ppermute | solution.py:194
  50.8 15.1 %collective-permute-start.8 = (f32[8,64,128]{2,1,0:T(8,128)S(1)}, f32[8,64,128]{2,1,0:T(8,128)S(1)}, u32[]{:S(2)}, u32[]{:S(2)}) collective-permute-start(f32[8,64,128]{2,1,0:T(8,128)S(1)} %constant_dynamic-update-slice_fusion.refs_6_.refs_4_), channel_id=1, source_target_pairs={{0,1},{1,0},{2,3},{3,2},{4,5},{5,4},{6,7},{7,6},{8,9},{9,8},{10,11... | collective-permute-start | bytes 786440 | tf_op jit(solution)/shard_map/ppermute | solution.py:194
  50.9 10.9 %collective-permute-start.16 = (f32[4,64,128]{2,1,0:T(8,128)S(1)}, f32[4,64,128]{2,1,0:T(8,128)S(1)}, u32[]{:S(2)}, u32[]{:S(2)}) collective-permute-start(f32[4,64,128]{2,1,0:T(8,128)S(1)} %add_add_fusion.2), channel_id=1, source_target_pairs={{0,128},{1,176},{2,240},{3,80},{4,16},{5,48},{6,112},{7,224},{8,20... | collective-permute-start | bytes 393224 | tf_op jit(solution)/shard_map/ppermute | solution.py:258
  55.1 17.7 %collective-permute-start.15 = (f32[8,64,128]{2,1,0:T(8,128)S(1)}, f32[8,64,128]{2,1,0:T(8,128)S(1)}, u32[]{:S(2)}, u32[]{:S(2)}) collective-permute-start(f32[8,64,128]{2,1,0:T(8,128)S(1)} %pad_maximum_fusion.refs_8_), channel_id=1, source_target_pairs={{0,1},{1,0},{2,3},{3,2},{4,5},{5,4},{6,7},{7,6},{8,9},{9,8},{10,11... | collective-permute-start | bytes 786440 | tf_op jit(solution)/shard_map/ppermute | solution.py:194
  61.8 9.5 %collective-permute-start.19 = (f32[4,64,128]{2,1,0:T(8,128)S(1)}, f32[4,64,128]{2,1,0:T(8,128)S(1)}, u32[]{:S(2)}, u32[]{:S(2)}) collective-permute-start(f32[4,64,128]{2,1,0:T(8,128)S(1)} %collective-permute-done.16.refs_10_), channel_id=1, source_target_pairs={{0,48},{16,32},{32,16},{48,0},{64,112},{80,96},{96,80},{112,64},{1... | collective-permute-start | bytes 393224 | tf_op jit(solution)/shard_map/ppermute | solution.py:198
  64.0 7.9 %collective-permute-start.18 = (f32[4,64,128]{2,1,0:T(8,128)S(1)}, f32[4,64,128]{2,1,0:T(8,128)S(1)}, u32[]{:S(2)}, u32[]{:S(2)}) collective-permute-start(f32[4,64,128]{2,1,0:T(8,128)S(1)} %collective-permute-done.16.refs_10_), channel_id=1, source_target_pairs={{0,32},{16,48},{32,0},{48,16},{64,96},{80,112},{96,64},{112,80},{1... | collective-permute-start | bytes 393224 | tf_op jit(solution)/shard_map/ppermute | solution.py:198
  65.1 7.7 %collective-permute-start.17 = (f32[4,64,128]{2,1,0:T(8,128)S(1)}, f32[4,64,128]{2,1,0:T(8,128)S(1)}, u32[]{:S(2)}, u32[]{:S(2)}) collective-permute-start(f32[4,64,128]{2,1,0:T(8,128)S(1)} %collective-permute-done.16.refs_10_), channel_id=1, source_target_pairs={{0,16},{16,0},{32,48},{48,32},{64,80},{80,64},{96,112},{112,96},{1... | collective-permute-start | bytes 393224 | tf_op jit(solution)/shard_map/ppermute | solution.py:198
  84.5 8.5 %collective-permute-start.23 = (f32[4,64,128]{2,1,0:T(8,128)S(1)}, f32[4,64,128]{2,1,0:T(8,128)S(1)}, u32[]{:S(2)}, u32[]{:S(2)}) collective-permute-start(f32[4,64,128]{2,1,0:T(8,128)S(1)} %slice_add_fusion.4), channel_id=1, source_target_pairs={{0,4},{1,5},{2,6},{3,7},{4,0},{5,1},{6,2},{7,3},{8,12},{9,13},{10,... | collective-permute-start | bytes 393224 | tf_op jit(solution)/shard_map/ppermute | solution.py:194
  94.8 12.7 %collective-permute-start.27 = (f32[4,64,128]{2,1,0:T(8,128)S(1)}, f32[4,64,128]{2,1,0:T(8,128)S(1)}, u32[]{:S(2)}, u32[]{:S(2)}) collective-permute-start(f32[4,64,128]{2,1,0:T(8,128)S(1)} %add_add_fusion.1), channel_id=1, source_target_pairs={{0,128},{1,176},{2,240},{3,80},{4,16},{5,48},{6,112},{7,224},{8,20... | collective-permute-start | bytes 393224 | tf_op jit(solution)/shard_map/ppermute | solution.py:258
  99.5 18.0 %collective-permute-start.26 = (f32[8,64,128]{2,1,0:T(8,128)S(1)}, f32[8,64,128]{2,1,0:T(8,128)S(1)}, u32[]{:S(2)}, u32[]{:S(2)}) collective-permute-start(f32[8,64,128]{2,1,0:T(8,128)S(1)} %pad_maximum_fusion.1.refs_8_), channel_id=1, source_target_pairs={{0,1},{1,0},{2,3},{3,2},{4,5},{5,4},{6,7},{7,6},{8,9},{9,8},{10,11... | collective-permute-start | bytes 786440 | tf_op jit(solution)/shard_map/ppermute | solution.py:194
  107.5 9.4 %collective-permute-start.30 = (f32[4,64,128]{2,1,0:T(8,128)S(1)}, f32[4,64,128]{2,1,0:T(8,128)S(1)}, u32[]{:S(2)}, u32[]{:S(2)}) collective-permute-start(f32[4,64,128]{2,1,0:T(8,128)S(1)} %collective-permute-done.27.refs_10_), channel_id=1, source_target_pairs={{0,48},{16,32},{32,16},{48,0},{64,112},{80,96},{96,80},{112,64},{1... | collective-permute-start | bytes 393224 | tf_op jit(solution)/shard_map/ppermute | solution.py:198
  108.0 9.0 %collective-permute-start.29 = (f32[4,64,128]{2,1,0:T(8,128)S(1)}, f32[4,64,128]{2,1,0:T(8,128)S(1)}, u32[]{:S(2)}, u32[]{:S(2)}) collective-permute-start(f32[4,64,128]{2,1,0:T(8,128)S(1)} %collective-permute-done.27.refs_10_), channel_id=1, source_target_pairs={{0,32},{16,48},{32,0},{48,16},{64,96},{80,112},{96,64},{112,80},{1... | collective-permute-start | bytes 393224 | tf_op jit(solution)/shard_map/ppermute | solution.py:198
  108.5 9.0 %collective-permute-start.28 = (f32[4,64,128]{2,1,0:T(8,128)S(1)}, f32[4,64,128]{2,1,0:T(8,128)S(1)}, u32[]{:S(2)}, u32[]{:S(2)}) collective-permute-start(f32[4,64,128]{2,1,0:T(8,128)S(1)} %collective-permute-done.27.refs_10_), channel_id=1, source_target_pairs={{0,16},{16,0},{32,48},{48,32},{64,80},{80,64},{96,112},{112,96},{1... | collective-permute-start | bytes 393224 | tf_op jit(solution)/shard_map/ppermute | solution.py:198
  129.1 7.5 %collective-permute-start.35 = (f32[4,64,128]{2,1,0:T(8,128)S(1)}, f32[4,64,128]{2,1,0:T(8,128)S(1)}, u32[]{:S(2)}, u32[]{:S(2)}) collective-permute-start(f32[4,64,128]{2,1,0:T(8,128)S(1)} %slice_add_fusion.3), channel_id=1, source_target_pairs={{0,6},{1,7},{2,4},{3,5},{4,2},{5,3},{6,0},{7,1},{8,14},{9,15},{10,... | collective-permute-start | bytes 393224 | tf_op jit(solution)/shard_map/ppermute | solution.py:194
  129.2 7.7 %collective-permute-start.34 = (f32[4,64,128]{2,1,0:T(8,128)S(1)}, f32[4,64,128]{2,1,0:T(8,128)S(1)}, u32[]{:S(2)}, u32[]{:S(2)}) collective-permute-start(f32[4,64,128]{2,1,0:T(8,128)S(1)} %slice_add_fusion.3), channel_id=1, source_target_pairs={{0,4},{1,5},{2,6},{3,7},{4,0},{5,1},{6,2},{7,3},{8,12},{9,13},{10,... | collective-permute-start | bytes 393224 | tf_op jit(solution)/shard_map/ppermute | solution.py:194
  139.2 12.2 %collective-permute-start.38 = (f32[4,64,128]{2,1,0:T(8,128)S(1)}, f32[4,64,128]{2,1,0:T(8,128)S(1)}, u32[]{:S(2)}, u32[]{:S(2)}) collective-permute-start(f32[4,64,128]{2,1,0:T(8,128)S(1)} %add_add_fusion), channel_id=1, source_target_pairs={{0,128},{1,176},{2,240},{3,80},{4,16},{5,48},{6,112},{7,224},{8,20... | collective-permute-start | bytes 393224 | tf_op jit(solution)/shard_map/ppermute | solution.py:258
  143.6 17.1 %collective-permute-start.37 = (f32[8,64,128]{2,1,0:T(8,128)S(1)}, f32[8,64,128]{2,1,0:T(8,128)S(1)}, u32[]{:S(2)}, u32[]{:S(2)}) collective-permute-start(f32[8,64,128]{2,1,0:T(8,128)S(1)} %pad_maximum_fusion.2.refs_6_), channel_id=1, source_target_pairs={{0,1},{1,0},{2,3},{3,2},{4,5},{5,4},{6,7},{7,6},{8,9},{9,8},{10,11... | collective-permute-start | bytes 786440 | tf_op jit(solution)/shard_map/ppermute | solution.py:194
  151.4 8.6 %collective-permute-start.41 = (f32[4,64,128]{2,1,0:T(8,128)S(1)}, f32[4,64,128]{2,1,0:T(8,128)S(1)}, u32[]{:S(2)}, u32[]{:S(2)}) collective-permute-start(f32[4,64,128]{2,1,0:T(8,128)S(1)} %collective-permute-done.38.refs_8_), channel_id=1, source_target_pairs={{0,48},{16,32},{32,16},{48,0},{64,112},{80,96},{96,80},{112,64},{1... | collective-permute-start | bytes 393224 | tf_op jit(solution)/shard_map/ppermute | solution.py:198
  151.7 8.4 %collective-permute-start.40 = (f32[4,64,128]{2,1,0:T(8,128)S(1)}, f32[4,64,128]{2,1,0:T(8,128)S(1)}, u32[]{:S(2)}, u32[]{:S(2)}) collective-permute-start(f32[4,64,128]{2,1,0:T(8,128)S(1)} %collective-permute-done.38.refs_8_), channel_id=1, source_target_pairs={{0,32},{16,48},{32,0},{48,16},{64,96},{80,112},{96,64},{112,80},{1... | collective-permute-start | bytes 393224 | tf_op jit(solution)/shard_map/ppermute | solution.py:198
  151.7 9.0 %collective-permute-start.39 = (f32[4,64,128]{2,1,0:T(8,128)S(1)}, f32[4,64,128]{2,1,0:T(8,128)S(1)}, u32[]{:S(2)}, u32[]{:S(2)}) collective-permute-start(f32[4,64,128]{2,1,0:T(8,128)S(1)} %collective-permute-done.38.refs_8_), channel_id=1, source_target_pairs={{0,16},{16,0},{32,48},{48,32},{64,80},{80,64},{96,112},{112,96},{1... | collective-permute-start | bytes 393224 | tf_op jit(solution)/shard_map/ppermute | solution.py:198
  (18 other events, 89.4 us)
